TPU v7x, 256 devices: a whole 4x4x8 slice. The times are simulated.
256 devices in a mesh: shard: 4 (over y_lo, core), replica: 64 (over z, y_hi, x).
Axes of the slice: x: 4, y: 4 (y_hi: 2, y_lo: 2; y = y_hi * 2 + y_lo), z: 8, core: 2. Of those that a mesh axis runs over, the one named last changes fastest.
Arguments:
- tokens_in: bfloat16 [65536, 8192], P(('shard', 'replica')), may hold values from -6 to 6
- key_cotangent: bfloat16 [65536, 512], P(('shard', 'replica')), may hold values from -6 to 6
- key_weight: bfloat16 [8192, 512], P('shard'), may hold values from -0.0625 to 0.0625
- master_store: float32 [8192, 512], P(('shard', 'replica')), may hold values from -0.015625 to 0.015625
- first_moment: float32 [8192, 512], P(('shard', 'replica')), may hold values from -4 to 4
- second_moment: float32 [8192, 512], P(('shard', 'replica')), may hold values from 0.25 to 4
- writer: int32 [4, 64], P('shard'), may hold values from 0 to 63, each once within a row
Outputs:
- input_grad: bfloat16 [65536, 8192], P(('shard', 'replica'))
- master_new: float32 [8192, 512], P(('shard', 'replica'))
- moment_one: float32 [8192, 512], P(('shard', 'replica'))
- moment_two: float32 [8192, 512], P(('shard', 'replica'))
- weight_new: bfloat16 [8192, 512], P('shard')
Inputs may be any that keep to these rules, and one draw needn't show every extreme that they name: Each row is a permutation: replica r of shard s holds the states of row block writer[s, r] of that shard.
All inputs are finite; a program needn't handle non-finite values.
Results may differ from a plain program's by a relative error of at most 0.0027.
Values may be sent and summed in bfloat16 or wider, within the bound.
No kernel may reach another device: no remote copies, remote signals or barrier semaphores. Data moves between devices by JAX's collectives and lax.ppermute only.
A program may use at most 128 MiB of HBM per device.

v0:
```python
import jax
import jax.numpy as jnp
from jax import lax
from jax.sharding import PartitionSpec as P

beta_first = 0.9
beta_second = 0.95
learn_rate = 0.0003
decay_rate = 0.1
adam_eps = 1e-08
step_count = 100


def on_device(
    tokens_in, key_cotangent, key_weight, master_store, first_moment, second_moment, writer
):
    shard_count = lax.axis_size("shard")
    replica_count = lax.axis_size("replica")
    rows_here = key_weight.shape[0]
    block_rows = master_store.shape[0]
    writer_row = writer[0]
    tok_rows = tokens_in.shape[0]
    input_grad = lax.dot_general(
        key_cotangent,
        lax.all_gather(key_weight, "shard", axis=0, tiled=True),
        (((1,), (1,)), ((), ())),
        preferred_element_type=jnp.float32,
    ).astype(jnp.bfloat16)
    shard_grad = lax.psum_scatter(
        lax.dot_general(
            tokens_in, key_cotangent, (((0,), (0,)), ((), ())), preferred_element_type=jnp.float32
        ).astype(jnp.bfloat16),
        "shard",
        scatter_dimension=0,
        tiled=True,
    ).astype(jnp.float32)
    summed = lax.psum(shard_grad, "replica")
    blocks = summed.reshape(replica_count, block_rows, -1)
    own_block = lax.dynamic_index_in_dim(
        blocks, writer_row[lax.axis_index("replica")], 0, keepdims=False
    )
    grad_scale = (tok_rows * shard_count * replica_count) ** (-0.5)
    stored_grad = own_block * grad_scale
    moment_one = beta_first * first_moment + (1.0 - beta_first) * stored_grad
    moment_two = beta_second * second_moment + (1.0 - beta_second) * stored_grad * stored_grad
    corrected_one = moment_one / (1.0 - beta_first**step_count)
    corrected_two = moment_two / (1.0 - beta_second**step_count)
    master_new = master_store - learn_rate * (
        corrected_one / (jnp.sqrt(corrected_two) + adam_eps) + decay_rate * master_store
    )
    fresh_blocks = lax.all_gather(master_new.astype(jnp.bfloat16), "replica", axis=0, tiled=True)
    arranged = fresh_blocks.reshape(replica_count, block_rows, -1)
    placed = jnp.zeros_like(arranged).at[writer_row].set(arranged)
    weight_new = placed.reshape(rows_here, -1)
    return (input_grad, master_new, moment_one, moment_two, weight_new)


def solution(mesh):
    in_specs = (
        P(("shard", "replica"), None),
        P(("shard", "replica"), None),
        P("shard", None),
        P(("shard", "replica"), None),
        P(("shard", "replica"), None),
        P(("shard", "replica"), None),
        P("shard", None),
    )
    out_specs = (
        P(("shard", "replica"), None),
        P(("shard", "replica"), None),
        P(("shard", "replica"), None),
        P(("shard", "replica"), None),
        P("shard", None),
    )
    return jax.shard_map(
        on_device, mesh=mesh, in_specs=in_specs, out_specs=out_specs, check_vma=False
    )
```

profile of v0, /device:TPU:1, one launch (start us, length us, event | category | flops | bytes accessed | tf_op | source)
XLA Modules:
  0.0 635.3 jit_solution(9100990114063027115)
XLA Ops:
  7.2 0.0 copy-start
  7.2 0.0 reduce-scatter.2.cloned.1.call-start
  7.2 0.9 copy-done
  8.1 7.8 %convolution_convert_fusion = bf16[8192,512]{1,0:T(8,128)(2,1)} fusion(bf16[256,8192]{1,0:T(8,128)(2,1)} %param.7, bf16[256,512]{1,0:T(8,128)(2,1)S(1)} %copy-done), kind=kOutput, calls=%fused_computation.1 | convolution fusion | flops 2151677952 | bytes 12845056 | tf_op jit(solution)/shard_map/dot_general | solution.py:30
  15.9 0.0 copy-start.5
  15.9 0.0 reduce-scatter.2.cloned.1.call-update
  16.0 0.0 copy-start.2
  16.0 0.0 copy-start.3
  16.0 0.0 copy-start.4
  16.0 0.0 all-gather.3.cloned.1.call-start
  16.0 0.7 all-gather.3.cloned.1.call-update
  16.7 0.0 all-gather.5.cloned.1.call-start
  16.8 0.0 copy-done.5
  16.8 0.6 constant_dynamic-slice_fusion
  19.3 82.4 %reduce-scatter.2.cloned.1.call-done = bf16[2048,512]{1,0:T(8,128)(2,1)} async-done(((bf16[8192,512]{1,0:T(8,128)(2,1)}), bf16[2048,512]{1,0:T(8,128)(2,1)}) %reduce-scatter.2.cloned.1.call-update) | async-done | bytes 2097168 | tf_op jit(solution)/shard_map/reduce_scatter | solution.py:29
  101.8 355.9 %all-reduce.1 = f32[64,32,512]{2,1,0:T(8,128)} all-reduce(bf16[64,32,512]{2,1,0:T(8,128)(2,1)} %bitcast.20), channel_id=1, replica_groups=mesh['shard'=4,'replica'=64] {'replica'}, use_global_device_ids=true, to_apply=%region_1.0 | all-reduce | flops 1048576 | bytes 6291456 | tf_op jit(solution)/shard_map/psum | solution.py:37
  457.7 0.0 copy-done.2
  457.7 0.0 copy-done.3
  457.7 0.0 copy-done.4
  457.7 1.5 fusion.1
  459.2 0.0 all-gather.5.cloned.1.call-update
  459.3 0.0 all-gather.3.cloned.1.call-done
  459.3 7.8 %convolution_convert_fusion.1 = bf16[256,8192]{1,0:T(8,128)(2,1)} fusion(bf16[256,512]{1,0:T(8,128)(2,1)S(1)} %copy-done, bf16[8192,512]{1,0:T(8,128)(2,1)} %all-gather.3.cloned.1.call-done), kind=kOutput, calls=%fused_computation.2 | convolution fusion | flops 2149580800 | bytes 12845056 | tf_op jit(solution)/shard_map/dot_general | solution.py:23
  467.1 153.5 %all-gather.5.cloned.1.call-done = bf16[2048,512]{1,0:T(8,128)(2,1)} async-done(((bf16[32,512]{1,0:T(8,128)(2,1)}), bf16[2048,512]{1,0:T(8,128)(2,1)}) %all-gather.5.cloned.1.call-update) | async-done | bytes 2097168 | tf_op jit(solution)/shard_map/all_gather | solution.py:51
  620.6 0.2 broadcast_in_dim.4
  620.9 6.6 %scatter_fusion = bf16[64,32,512]{2,1,0:T(8,128)(2,1)S(1)} fusion(bf16[64,32,512]{2,1,0:T(8,128)(2,1)S(1)} %broadcast_in_dim.4, s32[64]{0:T(128)S(1)} %fusion, bf16[64,32,512]{2,1,0:T(8,128)(2,1)} %bitcast.21), kind=kCustom, calls=%fused_computation | custom fusion | bytes 6291712 | tf_op jit(solution)/shard_map/scatter | solution.py:53
  627.5 0.0 copy-start.1
  627.5 1.3 copy-done.1
  (1 shorter events, 0.0 us)
Async XLA Ops:
  7.2 1.0 copy-start
  7.2 94.6 %reduce-scatter.2.cloned.1.call-start = ((), (), s32[]{:S(2)}) async-start(), calls=%async_computation.2 | async-start | bytes 10485760 | tf_op jit(solution)/shard_map/reduce_scatter | solution.py:29
  15.9 0.9 copy-start.5
  16.0 441.7 %copy-start.2 = (f32[32,512]{1,0:T(8,128)S(1)}, f32[32,512]{1,0:T(8,128)}, u32[]{:S(2)}) copy-start(f32[32,512]{1,0:T(8,128)} %param.10) | copy-start | bytes 196612
  16.0 441.7 %copy-start.3 = (f32[32,512]{1,0:T(8,128)S(1)}, f32[32,512]{1,0:T(8,128)}, u32[]{:S(2)}) copy-start(f32[32,512]{1,0:T(8,128)} %param.11) | copy-start | bytes 196612
  16.0 441.7 %copy-start.4 = (f32[32,512]{1,0:T(8,128)S(1)}, f32[32,512]{1,0:T(8,128)}, u32[]{:S(2)}) copy-start(f32[32,512]{1,0:T(8,128)} %param.12) | copy-start | bytes 196612
  16.0 443.3 %all-gather.3.cloned.1.call-start = ((), (), s32[]{:S(2)}) async-start(), calls=%async_computation.1 | async-start | bytes 10485760 | tf_op jit(solution)/shard_map/all_gather | solution.py:25
  16.7 603.9 %all-gather.5.cloned.1.call-start = ((), (), s32[]{:S(2)}) async-start(), calls=%async_computation.3 | async-start | bytes 2129920 | tf_op jit(solution)/shard_map/all_gather | solution.py:51
  627.5 1.3 copy-start.1
Sparse Core Ops, SparseCore 0:
  16.1 85.6 reduce-scatter.1
  103.6 107.7 all-gather.2
  459.4 161.1 all-gather.4
where the time goes:
time: 638 us; the launch traced here: 635 us
  blocking collectives  356 us (56%)
  waiting for transfers between devices  237 us (37%)
  between operations  15.8 us (2%)
  matrix products  15.6 us (2%)
  local copies, waits for them, and re-layouts  9.68 us (2%)
    psum x1, blocking collectives, on_device(): summed = lax.psum(shard_grad, 'replica')  356 us
    all_gather x1, waiting for transfers between devices, on_device(): lax.all_gather(master_new.astype(jnp.bfloat16), 'replica', axis=0, tiled=...  154 us
    reduce_scatter x1, waiting for transfers between devices, on_device(): lax.psum_scatter(lax.dot_general(tokens_in, key_cotangent, (((0,), (0,)),...  82.4 us
  transfers between devices with their start and end apart: 3, of which 2 were waited for; matrix products, arithmetic and copies ran while one was open for 2% of the time, Pallas kernels for 0%

commit v1 on v0

v1 whole, which is shorter than its diff:
```python
import functools

import jax
import jax.numpy as jnp
from jax import lax
from jax.experimental import pallas as pl
from jax.experimental.pallas import tpu as pltpu
from jax.sharding import Mesh
from jax.sharding import PartitionSpec as P

beta_first = 0.9
beta_second = 0.95
learn_rate = 0.0003
decay_rate = 0.1
adam_eps = 1e-08
step_count = 100

NYL, NC, NZ, NYH, NX = 2, 2, 8, 2, 4
NY = NYL * NYH
AXES = ("yl", "c", "z", "yh", "x")
VMEM_LIMIT = 48 * 1024 * 1024


def shift(axis, step):
    if axis == "y":
        spot = lambda y: (y % NYL) * NYH + y // NYL
        return [(spot(y), spot((y + step) % NY)) for y in range(NY)]
    size = {"x": NX, "z": NZ, "c": NC, "yl": NYL, "yh": NYH}[axis]
    return [(i, (i + step) % size) for i in range(size)]


def send(value, axis, step):
    return lax.ppermute(value, ("yl", "yh") if axis == "y" else axis, shift(axis, step))


def vmem():
    return pl.BlockSpec(memory_space=pltpu.VMEM)


def both_cores_kernel(far, place, order, own_tok, own_key, got_tok, got_key, *rest):
    outs, total = rest[:-1], rest[-1]
    x, y, z = place[0], place[1], place[2]
    rows, half = total.shape[0], outs[0].shape[2]
    cut = min(512, rows)
    for q in range(rows // cut):
        piece = slice(q * cut, (q + 1) * cut)

        def partial(tok, key):
            value = lax.dot_general(
                tok[:, piece], key[...], (((0,), (0,)), ((), ())), preferred_element_type=jnp.float32
            )
            return value.astype(jnp.bfloat16).astype(jnp.float32)

        total[piece, :] = partial(own_tok, own_key) + partial(got_tok, got_key)
    steps_y = (1, 3) if far else (0, 2)
    for k in range(NX):
        to_x = lax.rem(x + k, NX)
        for n, j in enumerate(steps_y):
            to_yh = lax.div(lax.rem(y + j, NY), NYL)
            for m in range(NZ):
                to_z = lax.rem(z + m, NZ)
                block = order[0, (to_z * NYH + to_yh) * NX + to_x]
                start = pl.multiple_of(block * (2 * half), 2 * half)
                first = total[pl.ds(start, half), :]
                second = total[pl.ds(start + half, half), :]
                outs[k][n, m] = first.astype(outs[k].dtype)
                outs[NX + n][k, m] = second.astype(outs[NX + n].dtype)


def both_cores(far, place, order, own_tok, own_key, got_tok, got_key, block_rows):
    rows, width = got_tok.shape[1], own_key.shape[1]
    half = block_rows // 2
    near = jnp.bfloat16 if far else jnp.float32
    shapes = [
        jax.ShapeDtypeStruct((2, NZ, half, width), jnp.float32 if k == 0 else jnp.bfloat16)
        for k in range(NX)
    ]
    shapes += [
        jax.ShapeDtypeStruct((NX, NZ, half, width), near if n == 0 else jnp.bfloat16)
        for n in range(2)
    ]
    return pl.pallas_call(
        functools.partial(both_cores_kernel, far),
        grid_spec=pltpu.PrefetchScalarGridSpec(
            num_scalar_prefetch=2,
            grid=(1,),
            in_specs=[
                pl.BlockSpec((own_tok.shape[0], rows), lambda i, place, order: (0, place[3])),
                vmem(),
                vmem(),
                vmem(),
            ],
            out_specs=[vmem()] * len(shapes),
            scratch_shapes=[pltpu.VMEM((rows, width), jnp.float32)],
        ),
        out_shape=shapes,
        compiler_params=pltpu.CompilerParams(vmem_limit_bytes=VMEM_LIMIT),
    )(place, order, own_tok, own_key, got_tok, got_key)


def input_grad_kernel(place, key, *rest):
    pieces, out = rest[:-1], rest[-1]
    step = pl.program_id(0)
    for n in range(8):
        piece = pieces[(0, 0, 1, 1, 2, 3, 4, 5)[n]]

        @pl.when(step == n)
        def _(piece=piece):
            out[...] = lax.dot_general(
                key[...], piece[...], (((1,), (1,)), ((), ())), preferred_element_type=jnp.float32
            ).astype(out.dtype)


def input_grad_of(place, key, own, core, low, high, low_core, high_core, width):
    rows = low.shape[0]
    whole = lambda i, place: (0, 0)

    def column(i, place):
        yl = lax.rem(place[0] + lax.div(i, 4), 2)
        c = lax.rem(place[1] + lax.div(lax.rem(i, 4), 2), 2)
        return 0, (yl * NC + c) * 2 + lax.rem(i, 2)

    return pl.pallas_call(
        input_grad_kernel,
        grid_spec=pltpu.PrefetchScalarGridSpec(
            num_scalar_prefetch=1,
            grid=(8,),
            in_specs=[
                pl.BlockSpec(key.shape, whole),
                pl.BlockSpec((rows, key.shape[1]), lambda i, place: (jnp.minimum(i, 1), 0)),
                pl.BlockSpec(
                    (rows, key.shape[1]), lambda i, place: (jnp.clip(i - 2, 0, 1), 0)
                ),
            ]
            + [pl.BlockSpec((rows, key.shape[1]), whole)] * 4,
            out_specs=pl.BlockSpec((key.shape[0], rows), column),
        ),
        out_shape=jax.ShapeDtypeStruct((key.shape[0], width), jnp.bfloat16),
        compiler_params=pltpu.CompilerParams(vmem_limit_bytes=VMEM_LIMIT),
    )(place, key, own, core, low, high, low_core, high_core)


def place_kernel(place, order, *rest):
    parts, out = rest[:-1], rest[-1]
    x, yh, z = place[0], place[1], place[2]
    block_rows = parts[0].shape[2]
    for k in range(NX):
        from_x = lax.rem(x + NX - k, NX)
        for n in range(NYH):
            from_yh = lax.rem(yh + n, NYH)
            for m in range(NZ):
                from_z = lax.rem(z + NZ - m, NZ)
                block = order[0, (from_z * NYH + from_yh) * NX + from_x]
                start = pl.multiple_of(block * block_rows, block_rows)
                out[pl.ds(start, block_rows), :] = parts[k][n, m]


def put_in_rows(place, order, parts, rows):
    return pl.pallas_call(
        place_kernel,
        grid_spec=pltpu.PrefetchScalarGridSpec(
            num_scalar_prefetch=2,
            grid=(1,),
            in_specs=[vmem()] * len(parts),
            out_specs=vmem(),
        ),
        out_shape=jax.ShapeDtypeStruct((rows, parts[0].shape[3]), parts[0].dtype),
        compiler_params=pltpu.CompilerParams(vmem_limit_bytes=VMEM_LIMIT),
    )(place, order, *parts)


def f32(value):
    return value.astype(jnp.float32)


def on_device(
    tokens_in, key_cotangent, key_weight, master_store, first_moment, second_moment, writer
):
    yl, c, z, yh, x = (lax.axis_index(name) for name in AXES)
    y = yh * NYL + yl
    tok_rows, width = tokens_in.shape
    rows_here = key_weight.shape[0]
    block_rows = master_store.shape[0]

    with jax.named_scope("core_swap"):
        got_key = send(key_cotangent, "c", 1)
        near_order = writer
        far_order = send(writer, "yl", 1)
        summed = {}
        for far in (1, 0):
            shard = (yl ^ far) * NC
            other = lax.dynamic_slice(
                tokens_in, (0, (shard + 1 - c) * rows_here), (tok_rows, rows_here)
            )
            got_tok = send(other, "c", 1)
            place = jnp.stack([x, y, z, shard + c]).astype(jnp.int32)
            summed[far] = both_cores(
                far,
                place,
                far_order if far else near_order,
                tokens_in,
                key_cotangent,
                got_tok,
                got_key,
                block_rows,
            )

    with jax.named_scope("first_stage"):
        first = {}
        for far in (1, 0):
            parts = summed[far][:NX]
            got = [send(parts[k], "x", k) for k in range(1, NX)]
            first[far] = f32(parts[0])
            for value in got:
                first[far] = first[far] + f32(value)
        second = f32(summed[0][NX])
        got = [
            send(summed[1][NX], "y", 1),
            send(summed[1][NX + 1], "y", 3),
            send(summed[0][NX + 1], "y", 2),
        ]
        for value in got:
            second = second + f32(value)

    with jax.named_scope("second_stage"):
        out_y = {1: first[1][0], 3: first[1][1], 2: first[0][1]}
        got_y = [send(value.astype(jnp.bfloat16), "y", j) for j, value in out_y.items()]
        got_x = [send(second[k].astype(jnp.bfloat16), "x", k) for k in range(1, NX)]
        first_half = first[0][0]
        for value in got_y:
            first_half = first_half + f32(value)
        second_half = second[0]
        for value in got_x:
            second_half = second_half + f32(value)

    with jax.named_scope("weights"):
        held, first_half, second_half = lax.optimization_barrier(
            (key_weight, first_half, second_half)
        )
        low = send(held[: rows_here // 2], "y", 1)
        high = send(held[rows_here // 2 :], "y", 3)
        core = send(held, "c", 1)
        low_core, high_core = send(low, "c", 1), send(high, "c", 1)
        input_grad = input_grad_of(
            jnp.stack([yl, c]).astype(jnp.int32),
            key_cotangent,
            held,
            core,
            low,
            high,
            low_core,
            high_core,
            width,
        )

    with jax.named_scope("third_stage"):
        blocks = [jnp.concatenate([first_half[m], second_half[m]], axis=0) for m in range(NZ)]
        own_block = blocks[0]
        for value in [send(blocks[m], "z", m) for m in range(1, NZ)]:
            own_block = own_block + value

    with jax.named_scope("adam"):
        devices = NYL * NC * NZ * NYH * NX
        stored_grad = own_block * (tok_rows * devices) ** (-0.5)
        moment_one = beta_first * first_moment + (1.0 - beta_first) * stored_grad
        moment_two = beta_second * second_moment + (1.0 - beta_second) * stored_grad * stored_grad
        corrected_one = moment_one / (1.0 - beta_first**step_count)
        corrected_two = moment_two / (1.0 - beta_second**step_count)
        master_new = master_store - learn_rate * (
            corrected_one / (jnp.sqrt(corrected_two) + adam_eps) + decay_rate * master_store
        )

    with jax.named_scope("fresh_weights"):
        fresh = master_new.astype(jnp.bfloat16)
        column = jnp.stack([fresh] + [send(fresh, "z", m) for m in range(1, NZ)])
        plane = jnp.stack([column, send(column, "yh", 1)])
        parts = [plane] + [send(plane, "x", k) for k in range(1, NX)]
        place = jnp.stack([x, yh, z]).astype(jnp.int32)
        weight_new = put_in_rows(place, near_order, parts, rows_here)
    return (input_grad, master_new, moment_one, moment_two, weight_new)


def solution(mesh):
    fine = Mesh(mesh.devices.reshape(NYL, NC, NZ, NYH, NX), AXES)
    shard, every = ("yl", "c"), AXES
    in_specs = (
        P(every, None),
        P(every, None),
        P(shard, None),
        P(every, None),
        P(every, None),
        P(every, None),
        P(shard, None),
    )
    out_specs = (P(every, None),) * 4 + (P(shard, None),)
    return jax.shard_map(
        on_device, mesh=fine, in_specs=in_specs, out_specs=out_specs, check_vma=False
    )
```

time: 638 us -> 170 us (0.27)
  the two profiles are of different devices: /device:TPU:1 before, /device:TPU:40 now
where the time goes in v1:
time: 170 us
  waiting for transfers between devices  85.6 us (50%)
  starting transfers between devices  59.7 us (35%)
  Pallas kernels  17.2 us (10%)
  local copies, waits for them, and re-layouts  4.78 us (3%)
  other arithmetic  1.93 us (1%)
    ppermute x42, waiting for transfers between devices, send(): lax.ppermute(value, ('yl', 'yh') if axis == 'y' else axis, shift(axis, st...  85.6 us
    ppermute x42, starting transfers between devices, send(): lax.ppermute(value, ('yl', 'yh') if axis == 'y' else axis, shift(axis, st...  59.7 us
    pallas_call x1, Pallas kernels, input_grad_of(): pl.pallas_call(input_grad_kernel, grid_spec=pltpu.PrefetchScalarGridSpec(...  8.48 us
    pallas_call x2, Pallas kernels, both_cores(): pl.pallas_call(functools.partial(both_cores_kernel, far), grid_spec=pltpu...  6.65 us
  transfers between devices with their start and end apart: 42, of which 22 were waited for; matrix products, arithmetic and copies ran while one was open for 1% of the time, Pallas kernels for 5%

profile of v1, /device:TPU:40, one launch (start us, length us, event | category | flops | bytes accessed | tf_op | source)
XLA Modules:
  0.0 170.2 jit_solution(1060392044815297620)
XLA Ops:
  0.7 3.2 %constant_dynamic-slice_fusion = (bf16[256,2048]{1,0:T(8,128)(2,1)}, bf16[256,2048]{1,0:T(8,128)(2,1)}) fusion(bf16[256,8192]{1,0:T(8,128)(2,1)} %own_tok.3, s32[]{:T(128)S(6)} %select_n.7, s32[]{:T(128)S(6)} %select_n.6), kind=kLoop, calls=%fused_computation.65 | loop fusion | bytes 4194312 | tf_op jit(solution)/shard_map/core_swap/dynamic_slice | solution.py:192
  3.8 0.5 collective-permute-start.6
  4.5 2.7 %collective-permute-done.1.got_key = bf16[256,512]{1,0:T(8,128)(2,1)S(1)} collective-permute-done((bf16[256,512]{1,0:T(8,128)(2,1)S(1)}, bf16[256,512]{1,0:T(8,128)(2,1)S(1)}, u32[]{:S(2)}, u32[]{:S(2)}) %collective-permute-start.1) | collective-permute-done | bytes 262176 | tf_op jit(solution)/shard_map/core_swap/ppermute | solution.py:33
  7.2 3.3 %core_swap.2 = (f32[2,8,16,512]{3,2,1,0:T(8,128)S(1)}, bf16[2,8,16,512]{3,2,1,0:T(8,128)(2,1)S(1)}, bf16[2,8,16,512]{3,2,1,0:T(8,128)(2,1)S(1)}, bf16[2,8,16,512...) custom-call(s32[4]{0:T(128)S(1)} %pad_add_fusion.1.place, ...), custom_call_target="tpu_custom_call" | custom-call | tf_op jit(solution)/shard_map/core_swap/pallas_call | solution.py:82
  10.6 2.8 %collective-permute-start.4 = (bf16[2,8,16,512]{3,2,1,0:T(8,128)(2,1)S(1)}, bf16[2,8,16,512]{3,2,1,0:T(8,128)(2,1)S(1)}, u32[]{:S(2)}, u32[]{:S(2)}) collective-permute-start(bf16[2,8,16,512]{3,2,1,0:T(8,128)(2,1)S(1)} %get-tuple-element.23), channel_id=1, source_target_pairs={{0,3},{1,0},{2,1},{3,2},{4,7},{5,4},{6,5},{7,6},{8,11},{9,8},{10,9... | collective-permute-start | bytes 786440 | tf_op jit(solution)/shard_map/first_stage/ppermute | solution.py:33
  13.4 0.8 collective-permute-start.3
  14.2 0.9 collective-permute-start.2
  15.1 0.4 collective-permute-start.5
  15.6 3.1 %collective-permute-done.5.order = s32[1,64]{1,0:T(1,128)S(1)} collective-permute-done((s32[1,64]{1,0:T(1,128)S(1)}, s32[1,64]{1,0:T(1,128)S(1)}, u32[]{:S(2)}, u32[]{:S(2)}) %collective-permute-start.5) | collective-permute-done | bytes 288 | tf_op jit(solution)/shard_map/core_swap/ppermute | solution.py:33
  18.6 3.3 %core_swap.3 = (f32[2,8,16,512]{3,2,1,0:T(8,128)S(1)}, bf16[2,8,16,512]{3,2,1,0:T(8,128)(2,1)S(1)}, bf16[2,8,16,512]{3,2,1,0:T(8,128)(2,1)S(1)}, bf16[2,8,16,512...) custom-call(s32[4]{0:T(128)S(1)} %get-tuple-element.42.place, ...), custom_call_target="tpu_custom_call" | custom-call | tf_op jit(solution)/shard_map/core_swap/pallas_call | solution.py:82
  22.0 2.4 %collective-permute-start.9 = (bf16[2,8,16,512]{3,2,1,0:T(8,128)(2,1)S(1)}, bf16[2,8,16,512]{3,2,1,0:T(8,128)(2,1)S(1)}, u32[]{:S(2)}, u32[]{:S(2)}) collective-permute-start(bf16[2,8,16,512]{3,2,1,0:T(8,128)(2,1)S(1)} %get-tuple-element.27), channel_id=1, source_target_pairs={{0,3},{1,0},{2,1},{3,2},{4,7},{5,4},{6,5},{7,6},{8,11},{9,8},{10,9... | collective-permute-start | bytes 786440 | tf_op jit(solution)/shard_map/first_stage/ppermute | solution.py:33
  24.4 1.5 collective-permute-start.8
  25.9 2.4 %collective-permute-start.15 = (bf16[4,8,16,512]{3,2,1,0:T(8,128)(2,1)S(1)}, bf16[4,8,16,512]{3,2,1,0:T(8,128)(2,1)S(1)}, u32[]{:S(2)}, u32[]{:S(2)}) collective-permute-start(bf16[4,8,16,512]{3,2,1,0:T(8,128)(2,1)S(1)} %get-tuple-element.31), channel_id=1, source_target_pairs={{0,4},{128,132},{4,0},{132,128},{1,5},{129,133},{5,1},{133,129},{2... | collective-permute-start | bytes 1572872 | tf_op jit(solution)/shard_map/first_stage/ppermute | solution.py:33
  28.3 1.5 collective-permute-done.2
  29.8 0.5 collective-permute-start.14
  30.4 5.7 %collective-permute-done.9 = bf16[2,8,16,512]{3,2,1,0:T(8,128)(2,1)S(1)} collective-permute-done((bf16[2,8,16,512]{3,2,1,0:T(8,128)(2,1)S(1)}, bf16[2,8,16,512]{3,2,1,0:T(8,128)(2,1)S(1)}, u32[]{:S(2)}, u32[]{:S(2)}) %collective-permute-start.9) | collective-permute-done | bytes 262176 | tf_op jit(solution)/shard_map/first_stage/ppermute | solution.py:33
  36.2 1.6 collective-permute-start.13
  37.8 1.2 collective-permute-start.12
  39.0 0.9 collective-permute-done.7
  39.8 0.2 add_convert_fusion
  40.0 1.6 collective-permute-start.11
  41.7 0.7 collective-permute-done.15
  42.4 1.5 collective-permute-start.10
  44.0 8.0 %collective-permute-done.14 = bf16[4,8,16,512]{3,2,1,0:T(8,128)(2,1)S(1)} collective-permute-done((bf16[4,8,16,512]{3,2,1,0:T(8,128)(2,1)S(1)}, bf16[4,8,16,512]{3,2,1,0:T(8,128)(2,1)S(1)}, u32[]{:S(2)}, u32[]{:S(2)}) %collective-permute-start.14) | collective-permute-done | bytes 524320 | tf_op jit(solution)/shard_map/first_stage/ppermute | solution.py:33
  52.0 2.2 %collective-permute-done.13 = bf16[4,8,16,512]{3,2,1,0:T(8,128)(2,1)S(1)} collective-permute-done((bf16[4,8,16,512]{3,2,1,0:T(8,128)(2,1)S(1)}, bf16[4,8,16,512]{3,2,1,0:T(8,128)(2,1)S(1)}, u32[]{:S(2)}, u32[]{:S(2)}) %collective-permute-start.13) | collective-permute-done | bytes 524320 | tf_op jit(solution)/shard_map/first_stage/ppermute | solution.py:33
  54.1 0.4 fusion.13
  54.6 2.1 %collective-permute-start.18 = (bf16[8,16,512]{2,1,0:T(8,128)(2,1)S(1)}, bf16[8,16,512]{2,1,0:T(8,128)(2,1)S(1)}, u32[]{:S(2)}, u32[]{:S(2)}) collective-permute-start(bf16[8,16,512]{2,1,0:T(8,128)(2,1)S(1)} %get-tuple-element.49), channel_id=1, source_target_pairs={{0,3},{1,0},{2,1},{3,2},{4,7},{5,4},{6,5},{7,6},{8,11},{9,8},{10,9... | collective-permute-start | bytes 393224 | tf_op jit(solution)/shard_map/second_stage/ppermute | solution.py:33
  56.7 2.2 %collective-permute-start.17 = (bf16[8,16,512]{2,1,0:T(8,128)(2,1)S(1)}, bf16[8,16,512]{2,1,0:T(8,128)(2,1)S(1)}, u32[]{:S(2)}, u32[]{:S(2)}) collective-permute-start(bf16[8,16,512]{2,1,0:T(8,128)(2,1)S(1)} %get-tuple-element.50), channel_id=1, source_target_pairs={{0,2},{1,3},{2,0},{3,1},{4,6},{5,7},{6,4},{7,5},{8,10},{9,11},{10,... | collective-permute-start | bytes 393224 | tf_op jit(solution)/shard_map/second_stage/ppermute | solution.py:33
  58.9 1.3 collective-permute-start.16
  60.3 0.3 collective-permute-done.18
  60.6 3.5 %collective-permute-done.17 = bf16[8,16,512]{2,1,0:T(8,128)(2,1)S(1)} collective-permute-done((bf16[8,16,512]{2,1,0:T(8,128)(2,1)S(1)}, bf16[8,16,512]{2,1,0:T(8,128)(2,1)S(1)}, u32[]{:S(2)}, u32[]{:S(2)}) %collective-permute-start.17) | collective-permute-done | bytes 131104 | tf_op jit(solution)/shard_map/second_stage/ppermute | solution.py:33
  64.1 1.4 collective-permute-done.16
  65.6 0.2 collective-permute-start.30
  65.8 6.3 %collective-permute-start.29 = (f32[32,512]{1,0:T(8,128)S(1)}, f32[32,512]{1,0:T(8,128)S(1)}, u32[]{:S(2)}, u32[]{:S(2)}) collective-permute-start(f32[32,512]{1,0:T(8,128)S(1)} %pad_maximum_fusion.6), channel_id=1, source_target_pairs={{0,48},{8,56},{16,0},{24,8},{32,16},{40,24},{48,32},{56,40},{1,49}... | collective-permute-start | bytes 196616 | tf_op jit(solution)/shard_map/third_stage/ppermute | solution.py:33
  72.1 1.0 collective-permute-start.28
  73.1 4.5 %collective-permute-start.27 = (f32[32,512]{1,0:T(8,128)S(1)}, f32[32,512]{1,0:T(8,128)S(1)}, u32[]{:S(2)}, u32[]{:S(2)}) collective-permute-start(f32[32,512]{1,0:T(8,128)S(1)} %pad_maximum_fusion.4), channel_id=1, source_target_pairs={{0,32},{8,40},{16,48},{24,56},{32,0},{40,8},{48,16},{56,24},{1,33}... | collective-permute-start | bytes 196616 | tf_op jit(solution)/shard_map/third_stage/ppermute | solution.py:33
  77.7 0.5 collective-permute-start.26
  78.2 2.9 %collective-permute-start.25 = (f32[32,512]{1,0:T(8,128)S(1)}, f32[32,512]{1,0:T(8,128)S(1)}, u32[]{:S(2)}, u32[]{:S(2)}) collective-permute-start(f32[32,512]{1,0:T(8,128)S(1)} %pad_maximum_fusion.2), channel_id=1, source_target_pairs={{0,16},{8,24},{16,32},{24,40},{32,48},{40,56},{48,0},{56,8},{1,17}... | collective-permute-start | bytes 196616 | tf_op jit(solution)/shard_map/third_stage/ppermute | solution.py:33
  81.1 1.0 collective-permute-start.24
  82.1 0.6 collective-permute-done.27
  82.7 5.1 %collective-permute-done.26 = f32[32,512]{1,0:T(8,128)S(1)} collective-permute-done((f32[32,512]{1,0:T(8,128)S(1)}, f32[32,512]{1,0:T(8,128)S(1)}, u32[]{:S(2)}, u32[]{:S(2)}) %collective-permute-start.26) | collective-permute-done | bytes 65568 | tf_op jit(solution)/shard_map/third_stage/ppermute | solution.py:33
  87.9 0.7 bitcast_dynamic-update-slice_fusion.7
  88.6 1.4 collective-permute-start.31
  90.2 2.0 %collective-permute-start.21 = (bf16[1024,512]{1,0:T(8,128)(2,1)S(1)}, bf16[1024,512]{1,0:T(8,128)(2,1)S(1)}, u32[]{:S(2)}, u32[]{:S(2)}) collective-permute-start(bf16[1024,512]{1,0:T(8,128)(2,1)S(1)} %get-tuple-element.46), channel_id=1, source_target_pairs={{0,132},{128,0},{4,128},{132,4},{1,133},{129,1},{5,129},{133,5},{2... | collective-permute-start | bytes 3145736 | tf_op jit(solution)/shard_map/weights/ppermute | solution.py:33
  92.2 2.4 %collective-permute-start.32 = (bf16[32,512]{1,0:T(8,128)(2,1)S(1)}, bf16[32,512]{1,0:T(8,128)(2,1)S(1)}, u32[]{:S(2)}, u32[]{:S(2)}) collective-permute-start(bf16[32,512]{1,0:T(8,128)(2,1)S(1)} %get-tuple-element.36), channel_id=1, source_target_pairs={{0,16},{8,24},{16,32},{24,40},{32,48},{40,56},{48,0},{56,8},{1,17}... | collective-permute-start | bytes 98312 | tf_op jit(solution)/shard_map/fresh_weights/ppermute | solution.py:33
  94.7 2.4 %collective-permute-start.33 = (bf16[32,512]{1,0:T(8,128)(2,1)S(1)}, bf16[32,512]{1,0:T(8,128)(2,1)S(1)}, u32[]{:S(2)}, u32[]{:S(2)}) collective-permute-start(bf16[32,512]{1,0:T(8,128)(2,1)S(1)} %get-tuple-element.36), channel_id=1, source_target_pairs={{0,24},{8,32},{16,40},{24,48},{32,56},{40,0},{48,8},{56,16},{1,25}... | collective-permute-start | bytes 98312 | tf_op jit(solution)/shard_map/fresh_weights/ppermute | solution.py:33
  97.1 1.6 collective-permute-done.32
  98.7 2.1 %collective-permute-start.34 = (bf16[32,512]{1,0:T(8,128)(2,1)S(1)}, bf16[32,512]{1,0:T(8,128)(2,1)S(1)}, u32[]{:S(2)}, u32[]{:S(2)}) collective-permute-start(bf16[32,512]{1,0:T(8,128)(2,1)S(1)} %get-tuple-element.36), channel_id=1, source_target_pairs={{0,32},{8,40},{16,48},{24,56},{32,0},{40,8},{48,16},{56,24},{1,33}... | collective-permute-start | bytes 98312 | tf_op jit(solution)/shard_map/fresh_weights/ppermute | solution.py:33
  100.8 1.5 collective-permute-done.33
  102.4 1.0 collective-permute-start.35
  103.4 3.7 %collective-permute-done.34 = bf16[32,512]{1,0:T(8,128)(2,1)S(1)} collective-permute-done((bf16[32,512]{1,0:T(8,128)(2,1)S(1)}, bf16[32,512]{1,0:T(8,128)(2,1)S(1)}, u32[]{:S(2)}, u32[]{:S(2)}) %collective-permute-start.34) | collective-permute-done | bytes 32800 | tf_op jit(solution)/shard_map/fresh_weights/ppermute | solution.py:33
  107.1 1.5 collective-permute-start.36
  108.6 1.2 collective-permute-done.35
  109.8 2.1 %collective-permute-done.36 = bf16[32,512]{1,0:T(8,128)(2,1)S(1)} collective-permute-done((bf16[32,512]{1,0:T(8,128)(2,1)S(1)}, bf16[32,512]{1,0:T(8,128)(2,1)S(1)}, u32[]{:S(2)}, u32[]{:S(2)}) %collective-permute-start.36) | collective-permute-done | bytes 32800 | tf_op jit(solution)/shard_map/fresh_weights/ppermute | solution.py:33
  112.0 1.8 %collective-permute-done.37 = bf16[32,512]{1,0:T(8,128)(2,1)S(1)} collective-permute-done((bf16[32,512]{1,0:T(8,128)(2,1)S(1)}, bf16[32,512]{1,0:T(8,128)(2,1)S(1)}, u32[]{:S(2)}, u32[]{:S(2)}) %collective-permute-start.37) | collective-permute-done | bytes 32800 | tf_op jit(solution)/shard_map/fresh_weights/ppermute | solution.py:33
  113.7 3.8 %collective-permute-start.38 = (bf16[8,32,512]{2,1,0:T(8,128)(2,1)S(1)}, bf16[8,32,512]{2,1,0:T(8,128)(2,1)S(1)}, u32[]{:S(2)}, u32[]{:S(2)}) collective-permute-start(bf16[8,32,512]{2,1,0:T(8,128)(2,1)S(1)} %bitcast_dynamic-update-slice_fusion), channel_id=1, source_target_pairs={{0,4},{4,0},{1,5},{5,1},{2,6},{6,2},{3,7},{7,3},{8,12},{12,8},{9,1... | collective-permute-start | bytes 786440 | tf_op jit(solution)/shard_map/fresh_weights/ppermute | solution.py:33
  117.6 6.5 %collective-permute-done.38 = bf16[8,32,512]{2,1,0:T(8,128)(2,1)S(1)} collective-permute-done((bf16[8,32,512]{2,1,0:T(8,128)(2,1)S(1)}, bf16[8,32,512]{2,1,0:T(8,128)(2,1)S(1)}, u32[]{:S(2)}, u32[]{:S(2)}) %collective-permute-start.38) | collective-permute-done | bytes 262176 | tf_op jit(solution)/shard_map/fresh_weights/ppermute | solution.py:33
  124.4 0.5 collective-permute-start.23
  124.8 1.9 %collective-permute-start.40 = (bf16[2,8,32,512]{3,2,1,0:T(8,128)(2,1)S(1)}, bf16[2,8,32,512]{3,2,1,0:T(8,128)(2,1)S(1)}, u32[]{:S(2)}, u32[]{:S(2)}) collective-permute-start(bf16[2,8,32,512]{3,2,1,0:T(8,128)(2,1)S(1)} %pad_maximum_fusion.rest_0_), channel_id=1, source_target_pairs={{0,2},{1,3},{2,0},{3,1},{4,6},{5,7},{6,4},{7,5},{8,10},{9,11},{10,... | collective-permute-start | bytes 1572872 | tf_op jit(solution)/shard_map/fresh_weights/ppermute | solution.py:33
  126.8 22.2 %collective-permute-done.39.rest_1_ = bf16[2,8,32,512]{3,2,1,0:T(8,128)(2,1)S(1)} collective-permute-done((bf16[2,8,32,512]{3,2,1,0:T(8,128)(2,1)S(1)}, bf16[2,8,32,512]{3,2,1,0:T(8,128)(2,1)S(1)}, u32[]{:S(2)}, u32[]{:S(2)}) %collective-permute-start.39) | collective-permute-done | bytes 524320 | tf_op jit(solution)/shard_map/fresh_weights/ppermute | solution.py:33
  149.2 9.0 %collective-permute-done.41.rest_3_ = bf16[2,8,32,512]{3,2,1,0:T(8,128)(2,1)S(1)} collective-permute-done((bf16[2,8,32,512]{3,2,1,0:T(8,128)(2,1)S(1)}, bf16[2,8,32,512]{3,2,1,0:T(8,128)(2,1)S(1)}, u32[]{:S(2)}, u32[]{:S(2)}) %collective-permute-start.41) | collective-permute-done | bytes 524320 | tf_op jit(solution)/shard_map/fresh_weights/ppermute | solution.py:33
  158.2 2.1 %fresh_weights.1 = bf16[2048,512]{1,0:T(8,128)(2,1)} custom-call(s32[3]{0:T(128)S(1)} %pad_add_fusion.4.place, s32[1,64]{1,0:T(1,128)S(1)} %copy-done.1, bf16[2,8,32,512]{3,2,1,0:T(8,128)(2,1)S(1)} %pad_maximum_fusion.rest_0_, bf16[2,8,32,512]{3,2,1,0:T(8,128)(2,1)S(1)} %collective-permute-done.39.rest_1_, ...), custom_call_target="tpu_custom_call" | custom-call | tf_op jit(solution)/shard_map/fresh_weights/pallas_call | solution.py:159
  160.4 1.3 copy-done.3
  161.7 8.5 %weights.1 = bf16[256,8192]{1,0:T(8,128)(2,1)} custom-call(s32[2]{0:T(128)S(1)} %pad_add_fusion.place, bf16[256,512]{1,0:T(8,128)(2,1)S(1)} %copy-done, bf16[2048,512]{1,0:T(8,128)(2,1)} %rest_0_, bf16[2048,512]{1,0:T(8,128)(2,1)} %copy-done.3, bf16[1024,512]{1,0:T(8,128)(2,1)S(1)} %collective-permute-done.20.rest_2_, ...), custom_call_target="tpu_custom_call" | custom-call | tf_op jit(solution)/shard_map/weights/pallas_call | solution.py:123
  (69 shorter events, 1.3 us)
Async XLA Ops:
  0.7 3.7 %copy-start = (bf16[256,512]{1,0:T(8,128)(2,1)S(1)}, bf16[256,512]{1,0:T(8,128)(2,1)}, u32[]{:S(2)}) copy-start(bf16[256,512]{1,0:T(8,128)(2,1)} %key.1) | copy-start | bytes 786436
  0.7 6.6 %copy-start.1 = (s32[1,64]{1,0:T(1,128)S(1)}, s32[1,64]{1,0:T(1,128)}, u32[]{:S(2)}) copy-start(s32[1,64]{1,0:T(1,128)} %order.3) | copy-start | bytes 772
  3.8 3.4 %collective-permute-start = (bf16[256,2048]{1,0:T(8,128)(2,1)}, bf16[256,2048]{1,0:T(8,128)(2,1)S(1)}, u32[]{:S(2)}, u32[]{:S(2)}) collective-permute-start(bf16[256,2048]{1,0:T(8,128)(2,1)} %get-tuple-element.45), channel_id=1, source_target_pairs={{0,64},{64,0},{1,65},{65,1},{2,66},{66,2},{3,67},{67,3},{4,68},{68... | collective-permute-start | bytes 3145736 | tf_op jit(solution)/shard_map/core_swap/ppermute | solution.py:33
  3.8 14.8 %collective-permute-start.6 = (bf16[256,2048]{1,0:T(8,128)(2,1)}, bf16[256,2048]{1,0:T(8,128)(2,1)S(1)}, u32[]{:S(2)}, u32[]{:S(2)}) collective-permute-start(bf16[256,2048]{1,0:T(8,128)(2,1)} %get-tuple-element.44), channel_id=1, source_target_pairs={{0,64},{64,0},{1,65},{65,1},{2,66},{66,2},{3,67},{67,3},{4,68},{68... | collective-permute-start | bytes 3145736 | tf_op jit(solution)/shard_map/core_swap/ppermute | solution.py:33
  4.3 2.9 %collective-permute-start.1 = (bf16[256,512]{1,0:T(8,128)(2,1)S(1)}, bf16[256,512]{1,0:T(8,128)(2,1)S(1)}, u32[]{:S(2)}, u32[]{:S(2)}) collective-permute-start(bf16[256,512]{1,0:T(8,128)(2,1)S(1)} %copy-done), channel_id=1, source_target_pairs={{0,64},{64,0},{1,65},{65,1},{2,66},{66,2},{3,67},{67,3},{4,68},{68... | collective-permute-start | bytes 786440 | tf_op jit(solution)/shard_map/core_swap/ppermute | solution.py:33
  10.6 15.3 %collective-permute-start.4 = (bf16[2,8,16,512]{3,2,1,0:T(8,128)(2,1)S(1)}, bf16[2,8,16,512]{3,2,1,0:T(8,128)(2,1)S(1)}, u32[]{:S(2)}, u32[]{:S(2)}) collective-permute-start(bf16[2,8,16,512]{3,2,1,0:T(8,128)(2,1)S(1)} %get-tuple-element.23), channel_id=1, source_target_pairs={{0,3},{1,0},{2,1},{3,2},{4,7},{5,4},{6,5},{7,6},{8,11},{9,8},{10,9... | collective-permute-start | bytes 786440 | tf_op jit(solution)/shard_map/first_stage/ppermute | solution.py:33
  13.4 12.5 %collective-permute-start.3 = (bf16[2,8,16,512]{3,2,1,0:T(8,128)(2,1)S(1)}, bf16[2,8,16,512]{3,2,1,0:T(8,128)(2,1)S(1)}, u32[]{:S(2)}, u32[]{:S(2)}) collective-permute-start(bf16[2,8,16,512]{3,2,1,0:T(8,128)(2,1)S(1)} %get-tuple-element.22), channel_id=1, source_target_pairs={{0,2},{1,3},{2,0},{3,1},{4,6},{5,7},{6,4},{7,5},{8,10},{9,11},{10,... | collective-permute-start | bytes 786440 | tf_op jit(solution)/shard_map/first_stage/ppermute | solution.py:33
  14.2 15.6 %collective-permute-start.2 = (bf16[2,8,16,512]{3,2,1,0:T(8,128)(2,1)S(1)}, bf16[2,8,16,512]{3,2,1,0:T(8,128)(2,1)S(1)}, u32[]{:S(2)}, u32[]{:S(2)}) collective-permute-start(bf16[2,8,16,512]{3,2,1,0:T(8,128)(2,1)S(1)} %get-tuple-element.21), channel_id=1, source_target_pairs={{0,1},{1,2},{2,3},{3,0},{4,5},{5,6},{6,7},{7,4},{8,9},{9,10},{10,1... | collective-permute-start | bytes 786440 | tf_op jit(solution)/shard_map/first_stage/ppermute | solution.py:33
  15.1 3.5 %collective-permute-start.5 = (s32[1,64]{1,0:T(1,128)S(1)}, s32[1,64]{1,0:T(1,128)S(1)}, u32[]{:S(2)}, u32[]{:S(2)}) collective-permute-start(s32[1,64]{1,0:T(1,128)S(1)} %copy-done.1), channel_id=1, source_target_pairs={{0,128},{128,0},{1,129},{129,1},{2,130},{130,2},{3,131},{131,3},{4... | collective-permute-start | bytes 776 | tf_op jit(solution)/shard_map/core_swap/ppermute | solution.py:33
  22.0 14.2 %collective-permute-start.9 = (bf16[2,8,16,512]{3,2,1,0:T(8,128)(2,1)S(1)}, bf16[2,8,16,512]{3,2,1,0:T(8,128)(2,1)S(1)}, u32[]{:S(2)}, u32[]{:S(2)}) collective-permute-start(bf16[2,8,16,512]{3,2,1,0:T(8,128)(2,1)S(1)} %get-tuple-element.27), channel_id=1, source_target_pairs={{0,3},{1,0},{2,1},{3,2},{4,7},{5,4},{6,5},{7,6},{8,11},{9,8},{10,9... | collective-permute-start | bytes 786440 | tf_op jit(solution)/shard_map/first_stage/ppermute | solution.py:33
  24.4 13.4 %collective-permute-start.8 = (bf16[2,8,16,512]{3,2,1,0:T(8,128)(2,1)S(1)}, bf16[2,8,16,512]{3,2,1,0:T(8,128)(2,1)S(1)}, u32[]{:S(2)}, u32[]{:S(2)}) collective-permute-start(bf16[2,8,16,512]{3,2,1,0:T(8,128)(2,1)S(1)} %get-tuple-element.26), channel_id=1, source_target_pairs={{0,2},{1,3},{2,0},{3,1},{4,6},{5,7},{6,4},{7,5},{8,10},{9,11},{10,... | collective-permute-start | bytes 786440 | tf_op jit(solution)/shard_map/first_stage/ppermute | solution.py:33
  25.9 13.9 %collective-permute-start.7 = (bf16[2,8,16,512]{3,2,1,0:T(8,128)(2,1)S(1)}, bf16[2,8,16,512]{3,2,1,0:T(8,128)(2,1)S(1)}, u32[]{:S(2)}, u32[]{:S(2)}) collective-permute-start(bf16[2,8,16,512]{3,2,1,0:T(8,128)(2,1)S(1)} %get-tuple-element.25), channel_id=1, source_target_pairs={{0,1},{1,2},{2,3},{3,0},{4,5},{5,6},{6,7},{7,4},{8,9},{9,10},{10,1... | collective-permute-start | bytes 786440 | tf_op jit(solution)/shard_map/first_stage/ppermute | solution.py:33
  25.9 16.5 %collective-permute-start.15 = (bf16[4,8,16,512]{3,2,1,0:T(8,128)(2,1)S(1)}, bf16[4,8,16,512]{3,2,1,0:T(8,128)(2,1)S(1)}, u32[]{:S(2)}, u32[]{:S(2)}) collective-permute-start(bf16[4,8,16,512]{3,2,1,0:T(8,128)(2,1)S(1)} %get-tuple-element.31), channel_id=1, source_target_pairs={{0,4},{128,132},{4,0},{132,128},{1,5},{129,133},{5,1},{133,129},{2... | collective-permute-start | bytes 1572872 | tf_op jit(solution)/shard_map/first_stage/ppermute | solution.py:33
  29.8 22.1 %collective-permute-start.14 = (bf16[4,8,16,512]{3,2,1,0:T(8,128)(2,1)S(1)}, bf16[4,8,16,512]{3,2,1,0:T(8,128)(2,1)S(1)}, u32[]{:S(2)}, u32[]{:S(2)}) collective-permute-start(bf16[4,8,16,512]{3,2,1,0:T(8,128)(2,1)S(1)} %get-tuple-element.30), channel_id=1, source_target_pairs={{0,132},{128,0},{4,128},{132,4},{1,133},{129,1},{5,129},{133,5},{2... | collective-permute-start | bytes 1572872 | tf_op jit(solution)/shard_map/first_stage/ppermute | solution.py:33
  36.2 17.9 %collective-permute-start.13 = (bf16[4,8,16,512]{3,2,1,0:T(8,128)(2,1)S(1)}, bf16[4,8,16,512]{3,2,1,0:T(8,128)(2,1)S(1)}, u32[]{:S(2)}, u32[]{:S(2)}) collective-permute-start(bf16[4,8,16,512]{3,2,1,0:T(8,128)(2,1)S(1)} %get-tuple-element.29), channel_id=1, source_target_pairs={{0,128},{128,4},{4,132},{132,0},{1,129},{129,5},{5,133},{133,1},{2... | collective-permute-start | bytes 1572872 | tf_op jit(solution)/shard_map/first_stage/ppermute | solution.py:33
  37.8 21.1 %collective-permute-start.12 = (bf16[8,16,512]{2,1,0:T(8,128)(2,1)S(1)}, bf16[8,16,512]{2,1,0:T(8,128)(2,1)S(1)}, u32[]{:S(2)}, u32[]{:S(2)}) collective-permute-start(bf16[8,16,512]{2,1,0:T(8,128)(2,1)S(1)} %fusion.6), channel_id=1, source_target_pairs={{0,4},{128,132},{4,0},{132,128},{1,5},{129,133},{5,1},{133,129},{2... | collective-permute-start | bytes 393224 | tf_op jit(solution)/shard_map/second_stage/ppermute | solution.py:33
  40.0 20.2 %collective-permute-start.11 = (bf16[8,16,512]{2,1,0:T(8,128)(2,1)S(1)}, bf16[8,16,512]{2,1,0:T(8,128)(2,1)S(1)}, u32[]{:S(2)}, u32[]{:S(2)}) collective-permute-start(bf16[8,16,512]{2,1,0:T(8,128)(2,1)S(1)} %get-tuple-element.68), channel_id=1, source_target_pairs={{0,132},{128,0},{4,128},{132,4},{1,133},{129,1},{5,129},{133,5},{2... | collective-permute-start | bytes 393224 | tf_op jit(solution)/shard_map/second_stage/ppermute | solution.py:33
  42.4 17.8 %collective-permute-start.10 = (bf16[8,16,512]{2,1,0:T(8,128)(2,1)S(1)}, bf16[8,16,512]{2,1,0:T(8,128)(2,1)S(1)}, u32[]{:S(2)}, u32[]{:S(2)}) collective-permute-start(bf16[8,16,512]{2,1,0:T(8,128)(2,1)S(1)} %get-tuple-element.67), channel_id=1, source_target_pairs={{0,128},{128,4},{4,132},{132,0},{1,129},{129,5},{5,133},{133,1},{2... | collective-permute-start | bytes 393224 | tf_op jit(solution)/shard_map/second_stage/ppermute | solution.py:33
  54.5 27.6 %copy-start.2 = (bf16[2048,512]{1,0:T(8,128)(2,1)S(1)}, bf16[2048,512]{1,0:T(8,128)(2,1)}, u32[]{:S(2)}) copy-start(bf16[2048,512]{1,0:T(8,128)(2,1)} %rest_0_) | copy-start | bytes 6291460
  54.5 33.3 %copy-start.4 = (f32[32,512]{1,0:T(8,128)S(1)}, f32[32,512]{1,0:T(8,128)}, u32[]{:S(2)}) copy-start(f32[32,512]{1,0:T(8,128)} %param.10) | copy-start | bytes 196612
  54.6 33.3 %copy-start.5 = (f32[32,512]{1,0:T(8,128)S(1)}, f32[32,512]{1,0:T(8,128)}, u32[]{:S(2)}) copy-start(f32[32,512]{1,0:T(8,128)} %param.11) | copy-start | bytes 196612
  54.6 33.3 %copy-start.6 = (f32[32,512]{1,0:T(8,128)S(1)}, f32[32,512]{1,0:T(8,128)}, u32[]{:S(2)}) copy-start(f32[32,512]{1,0:T(8,128)} %param.12) | copy-start | bytes 196612
  54.6 6.0 %collective-permute-start.18 = (bf16[8,16,512]{2,1,0:T(8,128)(2,1)S(1)}, bf16[8,16,512]{2,1,0:T(8,128)(2,1)S(1)}, u32[]{:S(2)}, u32[]{:S(2)}) collective-permute-start(bf16[8,16,512]{2,1,0:T(8,128)(2,1)S(1)} %get-tuple-element.49), channel_id=1, source_target_pairs={{0,3},{1,0},{2,1},{3,2},{4,7},{5,4},{6,5},{7,6},{8,11},{9,8},{10,9... | collective-permute-start | bytes 393224 | tf_op jit(solution)/shard_map/second_stage/ppermute | solution.py:33
  56.7 7.5 %collective-permute-start.17 = (bf16[8,16,512]{2,1,0:T(8,128)(2,1)S(1)}, bf16[8,16,512]{2,1,0:T(8,128)(2,1)S(1)}, u32[]{:S(2)}, u32[]{:S(2)}) collective-permute-start(bf16[8,16,512]{2,1,0:T(8,128)(2,1)S(1)} %get-tuple-element.50), channel_id=1, source_target_pairs={{0,2},{1,3},{2,0},{3,1},{4,6},{5,7},{6,4},{7,5},{8,10},{9,11},{10,... | collective-permute-start | bytes 393224 | tf_op jit(solution)/shard_map/second_stage/ppermute | solution.py:33
  58.9 6.6 %collective-permute-start.16 = (bf16[8,16,512]{2,1,0:T(8,128)(2,1)S(1)}, bf16[8,16,512]{2,1,0:T(8,128)(2,1)S(1)}, u32[]{:S(2)}, u32[]{:S(2)}) collective-permute-start(bf16[8,16,512]{2,1,0:T(8,128)(2,1)S(1)} %get-tuple-element.48), channel_id=1, source_target_pairs={{0,1},{1,2},{2,3},{3,0},{4,5},{5,6},{6,7},{7,4},{8,9},{9,10},{10,1... | collective-permute-start | bytes 393224 | tf_op jit(solution)/shard_map/second_stage/ppermute | solution.py:33
  65.6 12.5 %collective-permute-start.30 = (f32[32,512]{1,0:T(8,128)S(1)}, f32[32,512]{1,0:T(8,128)S(1)}, u32[]{:S(2)}, u32[]{:S(2)}) collective-permute-start(f32[32,512]{1,0:T(8,128)S(1)} %pad_maximum_fusion.7), channel_id=1, source_target_pairs={{0,56},{8,0},{16,8},{24,16},{32,24},{40,32},{48,40},{56,48},{1,57}... | collective-permute-start | bytes 196616 | tf_op jit(solution)/shard_map/third_stage/ppermute | solution.py:33
  65.8 15.3 %collective-permute-start.29 = (f32[32,512]{1,0:T(8,128)S(1)}, f32[32,512]{1,0:T(8,128)S(1)}, u32[]{:S(2)}, u32[]{:S(2)}) collective-permute-start(f32[32,512]{1,0:T(8,128)S(1)} %pad_maximum_fusion.6), channel_id=1, source_target_pairs={{0,48},{8,56},{16,0},{24,8},{32,16},{40,24},{48,32},{56,40},{1,49}... | collective-permute-start | bytes 196616 | tf_op jit(solution)/shard_map/third_stage/ppermute | solution.py:33
  72.1 10.0 %collective-permute-start.28 = (f32[32,512]{1,0:T(8,128)S(1)}, f32[32,512]{1,0:T(8,128)S(1)}, u32[]{:S(2)}, u32[]{:S(2)}) collective-permute-start(f32[32,512]{1,0:T(8,128)S(1)} %pad_maximum_fusion.5), channel_id=1, source_target_pairs={{0,40},{8,48},{16,56},{24,0},{32,8},{40,16},{48,24},{56,32},{1,41}... | collective-permute-start | bytes 196616 | tf_op jit(solution)/shard_map/third_stage/ppermute | solution.py:33
  73.1 9.5 %collective-permute-start.27 = (f32[32,512]{1,0:T(8,128)S(1)}, f32[32,512]{1,0:T(8,128)S(1)}, u32[]{:S(2)}, u32[]{:S(2)}) collective-permute-start(f32[32,512]{1,0:T(8,128)S(1)} %pad_maximum_fusion.4), channel_id=1, source_target_pairs={{0,32},{8,40},{16,48},{24,56},{32,0},{40,8},{48,16},{56,24},{1,33}... | collective-permute-start | bytes 196616 | tf_op jit(solution)/shard_map/third_stage/ppermute | solution.py:33
  77.7 10.2 %collective-permute-start.26 = (f32[32,512]{1,0:T(8,128)S(1)}, f32[32,512]{1,0:T(8,128)S(1)}, u32[]{:S(2)}, u32[]{:S(2)}) collective-permute-start(f32[32,512]{1,0:T(8,128)S(1)} %pad_maximum_fusion.3), channel_id=1, source_target_pairs={{0,24},{8,32},{16,40},{24,48},{32,56},{40,0},{48,8},{56,16},{1,25}... | collective-permute-start | bytes 196616 | tf_op jit(solution)/shard_map/third_stage/ppermute | solution.py:33
  78.2 9.6 %collective-permute-start.25 = (f32[32,512]{1,0:T(8,128)S(1)}, f32[32,512]{1,0:T(8,128)S(1)}, u32[]{:S(2)}, u32[]{:S(2)}) collective-permute-start(f32[32,512]{1,0:T(8,128)S(1)} %pad_maximum_fusion.2), channel_id=1, source_target_pairs={{0,16},{8,24},{16,32},{24,40},{32,48},{40,56},{48,0},{56,8},{1,17}... | collective-permute-start | bytes 196616 | tf_op jit(solution)/shard_map/third_stage/ppermute | solution.py:33
  81.1 6.7 %collective-permute-start.24 = (f32[32,512]{1,0:T(8,128)S(1)}, f32[32,512]{1,0:T(8,128)S(1)}, u32[]{:S(2)}, u32[]{:S(2)}) collective-permute-start(f32[32,512]{1,0:T(8,128)S(1)} %pad_maximum_fusion.1), channel_id=1, source_target_pairs={{0,8},{8,16},{16,24},{24,32},{32,40},{40,48},{48,56},{56,0},{1,9},... | collective-permute-start | bytes 196616 | tf_op jit(solution)/shard_map/third_stage/ppermute | solution.py:33
  82.1 78.2 %collective-permute-start.19 = (bf16[2048,512]{1,0:T(8,128)(2,1)S(1)}, bf16[2048,512]{1,0:T(8,128)(2,1)S(1)}, u32[]{:S(2)}, u32[]{:S(2)}) collective-permute-start(bf16[2048,512]{1,0:T(8,128)(2,1)S(1)} %copy-done.2), channel_id=1, source_target_pairs={{0,64},{64,0},{1,65},{65,1},{2,66},{66,2},{3,67},{67,3},{4,68},{68... | collective-permute-start | bytes 6291464 | tf_op jit(solution)/shard_map/weights/ppermute | solution.py:33
  88.6 6.1 %collective-permute-start.31 = (bf16[32,512]{1,0:T(8,128)(2,1)S(1)}, bf16[32,512]{1,0:T(8,128)(2,1)S(1)}, u32[]{:S(2)}, u32[]{:S(2)}) collective-permute-start(bf16[32,512]{1,0:T(8,128)(2,1)S(1)} %get-tuple-element.36), channel_id=1, source_target_pairs={{0,8},{8,16},{16,24},{24,32},{32,40},{40,48},{48,56},{56,0},{1,9},... | collective-permute-start | bytes 98312 | tf_op jit(solution)/shard_map/fresh_weights/ppermute | solution.py:33
  90.1 34.1 %collective-permute-start.20 = (bf16[1024,512]{1,0:T(8,128)(2,1)S(1)}, bf16[1024,512]{1,0:T(8,128)(2,1)S(1)}, u32[]{:S(2)}, u32[]{:S(2)}) collective-permute-start(bf16[1024,512]{1,0:T(8,128)(2,1)S(1)} %get-tuple-element.47), channel_id=1, source_target_pairs={{0,128},{128,4},{4,132},{132,0},{1,129},{129,5},{5,133},{133,1},{2... | collective-permute-start | bytes 3145736 | tf_op jit(solution)/shard_map/weights/ppermute | solution.py:33
  90.2 34.1 %collective-permute-start.21 = (bf16[1024,512]{1,0:T(8,128)(2,1)S(1)}, bf16[1024,512]{1,0:T(8,128)(2,1)S(1)}, u32[]{:S(2)}, u32[]{:S(2)}) collective-permute-start(bf16[1024,512]{1,0:T(8,128)(2,1)S(1)} %get-tuple-element.46), channel_id=1, source_target_pairs={{0,132},{128,0},{4,128},{132,4},{1,133},{129,1},{5,129},{133,5},{2... | collective-permute-start | bytes 3145736 | tf_op jit(solution)/shard_map/weights/ppermute | solution.py:33
  92.2 6.5 %collective-permute-start.32 = (bf16[32,512]{1,0:T(8,128)(2,1)S(1)}, bf16[32,512]{1,0:T(8,128)(2,1)S(1)}, u32[]{:S(2)}, u32[]{:S(2)}) collective-permute-start(bf16[32,512]{1,0:T(8,128)(2,1)S(1)} %get-tuple-element.36), channel_id=1, source_target_pairs={{0,16},{8,24},{16,32},{24,40},{32,48},{40,56},{48,0},{56,8},{1,17}... | collective-permute-start | bytes 98312 | tf_op jit(solution)/shard_map/fresh_weights/ppermute | solution.py:33
  94.7 7.7 %collective-permute-start.33 = (bf16[32,512]{1,0:T(8,128)(2,1)S(1)}, bf16[32,512]{1,0:T(8,128)(2,1)S(1)}, u32[]{:S(2)}, u32[]{:S(2)}) collective-permute-start(bf16[32,512]{1,0:T(8,128)(2,1)S(1)} %get-tuple-element.36), channel_id=1, source_target_pairs={{0,24},{8,32},{16,40},{24,48},{32,56},{40,0},{48,8},{56,16},{1,25}... | collective-permute-start | bytes 98312 | tf_op jit(solution)/shard_map/fresh_weights/ppermute | solution.py:33
  98.7 8.3 %collective-permute-start.34 = (bf16[32,512]{1,0:T(8,128)(2,1)S(1)}, bf16[32,512]{1,0:T(8,128)(2,1)S(1)}, u32[]{:S(2)}, u32[]{:S(2)}) collective-permute-start(bf16[32,512]{1,0:T(8,128)(2,1)S(1)} %get-tuple-element.36), channel_id=1, source_target_pairs={{0,32},{8,40},{16,48},{24,56},{32,0},{40,8},{48,16},{56,24},{1,33}... | collective-permute-start | bytes 98312 | tf_op jit(solution)/shard_map/fresh_weights/ppermute | solution.py:33
  102.4 7.5 %collective-permute-start.35 = (bf16[32,512]{1,0:T(8,128)(2,1)S(1)}, bf16[32,512]{1,0:T(8,128)(2,1)S(1)}, u32[]{:S(2)}, u32[]{:S(2)}) collective-permute-start(bf16[32,512]{1,0:T(8,128)(2,1)S(1)} %get-tuple-element.36), channel_id=1, source_target_pairs={{0,40},{8,48},{16,56},{24,0},{32,8},{40,16},{48,24},{56,32},{1,41}... | collective-permute-start | bytes 98312 | tf_op jit(solution)/shard_map/fresh_weights/ppermute | solution.py:33
  107.1 4.9 %collective-permute-start.36 = (bf16[32,512]{1,0:T(8,128)(2,1)S(1)}, bf16[32,512]{1,0:T(8,128)(2,1)S(1)}, u32[]{:S(2)}, u32[]{:S(2)}) collective-permute-start(bf16[32,512]{1,0:T(8,128)(2,1)S(1)} %get-tuple-element.36), channel_id=1, source_target_pairs={{0,48},{8,56},{16,0},{24,8},{32,16},{40,24},{48,32},{56,40},{1,49}... | collective-permute-start | bytes 98312 | tf_op jit(solution)/shard_map/fresh_weights/ppermute | solution.py:33
  109.8 3.9 %collective-permute-start.37 = (bf16[32,512]{1,0:T(8,128)(2,1)S(1)}, bf16[32,512]{1,0:T(8,128)(2,1)S(1)}, u32[]{:S(2)}, u32[]{:S(2)}) collective-permute-start(bf16[32,512]{1,0:T(8,128)(2,1)S(1)} %get-tuple-element.36), channel_id=1, source_target_pairs={{0,56},{8,0},{16,8},{24,16},{32,24},{40,32},{48,40},{56,48},{1,57}... | collective-permute-start | bytes 98312 | tf_op jit(solution)/shard_map/fresh_weights/ppermute | solution.py:33
  113.7 10.3 %collective-permute-start.38 = (bf16[8,32,512]{2,1,0:T(8,128)(2,1)S(1)}, bf16[8,32,512]{2,1,0:T(8,128)(2,1)S(1)}, u32[]{:S(2)}, u32[]{:S(2)}) collective-permute-start(bf16[8,32,512]{2,1,0:T(8,128)(2,1)S(1)} %bitcast_dynamic-update-slice_fusion), channel_id=1, source_target_pairs={{0,4},{4,0},{1,5},{5,1},{2,6},{6,2},{3,7},{7,3},{8,12},{12,8},{9,1... | collective-permute-start | bytes 786440 | tf_op jit(solution)/shard_map/fresh_weights/ppermute | solution.py:33
  124.1 24.9 %collective-permute-start.39 = (bf16[2,8,32,512]{3,2,1,0:T(8,128)(2,1)S(1)}, bf16[2,8,32,512]{3,2,1,0:T(8,128)(2,1)S(1)}, u32[]{:S(2)}, u32[]{:S(2)}) collective-permute-start(bf16[2,8,32,512]{3,2,1,0:T(8,128)(2,1)S(1)} %pad_maximum_fusion.rest_0_), channel_id=1, source_target_pairs={{0,1},{1,2},{2,3},{3,0},{4,5},{5,6},{6,7},{7,4},{8,9},{9,10},{10,1... | collective-permute-start | bytes 1572872 | tf_op jit(solution)/shard_map/fresh_weights/ppermute | solution.py:33
  124.2 36.1 %collective-permute-start.22 = (bf16[1024,512]{1,0:T(8,128)(2,1)S(1)}, bf16[1024,512]{1,0:T(8,128)(2,1)S(1)}, u32[]{:S(2)}, u32[]{:S(2)}) collective-permute-start(bf16[1024,512]{1,0:T(8,128)(2,1)S(1)} %collective-permute-done.20.rest_2_), channel_id=1, source_target_pairs={{0,64},{64,0},{1,65},{65,1},{2,66},{66,2},{3,67},{67,3},{4,68},{68... | collective-permute-start | bytes 3145736 | tf_op jit(solution)/shard_map/weights/ppermute | solution.py:33
  124.4 36.0 %collective-permute-start.23 = (bf16[1024,512]{1,0:T(8,128)(2,1)S(1)}, bf16[1024,512]{1,0:T(8,128)(2,1)S(1)}, u32[]{:S(2)}, u32[]{:S(2)}) collective-permute-start(bf16[1024,512]{1,0:T(8,128)(2,1)S(1)} %collective-permute-done.21.rest_3_), channel_id=1, source_target_pairs={{0,64},{64,0},{1,65},{65,1},{2,66},{66,2},{3,67},{67,3},{4,68},{68... | collective-permute-start | bytes 3145736 | tf_op jit(solution)/shard_map/weights/ppermute | solution.py:33
  124.8 24.3 %collective-permute-start.40 = (bf16[2,8,32,512]{3,2,1,0:T(8,128)(2,1)S(1)}, bf16[2,8,32,512]{3,2,1,0:T(8,128)(2,1)S(1)}, u32[]{:S(2)}, u32[]{:S(2)}) collective-permute-start(bf16[2,8,32,512]{3,2,1,0:T(8,128)(2,1)S(1)} %pad_maximum_fusion.rest_0_), channel_id=1, source_target_pairs={{0,2},{1,3},{2,0},{3,1},{4,6},{5,7},{6,4},{7,5},{8,10},{9,11},{10,... | collective-permute-start | bytes 1572872 | tf_op jit(solution)/shard_map/fresh_weights/ppermute | solution.py:33
  149.0 9.2 %collective-permute-start.41 = (bf16[2,8,32,512]{3,2,1,0:T(8,128)(2,1)S(1)}, bf16[2,8,32,512]{3,2,1,0:T(8,128)(2,1)S(1)}, u32[]{:S(2)}, u32[]{:S(2)}) collective-permute-start(bf16[2,8,32,512]{3,2,1,0:T(8,128)(2,1)S(1)} %pad_maximum_fusion.rest_0_), channel_id=1, source_target_pairs={{0,3},{1,0},{2,1},{3,2},{4,7},{5,4},{6,5},{7,6},{8,11},{9,8},{10,9... | collective-permute-start | bytes 1572872 | tf_op jit(solution)/shard_map/fresh_weights/ppermute | solution.py:33
  160.3 1.3 copy-start.3

commit v2 on v1

--- a/solution.py
+++ b/solution.py
@@ -39,8 +39,8 @@
 
 def both_cores_kernel(far, place, order, own_tok, own_key, got_tok, got_key, *rest):
     outs, total = rest[:-1], rest[-1]
-    x, y, z = place[0], place[1], place[2]
-    rows, half = total.shape[0], outs[0].shape[2]
+    x, y = place[0], place[1]
+    rows, half = total.shape[0], outs[0].shape[3]
     cut = min(512, rows)
     for q in range(rows // cut):
         piece = slice(q * cut, (q + 1) * cut)
@@ -52,32 +52,26 @@
             return value.astype(jnp.bfloat16).astype(jnp.float32)
 
         total[piece, :] = partial(own_tok, own_key) + partial(got_tok, got_key)
-    steps_y = (1, 3) if far else (0, 2)
     for k in range(NX):
         to_x = lax.rem(x + k, NX)
-        for n, j in enumerate(steps_y):
+        for n, j in enumerate((1, 3) if far else (0, 2)):
             to_yh = lax.div(lax.rem(y + j, NY), NYL)
-            for m in range(NZ):
-                to_z = lax.rem(z + m, NZ)
+            for to_z in range(NZ):
                 block = order[0, (to_z * NYH + to_yh) * NX + to_x]
                 start = pl.multiple_of(block * (2 * half), 2 * half)
                 first = total[pl.ds(start, half), :]
                 second = total[pl.ds(start + half, half), :]
-                outs[k][n, m] = first.astype(outs[k].dtype)
-                outs[NX + n][k, m] = second.astype(outs[NX + n].dtype)
+                outs[0][to_x, n, to_z] = first.astype(outs[0].dtype)
+                outs[1 + n][k, to_z] = second.astype(outs[1 + n].dtype)
 
 
 def both_cores(far, place, order, own_tok, own_key, got_tok, got_key, block_rows):
     rows, width = got_tok.shape[1], own_key.shape[1]
     half = block_rows // 2
-    near = jnp.bfloat16 if far else jnp.float32
     shapes = [
-        jax.ShapeDtypeStruct((2, NZ, half, width), jnp.float32 if k == 0 else jnp.bfloat16)
-        for k in range(NX)
-    ]
-    shapes += [
-        jax.ShapeDtypeStruct((NX, NZ, half, width), near if n == 0 else jnp.bfloat16)
-        for n in range(2)
+        jax.ShapeDtypeStruct((NX, 2, NZ, half, width), jnp.bfloat16),
+        jax.ShapeDtypeStruct((NX, NZ, half, width), jnp.bfloat16 if far else jnp.float32),
+        jax.ShapeDtypeStruct((NX, NZ, half, width), jnp.bfloat16),
     ]
     return pl.pallas_call(
         functools.partial(both_cores_kernel, far),
@@ -85,7 +79,7 @@
             num_scalar_prefetch=2,
             grid=(1,),
             in_specs=[
-                pl.BlockSpec((own_tok.shape[0], rows), lambda i, place, order: (0, place[3])),
+                pl.BlockSpec((own_tok.shape[0], rows), lambda i, place, order: (0, place[2])),
                 vmem(),
                 vmem(),
                 vmem(),
@@ -142,17 +136,13 @@
 
 def place_kernel(place, order, *rest):
     parts, out = rest[:-1], rest[-1]
-    x, yh, z = place[0], place[1], place[2]
-    block_rows = parts[0].shape[2]
+    x = place[0]
+    block_rows = parts[0].shape[1]
     for k in range(NX):
         from_x = lax.rem(x + NX - k, NX)
-        for n in range(NYH):
-            from_yh = lax.rem(yh + n, NYH)
-            for m in range(NZ):
-                from_z = lax.rem(z + NZ - m, NZ)
-                block = order[0, (from_z * NYH + from_yh) * NX + from_x]
-                start = pl.multiple_of(block * block_rows, block_rows)
-                out[pl.ds(start, block_rows), :] = parts[k][n, m]
+        for n in range(NZ * NYH):
+            start = pl.multiple_of(order[0, n * NX + from_x] * block_rows, block_rows)
+            out[pl.ds(start, block_rows), :] = parts[k][n]
 
 
 def put_in_rows(place, order, parts, rows):
@@ -164,7 +154,7 @@
             in_specs=[vmem()] * len(parts),
             out_specs=vmem(),
         ),
-        out_shape=jax.ShapeDtypeStruct((rows, parts[0].shape[3]), parts[0].dtype),
+        out_shape=jax.ShapeDtypeStruct((rows, parts[0].shape[2]), parts[0].dtype),
         compiler_params=pltpu.CompilerParams(vmem_limit_bytes=VMEM_LIMIT),
     )(place, order, *parts)
 
@@ -184,8 +174,7 @@
 
     with jax.named_scope("core_swap"):
         got_key = send(key_cotangent, "c", 1)
-        near_order = writer
-        far_order = send(writer, "yl", 1)
+        order = {0: writer, 1: send(writer, "yl", 1)}
         summed = {}
         for far in (1, 0):
             shard = (yl ^ far) * NC
@@ -193,11 +182,11 @@
                 tokens_in, (0, (shard + 1 - c) * rows_here), (tok_rows, rows_here)
             )
             got_tok = send(other, "c", 1)
-            place = jnp.stack([x, y, z, shard + c]).astype(jnp.int32)
+            place = jnp.stack([x, y, shard + c]).astype(jnp.int32)
             summed[far] = both_cores(
                 far,
                 place,
-                far_order if far else near_order,
+                order[far],
                 tokens_in,
                 key_cotangent,
                 got_tok,
@@ -205,20 +194,25 @@
                 block_rows,
             )
 
+    with jax.named_scope("weights"):
+        low = send(key_weight[: rows_here // 2], "y", 1)
+        high = send(key_weight[rows_here // 2 :], "y", 3)
+        core = send(key_weight, "c", 1)
+        low_core, high_core = send(low, "c", 1), send(high, "c", 1)
+
     with jax.named_scope("first_stage"):
+        got = [
+            send(summed[1][1], "y", 1),
+            send(summed[1][2], "y", 3),
+            send(summed[0][2], "y", 2),
+        ]
         first = {}
         for far in (1, 0):
-            parts = summed[far][:NX]
-            got = [send(parts[k], "x", k) for k in range(1, NX)]
+            parts = lax.all_to_all(summed[far][0], "x", 0, 0, tiled=True)
             first[far] = f32(parts[0])
-            for value in got:
-                first[far] = first[far] + f32(value)
-        second = f32(summed[0][NX])
-        got = [
-            send(summed[1][NX], "y", 1),
-            send(summed[1][NX + 1], "y", 3),
-            send(summed[0][NX + 1], "y", 2),
-        ]
+            for k in range(1, NX):
+                first[far] = first[far] + f32(parts[k])
+        second = summed[0][1]
         for value in got:
             second = second + f32(value)
 
@@ -233,31 +227,10 @@
         for value in got_x:
             second_half = second_half + f32(value)
 
-    with jax.named_scope("weights"):
-        held, first_half, second_half = lax.optimization_barrier(
-            (key_weight, first_half, second_half)
-        )
-        low = send(held[: rows_here // 2], "y", 1)
-        high = send(held[rows_here // 2 :], "y", 3)
-        core = send(held, "c", 1)
-        low_core, high_core = send(low, "c", 1), send(high, "c", 1)
-        input_grad = input_grad_of(
-            jnp.stack([yl, c]).astype(jnp.int32),
-            key_cotangent,
-            held,
-            core,
-            low,
-            high,
-            low_core,
-            high_core,
-            width,
-        )
-
     with jax.named_scope("third_stage"):
-        blocks = [jnp.concatenate([first_half[m], second_half[m]], axis=0) for m in range(NZ)]
-        own_block = blocks[0]
-        for value in [send(blocks[m], "z", m) for m in range(1, NZ)]:
-            own_block = own_block + value
+        blocks = jnp.concatenate([first_half, second_half], axis=1)
+        parts = lax.all_to_all(blocks, "z", 0, 0, tiled=True)
+        own_block = jnp.sum(parts, axis=0)
 
     with jax.named_scope("adam"):
         devices = NYL * NC * NZ * NYH * NX
@@ -271,12 +244,22 @@
         )
 
     with jax.named_scope("fresh_weights"):
-        fresh = master_new.astype(jnp.bfloat16)
-        column = jnp.stack([fresh] + [send(fresh, "z", m) for m in range(1, NZ)])
-        plane = jnp.stack([column, send(column, "yh", 1)])
+        fresh = jnp.broadcast_to(
+            master_new.astype(jnp.bfloat16), (NZ * NYH,) + master_new.shape
+        )
+        plane = lax.all_to_all(fresh, ("z", "yh"), 0, 0, tiled=True)
         parts = [plane] + [send(plane, "x", k) for k in range(1, NX)]
-        place = jnp.stack([x, yh, z]).astype(jnp.int32)
-        weight_new = put_in_rows(place, near_order, parts, rows_here)
+        place = jnp.stack([x]).astype(jnp.int32)
+        weight_new = put_in_rows(place, writer, parts, rows_here)
+
+    with jax.named_scope("input_grad"):
+        held, core, low, high, low_core, high_core, _ = lax.optimization_barrier(
+            (key_weight, core, low, high, low_core, high_core, plane)
+        )
+        place = jnp.stack([yl, c]).astype(jnp.int32)
+        input_grad = input_grad_of(
+            place, key_cotangent, held, core, low, high, low_core, high_core, width
+        )
     return (input_grad, master_new, moment_one, moment_two, weight_new)
 
 

time: 170 us -> 141 us (0.83)
  the two profiles are of different devices: /device:TPU:40 before, /device:TPU:1 now
where the time goes in v2:
time: 141 us; the launch traced here: 140 us
  waiting for transfers between devices  51.9 us (37%)
  starting transfers between devices  50.6 us (36%)
  Pallas kernels  20.1 us (14%)
  local copies, waits for them, and re-layouts  9.27 us (7%)
  other arithmetic  7.15 us (5%)
    ppermute x21, waiting for transfers between devices, send(): lax.ppermute(value, ('yl', 'yh') if axis == 'y' else axis, shift(axis, st...  40.1 us
    ppermute x21, starting transfers between devices, send(): lax.ppermute(value, ('yl', 'yh') if axis == 'y' else axis, shift(axis, st...  29 us
    pallas_call x1, Pallas kernels, input_grad_of(): pl.pallas_call(input_grad_kernel, grid_spec=pltpu.PrefetchScalarGridSpec(...  9.22 us
    pallas_call x2, Pallas kernels, both_cores(): pl.pallas_call(functools.partial(both_cores_kernel, far), grid_spec=pltpu...  8.84 us
    all_to_all x2, starting transfers between devices, on_device(): parts = lax.all_to_all(summed[far][0], 'x', 0, 0, tiled=True)  7.77 us
    all_to_all x1, starting transfers between devices, on_device(): parts = lax.all_to_all(blocks, 'z', 0, 0, tiled=True)  7.64 us
    all_to_all x2, waiting for transfers between devices, on_device(): parts = lax.all_to_all(summed[far][0], 'x', 0, 0, tiled=True)  6.36 us
    all_to_all x1, starting transfers between devices, on_device(): plane = lax.all_to_all(fresh, ('z', 'yh'), 0, 0, tiled=True)  6.2 us
  transfers between devices with their start and end apart: 25, of which 12 were waited for; matrix products, arithmetic and copies ran while one was open for 7% of the time, Pallas kernels for 13%

profile of v2, /device:TPU:1, one launch (start us, length us, event | category | flops | bytes accessed | tf_op | source)
XLA Modules:
  0.0 139.9 jit_solution(935001440467889964)
XLA Ops:
  0.7 3.2 %constant_dynamic-slice_fusion = (bf16[256,2048]{1,0:T(8,128)(2,1)}, bf16[256,2048]{1,0:T(8,128)(2,1)}) fusion(bf16[256,8192]{1,0:T(8,128)(2,1)} %own_tok.3, s32[]{:T(128)S(6)} %select_n.7, s32[]{:T(128)S(6)} %select_n.6), kind=kLoop, calls=%fused_computation.26 | loop fusion | bytes 4194312 | tf_op jit(solution)/shard_map/core_swap/dynamic_slice | solution.py:181
  3.8 3.2 %collective-permute-start.5 = (bf16[256,2048]{1,0:T(8,128)(2,1)}, bf16[256,2048]{1,0:T(8,128)(2,1)S(1)}, u32[]{:S(2)}, u32[]{:S(2)}) collective-permute-start(bf16[256,2048]{1,0:T(8,128)(2,1)} %get-tuple-element.36), channel_id=1, source_target_pairs={{0,64},{64,0},{1,65},{65,1},{2,66},{66,2},{3,67},{67,3},{4,68},{68... | collective-permute-start | bytes 3145736 | tf_op jit(solution)/shard_map/core_swap/ppermute | solution.py:33
  7.1 0.0 collective-permute-start.8
  7.1 0.5 collective-permute-start.6
  7.6 0.1 pad_add_fusion.1.place
  7.7 2.4 %collective-permute-done.6.got_key = bf16[256,512]{1,0:T(8,128)(2,1)S(1)} collective-permute-done((bf16[256,512]{1,0:T(8,128)(2,1)S(1)}, bf16[256,512]{1,0:T(8,128)(2,1)S(1)}, u32[]{:S(2)}, u32[]{:S(2)}) %collective-permute-start.6) | collective-permute-done | bytes 262176 | tf_op jit(solution)/shard_map/core_swap/ppermute | solution.py:33
  10.1 0.0 collective-permute-done.5.got_tok
  10.1 1.0 copy-done.1
  11.1 1.2 copy-done.2
  12.3 4.3 %core_swap.2 = (bf16[4,2,8,16,512]{4,3,2,1,0:T(8,128)(2,1)}, f32[4,8,16,512]{3,2,1,0:T(8,128)S(1)}, bf16[4,8,16,512]{3,2,1,0:T(8,128)(2,1)S(1)}) custom-call(s32[3]{0:T(128)S(1)} %pad_add_fusion.1.place, s32[1,64]{1,0:T(1,128)S(1)} %copy-done.3, bf16[256,8192]{1,0:T(8,128)(2,1)} %own_tok.3, bf16[256,512]{1,0:T(8,128)(2,1)S(1)} %copy-done, ...), custom_call_target="tpu_custom_call" | custom-call | tf_op jit(solution)/shard_map/core_swap/pallas_call | solution.py:76
  16.6 4.2 %all-to-all-start = ((bf16[4,2,8,16,512]{4,3,2,1,0:T(8,128)(2,1)}), bf16[4,2,8,16,512]{4,3,2,1,0:T(8,128)(2,1)}, u32[]{:S(2)}, u32[]{:S(2)}) async-start(bf16[4,2,8,16,512]{4,3,2,1,0:T(8,128)(2,1)} %get-tuple-element.17), calls=%async_computation | async-start | bytes 2097152 | tf_op jit(solution)/shard_map/first_stage/all_to_all | solution.py:211
  20.9 0.1 collective-permute-start.7
  21.0 0.1 pad_add_fusion.3.place
  21.1 2.2 %collective-permute-start.14 = (bf16[4,8,16,512]{3,2,1,0:T(8,128)(2,1)S(1)}, bf16[4,8,16,512]{3,2,1,0:T(8,128)(2,1)}, u32[]{:S(2)}, u32[]{:S(2)}) collective-permute-start(bf16[4,8,16,512]{3,2,1,0:T(8,128)(2,1)S(1)} %get-tuple-element.22), channel_id=1, source_target_pairs={{0,4},{128,132},{4,0},{132,128},{1,5},{129,133},{5,1},{133,129},{2... | collective-permute-start | bytes 1572872 | tf_op jit(solution)/shard_map/first_stage/ppermute | solution.py:33
  23.3 0.1 collective-permute-done.7.order
  23.4 4.5 %core_swap.3 = (bf16[4,2,8,16,512]{4,3,2,1,0:T(8,128)(2,1)}, bf16[4,8,16,512]{3,2,1,0:T(8,128)(2,1)}, bf16[4,8,16,512]{3,2,1,0:T(8,128)(2,1)}) custom-call(s32[3]{0:T(128)S(1)} %pad_add_fusion.3.place, s32[1,64]{1,0:T(1,128)S(1)} %collective-permute-done.7.order, bf16[256,8192]{1,0:T(8,128)(2,1)} %own_tok.3, bf16[256,512]{1,0:T(8,128)(2,1)S(1)} %copy-done, ...), custom_call_target="tpu_custom_call" | custom-call | tf_op jit(solution)/shard_map/core_swap/pallas_call | solution.py:76
  27.9 1.6 %collective-permute-start.13 = (bf16[4,8,16,512]{3,2,1,0:T(8,128)(2,1)}, bf16[4,8,16,512]{3,2,1,0:T(8,128)(2,1)}, u32[]{:S(2)}, u32[]{:S(2)}) collective-permute-start(bf16[4,8,16,512]{3,2,1,0:T(8,128)(2,1)} %get-tuple-element.21), channel_id=1, source_target_pairs={{0,132},{128,0},{4,128},{132,4},{1,133},{129,1},{5,129},{133,5},{2... | collective-permute-start | bytes 1572872 | tf_op jit(solution)/shard_map/first_stage/ppermute | solution.py:33
  29.5 6.4 %all-to-all-done = bf16[4,2,8,16,512]{4,3,2,1,0:T(8,128)(2,1)} async-done(((bf16[4,2,8,16,512]{4,3,2,1,0:T(8,128)(2,1)}), bf16[4,2,8,16,512]{4,3,2,1,0:T(8,128)(2,1)}, u32[]{:S(2)}, u32[]{:S(2)}) %all-to-all-start) | async-done | bytes 1048608 | tf_op jit(solution)/shard_map/first_stage/all_to_all | solution.py:211
  35.8 3.5 %all-to-all-start.1 = ((bf16[4,2,8,16,512]{4,3,2,1,0:T(8,128)(2,1)}), bf16[4,2,8,16,512]{4,3,2,1,0:T(8,128)(2,1)S(1)}, u32[]{:S(2)}, u32[]{:S(2)}) async-start(bf16[4,2,8,16,512]{4,3,2,1,0:T(8,128)(2,1)} %get-tuple-element.18), calls=%async_computation.1 | async-start | bytes 2097152 | tf_op jit(solution)/shard_map/first_stage/all_to_all | solution.py:211
  39.3 6.5 %collective-permute-done.13 = bf16[4,8,16,512]{3,2,1,0:T(8,128)(2,1)} collective-permute-done((bf16[4,8,16,512]{3,2,1,0:T(8,128)(2,1)}, bf16[4,8,16,512]{3,2,1,0:T(8,128)(2,1)}, u32[]{:S(2)}, u32[]{:S(2)}) %collective-permute-start.13) | collective-permute-done | bytes 524320 | tf_op jit(solution)/shard_map/first_stage/ppermute | solution.py:33
  45.9 1.9 %collective-permute-done.12 = bf16[4,8,16,512]{3,2,1,0:T(8,128)(2,1)} collective-permute-done((bf16[4,8,16,512]{3,2,1,0:T(8,128)(2,1)}, bf16[4,8,16,512]{3,2,1,0:T(8,128)(2,1)}, u32[]{:S(2)}, u32[]{:S(2)}) %collective-permute-start.12) | collective-permute-done | bytes 524320 | tf_op jit(solution)/shard_map/first_stage/ppermute | solution.py:33
  47.8 2.7 %fusion.8 = (bf16[4,8,16,512]{3,2,1,0:T(8,128)(2,1)S(1)}, f32[4,8,16,512]{3,2,1,0:T(8,128)}) fusion(bf16[4,8,16,512]{3,2,1,0:T(8,128)(2,1)} %collective-permute-done.14, bf16[4,8,16,512]{3,2,1,0:T(8,128)(2,1)} %collective-permute-done.13, f32[4,8,16,512]{3,2,1,0:T(8,128)S(1)} %get-tuple-element.19, bf16[4,8,16,512]{3,2,1,0:T(8,128)(2,1)} %collective-permute-done.12), kind=kLoop, calls=%fused_computation.29 | loop fusion | flops 1835008 | bytes 4194304 | tf_op jit(solution)/shard_map/convert.2
  50.6 2.6 %collective-permute-start.17 = (bf16[8,16,512]{2,1,0:T(8,128)(2,1)S(1)}, bf16[8,16,512]{2,1,0:T(8,128)(2,1)S(1)}, u32[]{:S(2)}, u32[]{:S(2)}) collective-permute-start(bf16[8,16,512]{2,1,0:T(8,128)(2,1)S(1)} %get-tuple-element.40), channel_id=1, source_target_pairs={{0,3},{1,0},{2,1},{3,2},{4,7},{5,4},{6,5},{7,6},{8,11},{9,8},{10,9... | collective-permute-start | bytes 393224 | tf_op jit(solution)/shard_map/second_stage/ppermute | solution.py:33
  53.2 0.6 collective-permute-start.16
  53.7 0.6 collective-permute-start.15
  54.3 1.3 convert_add_fusion.1
  55.7 2.3 %collective-permute-start.11 = (bf16[8,16,512]{2,1,0:T(8,128)(2,1)S(1)}, bf16[8,16,512]{2,1,0:T(8,128)(2,1)S(1)}, u32[]{:S(2)}, u32[]{:S(2)}) collective-permute-start(bf16[8,16,512]{2,1,0:T(8,128)(2,1)S(1)} %fusion.6), channel_id=1, source_target_pairs={{0,4},{128,132},{4,0},{132,128},{1,5},{129,133},{5,1},{133,129},{2... | collective-permute-start | bytes 393224 | tf_op jit(solution)/shard_map/second_stage/ppermute | solution.py:33
  58.0 0.0 all-to-all-done.1
  58.0 0.2 add_convert_fusion
  58.2 1.8 %collective-permute-start.10 = (bf16[8,16,512]{2,1,0:T(8,128)(2,1)S(1)}, bf16[8,16,512]{2,1,0:T(8,128)(2,1)S(1)}, u32[]{:S(2)}, u32[]{:S(2)}) collective-permute-start(bf16[8,16,512]{2,1,0:T(8,128)(2,1)S(1)} %get-tuple-element.43), channel_id=1, source_target_pairs={{0,132},{128,0},{4,128},{132,4},{1,133},{129,1},{5,129},{133,5},{2... | collective-permute-start | bytes 393224 | tf_op jit(solution)/shard_map/second_stage/ppermute | solution.py:33
  59.9 0.0 collective-permute-start.9
  60.0 2.9 %collective-permute-done.15 = bf16[8,16,512]{2,1,0:T(8,128)(2,1)S(1)} collective-permute-done((bf16[8,16,512]{2,1,0:T(8,128)(2,1)S(1)}, bf16[8,16,512]{2,1,0:T(8,128)(2,1)S(1)}, u32[]{:S(2)}, u32[]{:S(2)}) %collective-permute-start.15) | collective-permute-done | bytes 131104 | tf_op jit(solution)/shard_map/second_stage/ppermute | solution.py:33
  62.8 1.0 fusion.2
  63.9 0.0 collective-permute-done.11
  63.9 0.0 collective-permute-done.10
  63.9 1.1 collective-permute-done.9
  65.0 0.1 fusion.5
  65.0 0.8 pad_maximum_fusion
  65.9 7.6 %all-to-all-start.2 = ((f32[8,32,512]{2,1,0:T(8,128)}), f32[8,32,512]{2,1,0:T(8,128)S(1)}, u32[]{:S(2)}, u32[]{:S(2)}) async-start(f32[8,32,512]{2,1,0:T(8,128)} %pad_maximum_fusion), calls=%async_computation.2 | async-start | bytes 1048576 | tf_op jit(solution)/shard_map/third_stage/all_to_all | solution.py:232
  73.5 0.0 copy-start.5
  73.5 0.0 copy-start.6
  73.6 3.2 %collective-permute-start = (bf16[2048,512]{1,0:T(8,128)(2,1)}, bf16[2048,512]{1,0:T(8,128)(2,1)}, u32[]{:S(2)}, u32[]{:S(2)}) collective-permute-start(bf16[2048,512]{1,0:T(8,128)(2,1)} %rest_0_), channel_id=1, source_target_pairs={{0,64},{64,0},{1,65},{65,1},{2,66},{66,2},{3,67},{67,3},{4,68},{68... | collective-permute-start | bytes 6291464 | tf_op jit(solution)/shard_map/weights/ppermute | solution.py:33
  76.8 3.0 %fusion.9 = (bf16[1024,512]{1,0:T(8,128)(2,1)}, bf16[1024,512]{1,0:T(8,128)(2,1)}) fusion(bf16[2048,512]{1,0:T(8,128)(2,1)} %rest_0_), kind=kLoop, calls=%fused_computation.30 | loop fusion | bytes 4194304 | tf_op jit(solution)/shard_map/weights/slice | solution.py:199
  79.8 2.7 %collective-permute-start.2 = (bf16[1024,512]{1,0:T(8,128)(2,1)}, bf16[1024,512]{1,0:T(8,128)(2,1)S(1)}, u32[]{:S(2)}, u32[]{:S(2)}) collective-permute-start(bf16[1024,512]{1,0:T(8,128)(2,1)} %get-tuple-element.37), channel_id=1, source_target_pairs={{0,132},{128,0},{4,128},{132,4},{1,133},{129,1},{5,129},{133,5},{2... | collective-permute-start | bytes 3145736 | tf_op jit(solution)/shard_map/weights/ppermute | solution.py:33
  82.4 5.4 %all-to-all-done.2 = f32[8,32,512]{2,1,0:T(8,128)S(1)} async-done(((f32[8,32,512]{2,1,0:T(8,128)}), f32[8,32,512]{2,1,0:T(8,128)S(1)}, u32[]{:S(2)}, u32[]{:S(2)}) %all-to-all-start.2) | async-done | bytes 524320 | tf_op jit(solution)/shard_map/third_stage/all_to_all | solution.py:232
  87.9 0.7 fusion.7
  88.6 0.8 broadcast_in_dim.3
  89.4 6.2 %all-to-all-start.3 = ((bf16[16,32,512]{2,1,0:T(8,128)(2,1)}), bf16[16,32,512]{2,1,0:T(8,128)(2,1)S(1)}, u32[]{:S(2)}, u32[]{:S(2)}) async-start(bf16[16,32,512]{2,1,0:T(8,128)(2,1)} %broadcast_in_dim.3), calls=%async_computation.3 | async-start | bytes 1048576 | tf_op jit(solution)/shard_map/fresh_weights/all_to_all | solution.py:250
  95.6 12.8 %collective-permute-done.1.rest_2_ = bf16[1024,512]{1,0:T(8,128)(2,1)S(1)} collective-permute-done((bf16[1024,512]{1,0:T(8,128)(2,1)}, bf16[1024,512]{1,0:T(8,128)(2,1)S(1)}, u32[]{:S(2)}, u32[]{:S(2)}) %collective-permute-start.1) | collective-permute-done | bytes 1048608 | tf_op jit(solution)/shard_map/weights/ppermute | solution.py:33
  108.4 1.0 collective-permute-start.3
  109.4 0.7 collective-permute-done.2.rest_3_
  110.1 1.6 %collective-permute-start.4 = (bf16[1024,512]{1,0:T(8,128)(2,1)S(1)}, bf16[1024,512]{1,0:T(8,128)(2,1)}, u32[]{:S(2)}, u32[]{:S(2)}) collective-permute-start(bf16[1024,512]{1,0:T(8,128)(2,1)S(1)} %collective-permute-done.2.rest_3_), channel_id=1, source_target_pairs={{0,64},{64,0},{1,65},{65,1},{2,66},{66,2},{3,67},{67,3},{4,68},{68... | collective-permute-start | bytes 3145736 | tf_op jit(solution)/shard_map/weights/ppermute | solution.py:33
  111.8 0.0 all-to-all-done.3.rest_0_
  111.8 1.6 %collective-permute-start.18 = (bf16[16,32,512]{2,1,0:T(8,128)(2,1)S(1)}, bf16[16,32,512]{2,1,0:T(8,128)(2,1)S(1)}, u32[]{:S(2)}, u32[]{:S(2)}) collective-permute-start(bf16[16,32,512]{2,1,0:T(8,128)(2,1)S(1)} %all-to-all-done.3.rest_0_), channel_id=1, source_target_pairs={{0,1},{1,2},{2,3},{3,0},{4,5},{5,6},{6,7},{7,4},{8,9},{9,10},{10,1... | collective-permute-start | bytes 1572872 | tf_op jit(solution)/shard_map/fresh_weights/ppermute | solution.py:33
  113.4 2.5 %collective-permute-start.19 = (bf16[16,32,512]{2,1,0:T(8,128)(2,1)S(1)}, bf16[16,32,512]{2,1,0:T(8,128)(2,1)S(1)}, u32[]{:S(2)}, u32[]{:S(2)}) collective-permute-start(bf16[16,32,512]{2,1,0:T(8,128)(2,1)S(1)} %all-to-all-done.3.rest_0_), channel_id=1, source_target_pairs={{0,2},{1,3},{2,0},{3,1},{4,6},{5,7},{6,4},{7,5},{8,10},{9,11},{10,... | collective-permute-start | bytes 1572872 | tf_op jit(solution)/shard_map/fresh_weights/ppermute | solution.py:33
  115.9 0.0 collective-permute-done.rest_1_
  115.9 1.1 collective-permute-start.20
  117.0 0.1 pad_add_fusion.place
  117.1 0.0 collective-permute-done.3.rest_4_
  117.1 0.0 collective-permute-done.4.rest_5_
  117.1 9.2 %input_grad.1 = bf16[256,8192]{1,0:T(8,128)(2,1)} custom-call(s32[2]{0:T(128)S(1)} %pad_add_fusion.place, bf16[256,512]{1,0:T(8,128)(2,1)S(1)} %copy-done, bf16[2048,512]{1,0:T(8,128)(2,1)} %rest_0_, bf16[2048,512]{1,0:T(8,128)(2,1)} %collective-permute-done.rest_1_, bf16[1024,512]{1,0:T(8,128)(2,1)S(1)} %collective-permute-done.1.rest_2_, ...), custom_call_target="tpu_custom_call" | custom-call | tf_op jit(solution)/shard_map/input_grad/pallas_call | solution.py:117
  126.3 8.9 %collective-permute-done.19.rest_2_ = bf16[16,32,512]{2,1,0:T(8,128)(2,1)S(1)} collective-permute-done((bf16[16,32,512]{2,1,0:T(8,128)(2,1)S(1)}, bf16[16,32,512]{2,1,0:T(8,128)(2,1)S(1)}, u32[]{:S(2)}, u32[]{:S(2)}) %collective-permute-start.19) | collective-permute-done | bytes 524320 | tf_op jit(solution)/shard_map/fresh_weights/ppermute | solution.py:33
  135.2 2.7 %collective-permute-done.20.rest_3_ = bf16[16,32,512]{2,1,0:T(8,128)(2,1)S(1)} collective-permute-done((bf16[16,32,512]{2,1,0:T(8,128)(2,1)S(1)}, bf16[16,32,512]{2,1,0:T(8,128)(2,1)S(1)}, u32[]{:S(2)}, u32[]{:S(2)}) %collective-permute-start.20) | collective-permute-done | bytes 524320 | tf_op jit(solution)/shard_map/fresh_weights/ppermute | solution.py:33
  137.9 2.0 %fresh_weights.1 = bf16[2048,512]{1,0:T(8,128)(2,1)} custom-call(s32[1]{0:T(128)} %bitcast.2.place, s32[1,64]{1,0:T(1,128)S(1)} %copy-done.3, bf16[16,32,512]{2,1,0:T(8,128)(2,1)S(1)} %all-to-all-done.3.rest_0_, bf16[16,32,512]{2,1,0:T(8,128)(2,1)S(1)} %collective-permute-done.18.rest_1_, bf16[16,32,512]{2,1,0:T(8,128)(2,1)S(1)} %collective-permute-done.19.rest_2_, ...), custom_call_target="tpu_custom_call" | custom-call | tf_op jit(solution)/shard_map/fresh_weights/pallas_call | solution.py:149
  (21 shorter events, 0.1 us)
Async XLA Ops:
  0.7 6.4 %copy-start = (bf16[256,512]{1,0:T(8,128)(2,1)S(1)}, bf16[256,512]{1,0:T(8,128)(2,1)}, u32[]{:S(2)}) copy-start(bf16[256,512]{1,0:T(8,128)(2,1)} %key.1) | copy-start | bytes 786436
  0.7 10.4 %copy-start.3 = (s32[1,64]{1,0:T(1,128)S(1)}, s32[1,64]{1,0:T(1,128)}, u32[]{:S(2)}) copy-start(s32[1,64]{1,0:T(1,128)} %order.3) | copy-start | bytes 772
  3.8 6.3 %collective-permute-start.5 = (bf16[256,2048]{1,0:T(8,128)(2,1)}, bf16[256,2048]{1,0:T(8,128)(2,1)S(1)}, u32[]{:S(2)}, u32[]{:S(2)}) collective-permute-start(bf16[256,2048]{1,0:T(8,128)(2,1)} %get-tuple-element.36), channel_id=1, source_target_pairs={{0,64},{64,0},{1,65},{65,1},{2,66},{66,2},{3,67},{67,3},{4,68},{68... | collective-permute-start | bytes 3145736 | tf_op jit(solution)/shard_map/core_swap/ppermute | solution.py:33
  7.1 16.3 %collective-permute-start.8 = (bf16[256,2048]{1,0:T(8,128)(2,1)}, bf16[256,2048]{1,0:T(8,128)(2,1)S(1)}, u32[]{:S(2)}, u32[]{:S(2)}) collective-permute-start(bf16[256,2048]{1,0:T(8,128)(2,1)} %get-tuple-element.35), channel_id=1, source_target_pairs={{0,64},{64,0},{1,65},{65,1},{2,66},{66,2},{3,67},{67,3},{4,68},{68... | collective-permute-start | bytes 3145736 | tf_op jit(solution)/shard_map/core_swap/ppermute | solution.py:33
  7.1 3.0 %collective-permute-start.6 = (bf16[256,512]{1,0:T(8,128)(2,1)S(1)}, bf16[256,512]{1,0:T(8,128)(2,1)S(1)}, u32[]{:S(2)}, u32[]{:S(2)}) collective-permute-start(bf16[256,512]{1,0:T(8,128)(2,1)S(1)} %copy-done), channel_id=1, source_target_pairs={{0,64},{64,0},{1,65},{65,1},{2,66},{66,2},{3,67},{67,3},{4,68},{68... | collective-permute-start | bytes 786440 | tf_op jit(solution)/shard_map/core_swap/ppermute | solution.py:33
  10.1 1.0 copy-start.1
  11.1 1.2 copy-start.2
  16.6 19.2 %all-to-all-start = ((bf16[4,2,8,16,512]{4,3,2,1,0:T(8,128)(2,1)}), bf16[4,2,8,16,512]{4,3,2,1,0:T(8,128)(2,1)}, u32[]{:S(2)}, u32[]{:S(2)}) async-start(bf16[4,2,8,16,512]{4,3,2,1,0:T(8,128)(2,1)} %get-tuple-element.17), calls=%async_computation | async-start | bytes 2097152 | tf_op jit(solution)/shard_map/first_stage/all_to_all | solution.py:211
  20.9 2.5 %collective-permute-start.7 = (s32[1,64]{1,0:T(1,128)S(1)}, s32[1,64]{1,0:T(1,128)S(1)}, u32[]{:S(2)}, u32[]{:S(2)}) collective-permute-start(s32[1,64]{1,0:T(1,128)S(1)} %copy-done.3), channel_id=1, source_target_pairs={{0,128},{128,0},{1,129},{129,1},{2,130},{130,2},{3,131},{131,3},{4... | collective-permute-start | bytes 776 | tf_op jit(solution)/shard_map/core_swap/ppermute | solution.py:33
  21.1 18.3 %collective-permute-start.14 = (bf16[4,8,16,512]{3,2,1,0:T(8,128)(2,1)S(1)}, bf16[4,8,16,512]{3,2,1,0:T(8,128)(2,1)}, u32[]{:S(2)}, u32[]{:S(2)}) collective-permute-start(bf16[4,8,16,512]{3,2,1,0:T(8,128)(2,1)S(1)} %get-tuple-element.22), channel_id=1, source_target_pairs={{0,4},{128,132},{4,0},{132,128},{1,5},{129,133},{5,1},{133,129},{2... | collective-permute-start | bytes 1572872 | tf_op jit(solution)/shard_map/first_stage/ppermute | solution.py:33
  27.9 18.0 %collective-permute-start.13 = (bf16[4,8,16,512]{3,2,1,0:T(8,128)(2,1)}, bf16[4,8,16,512]{3,2,1,0:T(8,128)(2,1)}, u32[]{:S(2)}, u32[]{:S(2)}) collective-permute-start(bf16[4,8,16,512]{3,2,1,0:T(8,128)(2,1)} %get-tuple-element.21), channel_id=1, source_target_pairs={{0,132},{128,0},{4,128},{132,4},{1,133},{129,1},{5,129},{133,5},{2... | collective-permute-start | bytes 1572872 | tf_op jit(solution)/shard_map/first_stage/ppermute | solution.py:33
  29.5 18.4 %collective-permute-start.12 = (bf16[4,8,16,512]{3,2,1,0:T(8,128)(2,1)}, bf16[4,8,16,512]{3,2,1,0:T(8,128)(2,1)}, u32[]{:S(2)}, u32[]{:S(2)}) collective-permute-start(bf16[4,8,16,512]{3,2,1,0:T(8,128)(2,1)} %get-tuple-element.20), channel_id=1, source_target_pairs={{0,128},{128,4},{4,132},{132,0},{1,129},{129,5},{5,133},{133,1},{2... | collective-permute-start | bytes 1572872 | tf_op jit(solution)/shard_map/first_stage/ppermute | solution.py:33
  35.8 22.2 %all-to-all-start.1 = ((bf16[4,2,8,16,512]{4,3,2,1,0:T(8,128)(2,1)}), bf16[4,2,8,16,512]{4,3,2,1,0:T(8,128)(2,1)S(1)}, u32[]{:S(2)}, u32[]{:S(2)}) async-start(bf16[4,2,8,16,512]{4,3,2,1,0:T(8,128)(2,1)} %get-tuple-element.18), calls=%async_computation.1 | async-start | bytes 2097152 | tf_op jit(solution)/shard_map/first_stage/all_to_all | solution.py:211
  50.6 9.4 %collective-permute-start.17 = (bf16[8,16,512]{2,1,0:T(8,128)(2,1)S(1)}, bf16[8,16,512]{2,1,0:T(8,128)(2,1)S(1)}, u32[]{:S(2)}, u32[]{:S(2)}) collective-permute-start(bf16[8,16,512]{2,1,0:T(8,128)(2,1)S(1)} %get-tuple-element.40), channel_id=1, source_target_pairs={{0,3},{1,0},{2,1},{3,2},{4,7},{5,4},{6,5},{7,6},{8,11},{9,8},{10,9... | collective-permute-start | bytes 393224 | tf_op jit(solution)/shard_map/second_stage/ppermute | solution.py:33
  53.2 6.8 %collective-permute-start.16 = (bf16[8,16,512]{2,1,0:T(8,128)(2,1)S(1)}, bf16[8,16,512]{2,1,0:T(8,128)(2,1)S(1)}, u32[]{:S(2)}, u32[]{:S(2)}) collective-permute-start(bf16[8,16,512]{2,1,0:T(8,128)(2,1)S(1)} %get-tuple-element.41), channel_id=1, source_target_pairs={{0,2},{1,3},{2,0},{3,1},{4,6},{5,7},{6,4},{7,5},{8,10},{9,11},{10,... | collective-permute-start | bytes 393224 | tf_op jit(solution)/shard_map/second_stage/ppermute | solution.py:33
  53.7 9.1 %collective-permute-start.15 = (bf16[8,16,512]{2,1,0:T(8,128)(2,1)S(1)}, bf16[8,16,512]{2,1,0:T(8,128)(2,1)S(1)}, u32[]{:S(2)}, u32[]{:S(2)}) collective-permute-start(bf16[8,16,512]{2,1,0:T(8,128)(2,1)S(1)} %get-tuple-element.39), channel_id=1, source_target_pairs={{0,1},{1,2},{2,3},{3,0},{4,5},{5,6},{6,7},{7,4},{8,9},{9,10},{10,1... | collective-permute-start | bytes 393224 | tf_op jit(solution)/shard_map/second_stage/ppermute | solution.py:33
  55.7 8.2 %collective-permute-start.11 = (bf16[8,16,512]{2,1,0:T(8,128)(2,1)S(1)}, bf16[8,16,512]{2,1,0:T(8,128)(2,1)S(1)}, u32[]{:S(2)}, u32[]{:S(2)}) collective-permute-start(bf16[8,16,512]{2,1,0:T(8,128)(2,1)S(1)} %fusion.6), channel_id=1, source_target_pairs={{0,4},{128,132},{4,0},{132,128},{1,5},{129,133},{5,1},{133,129},{2... | collective-permute-start | bytes 393224 | tf_op jit(solution)/shard_map/second_stage/ppermute | solution.py:33
  58.2 5.7 %collective-permute-start.10 = (bf16[8,16,512]{2,1,0:T(8,128)(2,1)S(1)}, bf16[8,16,512]{2,1,0:T(8,128)(2,1)S(1)}, u32[]{:S(2)}, u32[]{:S(2)}) collective-permute-start(bf16[8,16,512]{2,1,0:T(8,128)(2,1)S(1)} %get-tuple-element.43), channel_id=1, source_target_pairs={{0,132},{128,0},{4,128},{132,4},{1,133},{129,1},{5,129},{133,5},{2... | collective-permute-start | bytes 393224 | tf_op jit(solution)/shard_map/second_stage/ppermute | solution.py:33
  59.9 5.0 %collective-permute-start.9 = (bf16[8,16,512]{2,1,0:T(8,128)(2,1)S(1)}, bf16[8,16,512]{2,1,0:T(8,128)(2,1)S(1)}, u32[]{:S(2)}, u32[]{:S(2)}) collective-permute-start(bf16[8,16,512]{2,1,0:T(8,128)(2,1)S(1)} %get-tuple-element.42), channel_id=1, source_target_pairs={{0,128},{128,4},{4,132},{132,0},{1,129},{129,5},{5,133},{133,1},{2... | collective-permute-start | bytes 393224 | tf_op jit(solution)/shard_map/second_stage/ppermute | solution.py:33
  65.9 21.9 %all-to-all-start.2 = ((f32[8,32,512]{2,1,0:T(8,128)}), f32[8,32,512]{2,1,0:T(8,128)S(1)}, u32[]{:S(2)}, u32[]{:S(2)}) async-start(f32[8,32,512]{2,1,0:T(8,128)} %pad_maximum_fusion), calls=%async_computation.2 | async-start | bytes 1048576 | tf_op jit(solution)/shard_map/third_stage/all_to_all | solution.py:232
  73.5 14.3 %copy-start.4 = (f32[32,512]{1,0:T(8,128)S(1)}, f32[32,512]{1,0:T(8,128)}, u32[]{:S(2)}) copy-start(f32[32,512]{1,0:T(8,128)} %param.10) | copy-start | bytes 196612
  73.5 14.3 %copy-start.5 = (f32[32,512]{1,0:T(8,128)S(1)}, f32[32,512]{1,0:T(8,128)}, u32[]{:S(2)}) copy-start(f32[32,512]{1,0:T(8,128)} %param.11) | copy-start | bytes 196612
  73.5 14.3 %copy-start.6 = (f32[32,512]{1,0:T(8,128)S(1)}, f32[32,512]{1,0:T(8,128)}, u32[]{:S(2)}) copy-start(f32[32,512]{1,0:T(8,128)} %param.12) | copy-start | bytes 196612
  73.6 42.3 %collective-permute-start = (bf16[2048,512]{1,0:T(8,128)(2,1)}, bf16[2048,512]{1,0:T(8,128)(2,1)}, u32[]{:S(2)}, u32[]{:S(2)}) collective-permute-start(bf16[2048,512]{1,0:T(8,128)(2,1)} %rest_0_), channel_id=1, source_target_pairs={{0,64},{64,0},{1,65},{65,1},{2,66},{66,2},{3,67},{67,3},{4,68},{68... | collective-permute-start | bytes 6291464 | tf_op jit(solution)/shard_map/weights/ppermute | solution.py:33
  79.8 28.7 %collective-permute-start.1 = (bf16[1024,512]{1,0:T(8,128)(2,1)}, bf16[1024,512]{1,0:T(8,128)(2,1)S(1)}, u32[]{:S(2)}, u32[]{:S(2)}) collective-permute-start(bf16[1024,512]{1,0:T(8,128)(2,1)} %get-tuple-element.38), channel_id=1, source_target_pairs={{0,128},{128,4},{4,132},{132,0},{1,129},{129,5},{5,133},{133,1},{2... | collective-permute-start | bytes 3145736 | tf_op jit(solution)/shard_map/weights/ppermute | solution.py:33
  79.8 30.4 %collective-permute-start.2 = (bf16[1024,512]{1,0:T(8,128)(2,1)}, bf16[1024,512]{1,0:T(8,128)(2,1)S(1)}, u32[]{:S(2)}, u32[]{:S(2)}) collective-permute-start(bf16[1024,512]{1,0:T(8,128)(2,1)} %get-tuple-element.37), channel_id=1, source_target_pairs={{0,132},{128,0},{4,128},{132,4},{1,133},{129,1},{5,129},{133,5},{2... | collective-permute-start | bytes 3145736 | tf_op jit(solution)/shard_map/weights/ppermute | solution.py:33
  89.4 22.4 %all-to-all-start.3 = ((bf16[16,32,512]{2,1,0:T(8,128)(2,1)}), bf16[16,32,512]{2,1,0:T(8,128)(2,1)S(1)}, u32[]{:S(2)}, u32[]{:S(2)}) async-start(bf16[16,32,512]{2,1,0:T(8,128)(2,1)} %broadcast_in_dim.3), calls=%async_computation.3 | async-start | bytes 1048576 | tf_op jit(solution)/shard_map/fresh_weights/all_to_all | solution.py:250
  108.4 8.6 %collective-permute-start.3 = (bf16[1024,512]{1,0:T(8,128)(2,1)S(1)}, bf16[1024,512]{1,0:T(8,128)(2,1)}, u32[]{:S(2)}, u32[]{:S(2)}) collective-permute-start(bf16[1024,512]{1,0:T(8,128)(2,1)S(1)} %collective-permute-done.1.rest_2_), channel_id=1, source_target_pairs={{0,64},{64,0},{1,65},{65,1},{2,66},{66,2},{3,67},{67,3},{4,68},{68... | collective-permute-start | bytes 3145736 | tf_op jit(solution)/shard_map/weights/ppermute | solution.py:33
  110.1 6.9 %collective-permute-start.4 = (bf16[1024,512]{1,0:T(8,128)(2,1)S(1)}, bf16[1024,512]{1,0:T(8,128)(2,1)}, u32[]{:S(2)}, u32[]{:S(2)}) collective-permute-start(bf16[1024,512]{1,0:T(8,128)(2,1)S(1)} %collective-permute-done.2.rest_3_), channel_id=1, source_target_pairs={{0,64},{64,0},{1,65},{65,1},{2,66},{66,2},{3,67},{67,3},{4,68},{68... | collective-permute-start | bytes 3145736 | tf_op jit(solution)/shard_map/weights/ppermute | solution.py:33
  111.8 14.5 %collective-permute-start.18 = (bf16[16,32,512]{2,1,0:T(8,128)(2,1)S(1)}, bf16[16,32,512]{2,1,0:T(8,128)(2,1)S(1)}, u32[]{:S(2)}, u32[]{:S(2)}) collective-permute-start(bf16[16,32,512]{2,1,0:T(8,128)(2,1)S(1)} %all-to-all-done.3.rest_0_), channel_id=1, source_target_pairs={{0,1},{1,2},{2,3},{3,0},{4,5},{5,6},{6,7},{7,4},{8,9},{9,10},{10,1... | collective-permute-start | bytes 1572872 | tf_op jit(solution)/shard_map/fresh_weights/ppermute | solution.py:33
  113.4 21.8 %collective-permute-start.19 = (bf16[16,32,512]{2,1,0:T(8,128)(2,1)S(1)}, bf16[16,32,512]{2,1,0:T(8,128)(2,1)S(1)}, u32[]{:S(2)}, u32[]{:S(2)}) collective-permute-start(bf16[16,32,512]{2,1,0:T(8,128)(2,1)S(1)} %all-to-all-done.3.rest_0_), channel_id=1, source_target_pairs={{0,2},{1,3},{2,0},{3,1},{4,6},{5,7},{6,4},{7,5},{8,10},{9,11},{10,... | collective-permute-start | bytes 1572872 | tf_op jit(solution)/shard_map/fresh_weights/ppermute | solution.py:33
  115.9 22.0 %collective-permute-start.20 = (bf16[16,32,512]{2,1,0:T(8,128)(2,1)S(1)}, bf16[16,32,512]{2,1,0:T(8,128)(2,1)S(1)}, u32[]{:S(2)}, u32[]{:S(2)}) collective-permute-start(bf16[16,32,512]{2,1,0:T(8,128)(2,1)S(1)} %all-to-all-done.3.rest_0_), channel_id=1, source_target_pairs={{0,3},{1,0},{2,1},{3,2},{4,7},{5,4},{6,5},{7,6},{8,11},{9,8},{10,9... | collective-permute-start | bytes 1572872 | tf_op jit(solution)/shard_map/fresh_weights/ppermute | solution.py:33

commit v3 on v2

v3 whole, which is shorter than its diff:
```python
import functools

import jax
import jax.numpy as jnp
from jax import lax
from jax.experimental import pallas as pl
from jax.experimental.pallas import tpu as pltpu
from jax.sharding import Mesh
from jax.sharding import PartitionSpec as P

beta_first = 0.9
beta_second = 0.95
learn_rate = 0.0003
decay_rate = 0.1
adam_eps = 1e-08
step_count = 100

NYL, NC, NZ, NYH, NX = 2, 2, 8, 2, 4
NY = NYL * NYH
AXES = ("yl", "c", "z", "yh", "x")
MIB = 1024 * 1024


def shift(axis, step):
    if axis == "y":
        spot = lambda y: (y % NYL) * NYH + y // NYL
        return [(spot(y), spot((y + step) % NY)) for y in range(NY)]
    size = {"x": NX, "z": NZ, "c": NC, "yl": NYL, "yh": NYH}[axis]
    return [(i, (i + step) % size) for i in range(size)]


def send(value, axis, step):
    return lax.ppermute(value, ("yl", "yh") if axis == "y" else axis, shift(axis, step))


def vmem():
    return pl.BlockSpec(memory_space=pltpu.VMEM)


def spec(block, index):
    return pl.BlockSpec(block, index)


def params(mib):
    return pltpu.CompilerParams(vmem_limit_bytes=mib * MIB)


def columns_kernel(place, tokens, far, near, sems):
    copies = []
    for n, out in enumerate((far, near)):
        rows = out.shape[1]
        start = pl.multiple_of(place[n] * rows, rows)
        copies.append(pltpu.make_async_copy(tokens.at[:, pl.ds(start, rows)], out, sems.at[n]))
    for copy in copies:
        copy.start()
    for copy in copies:
        copy.wait()


def columns_of(place, tokens, rows):
    shape = jax.ShapeDtypeStruct((tokens.shape[0], rows), tokens.dtype)
    return pl.pallas_call(
        columns_kernel,
        grid_spec=pltpu.PrefetchScalarGridSpec(
            num_scalar_prefetch=1,
            grid=(1,),
            in_specs=[pl.BlockSpec(memory_space=pl.ANY)],
            out_specs=[pl.BlockSpec(memory_space=pl.ANY)] * 2,
            scratch_shapes=[pltpu.SemaphoreType.DMA((2,))],
        ),
        out_shape=[shape, shape],
        compiler_params=params(6),
    )(place, pltpu.with_memory_space_constraint(tokens, pltpu.HBM))


def partial_of(tok, key):
    value = lax.dot_general(tok, key, (((0,), (0,)), ((), ())), preferred_element_type=jnp.float32)
    return value.astype(jnp.bfloat16)


def own_kernel(place, tok, key, out):
    out[0] = partial_of(tok[...], key[...])


def own_partials(place, tokens, key, rows):
    cut = min(512, rows)
    steps = rows // cut
    return pl.pallas_call(
        own_kernel,
        grid_spec=pltpu.PrefetchScalarGridSpec(
            num_scalar_prefetch=1,
            grid=(2, steps),
            in_specs=[
                spec((tokens.shape[0], cut), lambda n, q, place: (0, place[n] * steps + q)),
                spec(key.shape, lambda n, q, place: (0, 0)),
            ],
            out_specs=spec((1, cut, key.shape[1]), lambda n, q, place: (n, q, 0)),
        ),
        out_shape=jax.ShapeDtypeStruct((2, rows, key.shape[1]), jnp.bfloat16),
        compiler_params=params(8),
    )(place, pltpu.with_memory_space_constraint(tokens, pltpu.HBM), key)


def both_cores_kernel(place, far_order, near_order, own, far, near, key, *rest):
    by_x, by_y, total = rest[:NX], rest[NX : NX + NY], rest[-1]
    x, y = place[0], place[1]
    rows, half = total.shape[0], by_x[0].shape[2]
    cut = min(512, rows)
    for s, (tok, order) in enumerate(((far, far_order), (near, near_order))):
        for q in range(rows // cut):
            piece = slice(q * cut, (q + 1) * cut)
            got = partial_of(tok[:, piece], key[...])
            total[piece, :] = own[s, piece, :].astype(jnp.float32) + got.astype(jnp.float32)
        for j in (1 - s, 3 - s):
            to_yh = lax.div(lax.rem(y + j, NY), NYL)
            for k in range(NX):
                to_x = lax.rem(x + k, NX)
                for to_z in range(NZ):
                    block = order[0, (to_z * NYH + to_yh) * NX + to_x]
                    start = pl.multiple_of(block * (2 * half), 2 * half)
                    first = total[pl.ds(start, half), :]
                    second = total[pl.ds(start + half, half), :]
                    by_x[k][j, to_z] = first.astype(by_x[k].dtype)
                    by_y[j][k, to_z] = second.astype(by_y[j].dtype)


def both_cores(place, far_order, near_order, own, far, near, key, block_rows):
    rows, width = own.shape[1], own.shape[2]
    half = block_rows // 2
    shapes = [
        jax.ShapeDtypeStruct((count, NZ, half, width), jnp.bfloat16 if n else jnp.float32)
        for count, steps in ((NY, NX), (NX, NY))
        for n in range(steps)
    ]
    return pl.pallas_call(
        both_cores_kernel,
        grid_spec=pltpu.PrefetchScalarGridSpec(
            num_scalar_prefetch=3,
            grid=(1,),
            in_specs=[vmem()] * 4,
            out_specs=[vmem()] * len(shapes),
            scratch_shapes=[pltpu.VMEM((rows, width), jnp.float32)],
        ),
        out_shape=shapes,
        compiler_params=params(20),
    )(place, far_order, near_order, own, far, near, key)


def input_grad_kernel(place, key, weight, *rest):
    out = rest[-1]
    out[...] = lax.dot_general(
        key[...], weight[...], (((1,), (1,)), ((), ())), preferred_element_type=jnp.float32
    ).astype(out.dtype)


def input_grad_of(place, key, weight, width, before=None):
    cut = weight.shape[0] // 4
    extra = [] if before is None else [before]
    return pl.pallas_call(
        input_grad_kernel,
        grid_spec=pltpu.PrefetchScalarGridSpec(
            num_scalar_prefetch=1,
            grid=(4,),
            in_specs=[
                spec(key.shape, lambda i, place: (0, 0)),
                spec((cut, key.shape[1]), lambda i, place: (i, 0)),
            ]
            + [pl.BlockSpec(memory_space=pl.ANY)] * len(extra),
            out_specs=spec(
                (key.shape[0], cut),
                lambda i, place: (0, (lax.div(i, 2) * NC + place[0]) * 2 + lax.rem(i, 2)),
            ),
        ),
        out_shape=jax.ShapeDtypeStruct((key.shape[0], width), jnp.bfloat16),
        input_output_aliases={3: 0} if extra else {},
        compiler_params=params(10),
    )(place, key, weight, *extra)


def place_kernel(place, order, *rest):
    parts, out = rest[:-1], rest[-1]
    x = place[0]
    block_rows = parts[0].shape[1]
    for k in range(NX):
        from_x = lax.rem(x + NX - k, NX)
        for n in range(NZ * NYH):
            start = pl.multiple_of(order[0, n * NX + from_x] * block_rows, block_rows)
            out[pl.ds(start, block_rows), :] = parts[k][n]


def put_in_rows(place, order, parts, rows):
    return pl.pallas_call(
        place_kernel,
        grid_spec=pltpu.PrefetchScalarGridSpec(
            num_scalar_prefetch=2,
            grid=(1,),
            in_specs=[vmem()] * len(parts),
            out_specs=vmem(),
        ),
        out_shape=jax.ShapeDtypeStruct((rows, parts[0].shape[2]), parts[0].dtype),
        compiler_params=params(8),
    )(place, order, *parts)


def f32(value):
    return value.astype(jnp.float32)


def total_of(values):
    total = f32(values[0])
    for value in values[1:]:
        total = total + f32(value)
    return total


def on_device(
    tokens_in, key_cotangent, key_weight, master_store, first_moment, second_moment, writer
):
    yl, c, _, yh, x = (lax.axis_index(name) for name in AXES)
    tok_rows, width = tokens_in.shape
    rows_here = key_weight.shape[0]
    block_rows = master_store.shape[0]

    with jax.named_scope("core_swap"):
        here, there = yl * NC, (1 - yl) * NC
        got_key = send(key_cotangent, "c", 1)
        far_order = send(writer, "yl", 1)
        far, near = columns_of(
            jnp.stack([there + 1 - c, here + 1 - c]).astype(jnp.int32), tokens_in, rows_here
        )
        far, near = send(far, "c", 1), send(near, "c", 1)
        own = own_partials(
            jnp.stack([there + c, here + c]).astype(jnp.int32), tokens_in, key_cotangent, rows_here
        )
        place = jnp.stack([x, yh * NYL + yl]).astype(jnp.int32)
        parts = both_cores(place, far_order, writer, own, far, near, got_key, block_rows)
        by_x, by_y = list(parts[:NX]), list(parts[NX:])

    def sums(parts):
        values = [total_of([part[n] for part in parts]) for n in range(parts[0].shape[0])]
        return values[:1] + [value.astype(jnp.bfloat16) for value in values[1:]]

    with jax.named_scope("first_stage"):
        second = sums(by_y[:1] + [send(by_y[j], "y", j) for j in (1, 3, 2)])
        first = sums(by_x[:1] + [send(by_x[k], "x", k) for k in (1, 3, 2)])

    with jax.named_scope("weights"):
        held, first, second = lax.optimization_barrier((key_weight, first, second))
        column = lax.all_gather(held, "yl", axis=0, tiled=True)

    with jax.named_scope("second_stage"):
        second_half = total_of(second[:1] + [send(second[k], "x", k) for k in range(1, NX)])
        first_half = total_of(first[:1] + [send(first[j], "y", j) for j in range(1, NY)])

    with jax.named_scope("third_stage"):
        blocks = jnp.concatenate([first_half, second_half], axis=1)
        parts = lax.all_to_all(blocks, "z", 0, 0, tiled=True)
        own_block = jnp.sum(parts, axis=0)

    with jax.named_scope("adam"):
        devices = NYL * NC * NZ * NYH * NX
        stored_grad = own_block * (tok_rows * devices) ** (-0.5)
        moment_one = beta_first * first_moment + (1.0 - beta_first) * stored_grad
        moment_two = beta_second * second_moment + (1.0 - beta_second) * stored_grad * stored_grad
        corrected_one = moment_one / (1.0 - beta_first**step_count)
        corrected_two = moment_two / (1.0 - beta_second**step_count)
        master_new = master_store - learn_rate * (
            corrected_one / (jnp.sqrt(corrected_two) + adam_eps) + decay_rate * master_store
        )

    with jax.named_scope("fresh_weights"):
        fresh = jnp.broadcast_to(
            master_new.astype(jnp.bfloat16), (NZ * NYH,) + master_new.shape
        )
        plane = lax.all_to_all(fresh, ("z", "yh"), 0, 0, tiled=True)
        parts = [plane] + [send(plane, "x", k) for k in range(1, NX)]

    with jax.named_scope("input_grad"):
        column, _ = lax.optimization_barrier((column, plane))
        other = send(column, "c", 1)
        core = jnp.stack([c]).astype(jnp.int32)
        held = pltpu.with_memory_space_constraint(column, pltpu.HBM)
        input_grad = input_grad_of(core, key_cotangent, held, width)
        input_grad = input_grad_of(1 - core, key_cotangent, other, width, input_grad)

    with jax.named_scope("rows"):
        input_grad, *parts = lax.optimization_barrier((input_grad, *parts))
        place = jnp.stack([x]).astype(jnp.int32)
        weight_new = put_in_rows(place, writer, parts, rows_here)
    return (input_grad, master_new, moment_one, moment_two, weight_new)


def solution(mesh):
    fine = Mesh(mesh.devices.reshape(NYL, NC, NZ, NYH, NX), AXES)
    shard, every = ("yl", "c"), AXES
    in_specs = (
        P(every, None),
        P(every, None),
        P(shard, None),
        P(every, None),
        P(every, None),
        P(every, None),
        P(shard, None),
    )
    out_specs = (P(every, None),) * 4 + (P(shard, None),)
    return jax.shard_map(
        on_device, mesh=fine, in_specs=in_specs, out_specs=out_specs, check_vma=False
    )
```

time: 141 us -> 232 us (1.65)
  Pallas kernels: 20.1 us -> 83.9 us
  blocking collectives: 0 us -> 36.5 us
  starting transfers between devices: 50.6 us -> 35.1 us
  between operations: 0.85 us -> 14.2 us
  local copies, waits for them, and re-layouts: 9.27 us -> 0.06 us
  waiting for transfers between devices: 51.9 us -> 59.9 us
  other arithmetic: 7.15 us -> 1.91 us
    pallas_call x2 -> x3, Pallas kernels: 8.84 us -> 73.8 us  [the longest x1 65.2 us: columns_of(): pl.pallas_call(columns_kernel, grid_spec=pltpu.PrefetchScalarGridSpec(num...]
    all_to_all x0 -> x2, blocking collectives: none -> 36.5 us  [the longest x1 20.4 us: on_device(): parts = lax.all_to_all(blocks, 'z', 0, 0, tiled=True)]
    all_gather x0 -> x1, waiting for transfers between devices: none -> 21.7 us  [on_device(): column = lax.all_gather(held, 'yl', axis=0, tiled=True)]
    all_to_all x4 -> x0, starting transfers between devices: 21.6 us -> none  [the longest x2 7.77 us: on_device(): parts = lax.all_to_all(summed[far][0], 'x', 0, 0, tiled=True)]
    all_to_all x4 -> x0, waiting for transfers between devices: 11.8 us -> none  [the longest x2 6.36 us: on_device(): parts = lax.all_to_all(summed[far][0], 'x', 0, 0, tiled=True)]
    ppermute x21 -> x20, starting transfers between devices: 29 us -> 35 us  [send(): lax.ppermute(value, ('yl', 'yh') if axis == 'y' else axis, shift(axis, st...]
    dynamic_slice x1 -> x0, local copies, waits for them, and re-layouts: 3.15 us -> none  [on_device(): lax.dynamic_slice(tokens_in, (0, (shard + 1 - c) * rows_here), (tok_rows,...]
    slice x1 -> x0, local copies, waits for them, and re-layouts: 2.99 us -> none  [on_device(): high = send(key_weight[rows_here // 2:], 'y', 3)]
  transfers between devices with their start and end apart: 25 -> 21, of which waited for: 12 -> 9; matrix products, arithmetic and copies ran while one was open for 7% -> 1% of each run, Pallas kernels for 13% -> 6%
where the time goes in v3:
time: 232 us
  Pallas kernels  83.9 us (36%)
  waiting for transfers between devices  59.9 us (26%)
  blocking collectives  36.5 us (16%)
  starting transfers between devices  35.1 us (15%)
  between operations  14.2 us (6%)
    pallas_call x1, Pallas kernels, columns_of(): pl.pallas_call(columns_kernel, grid_spec=pltpu.PrefetchScalarGridSpec(num...  65.2 us
    ppermute x20, waiting for transfers between devices, send(): lax.ppermute(value, ('yl', 'yh') if axis == 'y' else axis, shift(axis, st...  38.1 us
    ppermute x20, starting transfers between devices, send(): lax.ppermute(value, ('yl', 'yh') if axis == 'y' else axis, shift(axis, st...  35 us
    all_gather x1, waiting for transfers between devices, on_device(): column = lax.all_gather(held, 'yl', axis=0, tiled=True)  21.7 us
    all_to_all x1, blocking collectives, on_device(): parts = lax.all_to_all(blocks, 'z', 0, 0, tiled=True)  20.4 us
    all_to_all x1, blocking collectives, on_device(): plane = lax.all_to_all(fresh, ('z', 'yh'), 0, 0, tiled=True)  16.1 us
    pallas_call x2, Pallas kernels, input_grad_of(): pl.pallas_call(input_grad_kernel, grid_spec=pltpu.PrefetchScalarGridSpec(...  8.08 us
    pallas_call x1, Pallas kernels, own_partials(): pl.pallas_call(own_kernel, grid_spec=pltpu.PrefetchScalarGridSpec(num_sca...  6.16 us
  transfers between devices with their start and end apart: 21, of which 9 were waited for; matrix products, arithmetic and copies ran while one was open for 1% of the time, Pallas kernels for 6%

profile of v3, /device:TPU:1, one launch (start us, length us, event | category | flops | bytes accessed | tf_op | source)
XLA Modules:
  0.0 231.5 jit_solution(995431722490870005)
XLA Ops:
  7.2 0.0 copy-start
  7.2 0.0 copy-start.1
  7.2 0.0 all-gather.2.cloned.1.call-start
  7.2 0.1 pad_add_fusion.2.place
  7.3 65.2 %core_swap.4 = (bf16[256,2048]{1,0:T(8,128)(2,1)}, bf16[256,2048]{1,0:T(8,128)(2,1)}) custom-call(s32[2]{0:T(128)S(1)} %pad_add_fusion.2.place, bf16[256,8192]{1,0:T(8,128)(2,1)} %tokens.1), custom_call_target="tpu_custom_call" | custom-call | tf_op jit(solution)/shard_map/core_swap/pallas_call | solution.py:62
  72.5 3.3 %collective-permute-start.1 = (bf16[256,2048]{1,0:T(8,128)(2,1)}, bf16[256,2048]{1,0:T(8,128)(2,1)S(1)}, u32[]{:S(2)}, u32[]{:S(2)}) collective-permute-start(bf16[256,2048]{1,0:T(8,128)(2,1)} %get-tuple-element.30), channel_id=1, source_target_pairs={{0,64},{64,0},{1,65},{65,1},{2,66},{66,2},{3,67},{67,3},{4,68},{68... | collective-permute-start | bytes 3145736 | tf_op jit(solution)/shard_map/core_swap/ppermute | solution.py:33
  75.8 0.1 collective-permute-start.2
  75.9 0.0 copy-done
  75.9 0.4 collective-permute-start.3
  76.4 0.0 copy-done.1
  76.4 0.0 collective-permute-start
  76.4 0.1 pad_add_fusion.1.place
  76.4 0.1 pad_add_fusion.place
  76.5 6.2 %core_swap.3.own = bf16[2,2048,512]{2,1,0:T(8,128)(2,1)S(1)} custom-call(s32[2]{0:T(128)S(1)} %pad_add_fusion.1.place, bf16[256,8192]{1,0:T(8,128)(2,1)} %tokens.1, bf16[256,512]{1,0:T(8,128)(2,1)S(1)} %copy-done), custom_call_target="tpu_custom_call" | custom-call | tf_op jit(solution)/shard_map/core_swap/pallas_call | solution.py:88
  82.7 0.0 collective-permute-done.far_order
  82.7 0.0 collective-permute-done.3.key
  82.7 0.0 collective-permute-done.1.far
  82.7 0.0 collective-permute-done.2.near
  82.7 2.4 %core_swap.5 = (f32[4,8,16,512]{3,2,1,0:T(8,128)S(1)}, bf16[4,8,16,512]{3,2,1,0:T(8,128)(2,1)S(1)}, bf16[4,8,16,512]{3,2,1,0:T(8,128)(2,1)S(1)}, bf16[4,8,16,512...) custom-call(s32[2]{0:T(128)S(1)} %pad_add_fusion.place, ...), custom_call_target="tpu_custom_call" | custom-call | tf_op jit(solution)/shard_map/core_swap/pallas_call | solution.py:135
  85.2 1.6 collective-permute-start.7
  86.7 1.2 collective-permute-start.8
  87.9 1.0 collective-permute-start.9
  88.9 1.2 collective-permute-start.4
  90.1 1.5 collective-permute-start.5
  91.6 8.5 %collective-permute-done.7 = bf16[4,8,16,512]{3,2,1,0:T(8,128)(2,1)S(1)} collective-permute-done((bf16[4,8,16,512]{3,2,1,0:T(8,128)(2,1)S(1)}, bf16[4,8,16,512]{3,2,1,0:T(8,128)(2,1)S(1)}, u32[]{:S(2)}, u32[]{:S(2)}) %collective-permute-start.7) | collective-permute-done | bytes 524320 | tf_op jit(solution)/shard_map/first_stage/ppermute | solution.py:33
  100.1 1.8 collective-permute-start.6
  101.9 0.0 collective-permute-done.8
  101.9 8.9 %collective-permute-done.9 = bf16[4,8,16,512]{3,2,1,0:T(8,128)(2,1)S(1)} collective-permute-done((bf16[4,8,16,512]{3,2,1,0:T(8,128)(2,1)S(1)}, bf16[4,8,16,512]{3,2,1,0:T(8,128)(2,1)S(1)}, u32[]{:S(2)}, u32[]{:S(2)}) %collective-permute-start.9) | collective-permute-done | bytes 524320 | tf_op jit(solution)/shard_map/first_stage/ppermute | solution.py:33
  110.8 0.4 fusion.5
  111.2 0.0 collective-permute-done.4
  111.2 0.0 collective-permute-done.5
  111.2 3.8 %collective-permute-done.6 = bf16[4,8,16,512]{3,2,1,0:T(8,128)(2,1)S(1)} collective-permute-done((bf16[4,8,16,512]{3,2,1,0:T(8,128)(2,1)S(1)}, bf16[4,8,16,512]{3,2,1,0:T(8,128)(2,1)S(1)}, u32[]{:S(2)}, u32[]{:S(2)}) %collective-permute-start.6) | collective-permute-done | bytes 524320 | tf_op jit(solution)/shard_map/first_stage/ppermute | solution.py:33
  115.0 0.4 fusion.2
  115.4 0.0 all-gather.2.cloned.1.call-update
  115.4 0.1 collective-permute-start.10
  115.5 10.7 %collective-permute-start.11 = (bf16[8,16,512]{2,1,0:T(8,128)(2,1)S(1)}, bf16[8,16,512]{2,1,0:T(8,128)(2,1)S(1)}, u32[]{:S(2)}, u32[]{:S(2)}) collective-permute-start(bf16[8,16,512]{2,1,0:T(8,128)(2,1)S(1)} %get-tuple-element.43), channel_id=1, source_target_pairs={{0,4},{128,132},{4,0},{132,128},{1,5},{129,133},{5,1},{133,129},{2... | collective-permute-start | bytes 393224 | tf_op jit(solution)/shard_map/second_stage/ppermute | solution.py:33
  126.2 2.0 collective-permute-start.12
  128.2 1.1 collective-permute-start.13
  129.3 2.4 %collective-permute-start.14 = (bf16[8,16,512]{2,1,0:T(8,128)(2,1)S(1)}, bf16[8,16,512]{2,1,0:T(8,128)(2,1)S(1)}, u32[]{:S(2)}, u32[]{:S(2)}) collective-permute-start(bf16[8,16,512]{2,1,0:T(8,128)(2,1)S(1)} %get-tuple-element.47), channel_id=1, source_target_pairs={{0,2},{1,3},{2,0},{3,1},{4,6},{5,7},{6,4},{7,5},{8,10},{9,11},{10,... | collective-permute-start | bytes 393224 | tf_op jit(solution)/shard_map/second_stage/ppermute | solution.py:33
  131.8 0.0 collective-permute-done.10
  131.8 1.2 collective-permute-start.15
  132.9 0.0 collective-permute-done.11
  133.0 0.0 collective-permute-done.12
  133.0 0.1 convert_add_fusion.1
  133.0 0.2 collective-permute-done.13
  133.2 2.4 %collective-permute-done.14 = bf16[8,16,512]{2,1,0:T(8,128)(2,1)S(1)} collective-permute-done((bf16[8,16,512]{2,1,0:T(8,128)(2,1)S(1)}, bf16[8,16,512]{2,1,0:T(8,128)(2,1)S(1)}, u32[]{:S(2)}, u32[]{:S(2)}) %collective-permute-start.14) | collective-permute-done | bytes 131104 | tf_op jit(solution)/shard_map/second_stage/ppermute | solution.py:33
  135.6 0.3 collective-permute-done.15
  135.9 0.1 convert_add_fusion
  136.0 20.4 %all_to_all.10 = f32[8,32,512]{2,1,0:T(8,128)S(1)} all-to-all(f32[8,32,512]{2,1,0:T(8,128)S(1)} %pad_maximum_fusion), channel_id=1, replica_groups=mesh['yl'=2,'c'=2,'z'=8,'yh'=2,'x'=4] {'z'}, dimensions={0} | all-to-all | bytes 1048576 | tf_op jit(solution)/shard_map/third_stage/all_to_all | solution.py:257
  156.4 0.0 copy-done.2
  156.5 0.7 fusion.6
  157.2 16.1 %all_to_all.11.rest_0_ = bf16[16,32,512]{2,1,0:T(8,128)(2,1)S(1)} all-to-all(bf16[16,32,512]{2,1,0:T(8,128)(2,1)S(1)} %broadcast_in_dim.3), channel_id=1, replica_groups=mesh['yl'=2,'c'=2,'z'=8,'yh'=2,'x'=4] {'z','yh'}, dimensions={0} | all-to-all | bytes 1048576 | tf_op jit(solution)/shard_map/fresh_weights/all_to_all | solution.py:275
  173.3 21.7 %all-gather.2.cloned.1.call-done.weight = bf16[4096,512]{1,0:T(8,128)(2,1)} async-done(((bf16[2048,512]{1,0:T(8,128)(2,1)}), bf16[4096,512]{1,0:T(8,128)(2,1)}) %all-gather.2.cloned.1.call-update) | async-done | bytes 4194320 | tf_op jit(solution)/shard_map/weights/all_gather | solution.py:249
  195.1 0.7 collective-permute-start.16
  195.8 1.2 collective-permute-start.17
  196.9 2.4 %collective-permute-start.18 = (bf16[16,32,512]{2,1,0:T(8,128)(2,1)S(1)}, bf16[16,32,512]{2,1,0:T(8,128)(2,1)S(1)}, u32[]{:S(2)}, u32[]{:S(2)}) collective-permute-start(bf16[16,32,512]{2,1,0:T(8,128)(2,1)S(1)} %all_to_all.11.rest_0_), channel_id=1, source_target_pairs={{0,2},{1,3},{2,0},{3,1},{4,6},{5,7},{6,4},{7,5},{8,10},{9,11},{10,... | collective-permute-start | bytes 1572872 | tf_op jit(solution)/shard_map/fresh_weights/ppermute | solution.py:33
  199.4 1.2 collective-permute-start.19
  200.5 5.1 %input_grad.2.rest_0_ = bf16[256,8192]{1,0:T(8,128)(2,1)} custom-call(s32[1]{0:T(128)} %bitcast.place, bf16[256,512]{1,0:T(8,128)(2,1)S(1)} %copy-done, bf16[4096,512]{1,0:T(8,128)(2,1)} %all-gather.2.cloned.1.call-done.weight), custom_call_target="tpu_custom_call" | custom-call | tf_op jit(solution)/shard_map/input_grad/pallas_call | solution.py:159
  205.6 0.0 collective-permute-done.16.weight
  205.6 3.0 %input_grad.3 = bf16[256,8192]{1,0:T(8,128)(2,1)} custom-call(s32[1]{0:T(128)S(6)} %sub.15.place, bf16[256,512]{1,0:T(8,128)(2,1)S(1)} %copy-done, bf16[4096,512]{1,0:T(8,128)(2,1)S(1)} %collective-permute-done.16.weight, bf16[256,8192]{1,0:T(8,128)(2,1)} %input_grad.2.rest_0_), custom_call_target="tpu_custom_call", output_to_operand_aliasing={{}: (3, {})} | custom-call | tf_op jit(solution)/shard_map/input_grad/pallas_call | solution.py:159
  208.6 1.9 collective-permute-done.17.rest_1_
  210.5 12.2 %collective-permute-done.18.rest_2_ = bf16[16,32,512]{2,1,0:T(8,128)(2,1)S(1)} collective-permute-done((bf16[16,32,512]{2,1,0:T(8,128)(2,1)S(1)}, bf16[16,32,512]{2,1,0:T(8,128)(2,1)S(1)}, u32[]{:S(2)}, u32[]{:S(2)}) %collective-permute-start.18) | collective-permute-done | bytes 524320 | tf_op jit(solution)/shard_map/fresh_weights/ppermute | solution.py:33
  222.7 0.0 collective-permute-done.19.rest_3_
  222.7 2.0 rows.1
  (8 shorter events, 0.1 us)
Async XLA Ops:
  7.2 68.8 %copy-start = (bf16[256,512]{1,0:T(8,128)(2,1)S(1)}, bf16[256,512]{1,0:T(8,128)(2,1)}, u32[]{:S(2)}) copy-start(bf16[256,512]{1,0:T(8,128)(2,1)} %key.5) | copy-start | bytes 786436
  7.2 69.2 %copy-start.1 = (s32[1,64]{1,0:T(1,128)S(1)}, s32[1,64]{1,0:T(1,128)}, u32[]{:S(2)}) copy-start(s32[1,64]{1,0:T(1,128)} %order.1) | copy-start | bytes 772
  7.2 187.9 %all-gather.2.cloned.1.call-start = ((), (), s32[]{:S(2)}) async-start(), calls=%async_computation.2 | async-start | bytes 6291456 | tf_op jit(solution)/shard_map/weights/all_gather | solution.py:249
  72.5 10.2 %collective-permute-start.1 = (bf16[256,2048]{1,0:T(8,128)(2,1)}, bf16[256,2048]{1,0:T(8,128)(2,1)S(1)}, u32[]{:S(2)}, u32[]{:S(2)}) collective-permute-start(bf16[256,2048]{1,0:T(8,128)(2,1)} %get-tuple-element.30), channel_id=1, source_target_pairs={{0,64},{64,0},{1,65},{65,1},{2,66},{66,2},{3,67},{67,3},{4,68},{68... | collective-permute-start | bytes 3145736 | tf_op jit(solution)/shard_map/core_swap/ppermute | solution.py:33
  75.8 6.9 %collective-permute-start.2 = (bf16[256,2048]{1,0:T(8,128)(2,1)}, bf16[256,2048]{1,0:T(8,128)(2,1)S(1)}, u32[]{:S(2)}, u32[]{:S(2)}) collective-permute-start(bf16[256,2048]{1,0:T(8,128)(2,1)} %get-tuple-element.31), channel_id=1, source_target_pairs={{0,64},{64,0},{1,65},{65,1},{2,66},{66,2},{3,67},{67,3},{4,68},{68... | collective-permute-start | bytes 3145736 | tf_op jit(solution)/shard_map/core_swap/ppermute | solution.py:33
  75.9 6.8 %collective-permute-start.3 = (bf16[256,512]{1,0:T(8,128)(2,1)S(1)}, bf16[256,512]{1,0:T(8,128)(2,1)S(1)}, u32[]{:S(2)}, u32[]{:S(2)}) collective-permute-start(bf16[256,512]{1,0:T(8,128)(2,1)S(1)} %copy-done), channel_id=1, source_target_pairs={{0,64},{64,0},{1,65},{65,1},{2,66},{66,2},{3,67},{67,3},{4,68},{68... | collective-permute-start | bytes 786440 | tf_op jit(solution)/shard_map/core_swap/ppermute | solution.py:33
  76.4 6.3 %collective-permute-start = (s32[1,64]{1,0:T(1,128)S(1)}, s32[1,64]{1,0:T(1,128)S(1)}, u32[]{:S(2)}, u32[]{:S(2)}) collective-permute-start(s32[1,64]{1,0:T(1,128)S(1)} %copy-done.1), channel_id=1, source_target_pairs={{0,128},{128,0},{1,129},{129,1},{2,130},{130,2},{3,131},{131,3},{4... | collective-permute-start | bytes 776 | tf_op jit(solution)/shard_map/core_swap/ppermute | solution.py:33
  85.2 14.9 %collective-permute-start.7 = (bf16[4,8,16,512]{3,2,1,0:T(8,128)(2,1)S(1)}, bf16[4,8,16,512]{3,2,1,0:T(8,128)(2,1)S(1)}, u32[]{:S(2)}, u32[]{:S(2)}) collective-permute-start(bf16[4,8,16,512]{3,2,1,0:T(8,128)(2,1)S(1)} %get-tuple-element.37), channel_id=1, source_target_pairs={{0,128},{128,4},{4,132},{132,0},{1,129},{129,5},{5,133},{133,1},{2... | collective-permute-start | bytes 1572872 | tf_op jit(solution)/shard_map/first_stage/ppermute | solution.py:33
  86.7 15.2 %collective-permute-start.8 = (bf16[4,8,16,512]{3,2,1,0:T(8,128)(2,1)S(1)}, bf16[4,8,16,512]{3,2,1,0:T(8,128)(2,1)S(1)}, u32[]{:S(2)}, u32[]{:S(2)}) collective-permute-start(bf16[4,8,16,512]{3,2,1,0:T(8,128)(2,1)S(1)} %get-tuple-element.38), channel_id=1, source_target_pairs={{0,132},{128,0},{4,128},{132,4},{1,133},{129,1},{5,129},{133,5},{2... | collective-permute-start | bytes 1572872 | tf_op jit(solution)/shard_map/first_stage/ppermute | solution.py:33
  87.9 22.9 %collective-permute-start.9 = (bf16[4,8,16,512]{3,2,1,0:T(8,128)(2,1)S(1)}, bf16[4,8,16,512]{3,2,1,0:T(8,128)(2,1)S(1)}, u32[]{:S(2)}, u32[]{:S(2)}) collective-permute-start(bf16[4,8,16,512]{3,2,1,0:T(8,128)(2,1)S(1)} %get-tuple-element.39), channel_id=1, source_target_pairs={{0,4},{128,132},{4,0},{132,128},{1,5},{129,133},{5,1},{133,129},{2... | collective-permute-start | bytes 1572872 | tf_op jit(solution)/shard_map/first_stage/ppermute | solution.py:33
  88.9 22.3 %collective-permute-start.4 = (bf16[4,8,16,512]{3,2,1,0:T(8,128)(2,1)S(1)}, bf16[4,8,16,512]{3,2,1,0:T(8,128)(2,1)S(1)}, u32[]{:S(2)}, u32[]{:S(2)}) collective-permute-start(bf16[4,8,16,512]{3,2,1,0:T(8,128)(2,1)S(1)} %get-tuple-element.33), channel_id=1, source_target_pairs={{0,1},{1,2},{2,3},{3,0},{4,5},{5,6},{6,7},{7,4},{8,9},{9,10},{10,1... | collective-permute-start | bytes 1572872 | tf_op jit(solution)/shard_map/first_stage/ppermute | solution.py:33
  90.1 21.1 %collective-permute-start.5 = (bf16[4,8,16,512]{3,2,1,0:T(8,128)(2,1)S(1)}, bf16[4,8,16,512]{3,2,1,0:T(8,128)(2,1)S(1)}, u32[]{:S(2)}, u32[]{:S(2)}) collective-permute-start(bf16[4,8,16,512]{3,2,1,0:T(8,128)(2,1)S(1)} %get-tuple-element.34), channel_id=1, source_target_pairs={{0,3},{1,0},{2,1},{3,2},{4,7},{5,4},{6,5},{7,6},{8,11},{9,8},{10,9... | collective-permute-start | bytes 1572872 | tf_op jit(solution)/shard_map/first_stage/ppermute | solution.py:33
  100.1 14.9 %collective-permute-start.6 = (bf16[4,8,16,512]{3,2,1,0:T(8,128)(2,1)S(1)}, bf16[4,8,16,512]{3,2,1,0:T(8,128)(2,1)S(1)}, u32[]{:S(2)}, u32[]{:S(2)}) collective-permute-start(bf16[4,8,16,512]{3,2,1,0:T(8,128)(2,1)S(1)} %get-tuple-element.35), channel_id=1, source_target_pairs={{0,2},{1,3},{2,0},{3,1},{4,6},{5,7},{6,4},{7,5},{8,10},{9,11},{10,... | collective-permute-start | bytes 1572872 | tf_op jit(solution)/shard_map/first_stage/ppermute | solution.py:33
  115.0 41.5 %copy-start.2 = (f32[32,512]{1,0:T(8,128)S(1)}, f32[32,512]{1,0:T(8,128)}, u32[]{:S(2)}) copy-start(f32[32,512]{1,0:T(8,128)} %param.10) | copy-start | bytes 196612
  115.0 41.5 %copy-start.3 = (f32[32,512]{1,0:T(8,128)S(1)}, f32[32,512]{1,0:T(8,128)}, u32[]{:S(2)}) copy-start(f32[32,512]{1,0:T(8,128)} %param.11) | copy-start | bytes 196612
  115.0 41.5 %copy-start.4 = (f32[32,512]{1,0:T(8,128)S(1)}, f32[32,512]{1,0:T(8,128)}, u32[]{:S(2)}) copy-start(f32[32,512]{1,0:T(8,128)} %param.12) | copy-start | bytes 196612
  115.4 16.4 %collective-permute-start.10 = (bf16[8,16,512]{2,1,0:T(8,128)(2,1)S(1)}, bf16[8,16,512]{2,1,0:T(8,128)(2,1)S(1)}, u32[]{:S(2)}, u32[]{:S(2)}) collective-permute-start(bf16[8,16,512]{2,1,0:T(8,128)(2,1)S(1)} %get-tuple-element.42), channel_id=1, source_target_pairs={{0,128},{128,4},{4,132},{132,0},{1,129},{129,5},{5,133},{133,1},{2... | collective-permute-start | bytes 393224 | tf_op jit(solution)/shard_map/second_stage/ppermute | solution.py:33
  115.5 17.4 %collective-permute-start.11 = (bf16[8,16,512]{2,1,0:T(8,128)(2,1)S(1)}, bf16[8,16,512]{2,1,0:T(8,128)(2,1)S(1)}, u32[]{:S(2)}, u32[]{:S(2)}) collective-permute-start(bf16[8,16,512]{2,1,0:T(8,128)(2,1)S(1)} %get-tuple-element.43), channel_id=1, source_target_pairs={{0,4},{128,132},{4,0},{132,128},{1,5},{129,133},{5,1},{133,129},{2... | collective-permute-start | bytes 393224 | tf_op jit(solution)/shard_map/second_stage/ppermute | solution.py:33
  126.2 6.7 %collective-permute-start.12 = (bf16[8,16,512]{2,1,0:T(8,128)(2,1)S(1)}, bf16[8,16,512]{2,1,0:T(8,128)(2,1)S(1)}, u32[]{:S(2)}, u32[]{:S(2)}) collective-permute-start(bf16[8,16,512]{2,1,0:T(8,128)(2,1)S(1)} %get-tuple-element.44), channel_id=1, source_target_pairs={{0,132},{128,0},{4,128},{132,4},{1,133},{129,1},{5,129},{133,5},{2... | collective-permute-start | bytes 393224 | tf_op jit(solution)/shard_map/second_stage/ppermute | solution.py:33
  128.2 5.0 %collective-permute-start.13 = (bf16[8,16,512]{2,1,0:T(8,128)(2,1)S(1)}, bf16[8,16,512]{2,1,0:T(8,128)(2,1)S(1)}, u32[]{:S(2)}, u32[]{:S(2)}) collective-permute-start(bf16[8,16,512]{2,1,0:T(8,128)(2,1)S(1)} %get-tuple-element.46), channel_id=1, source_target_pairs={{0,1},{1,2},{2,3},{3,0},{4,5},{5,6},{6,7},{7,4},{8,9},{9,10},{10,1... | collective-permute-start | bytes 393224 | tf_op jit(solution)/shard_map/second_stage/ppermute | solution.py:33
  129.3 6.3 %collective-permute-start.14 = (bf16[8,16,512]{2,1,0:T(8,128)(2,1)S(1)}, bf16[8,16,512]{2,1,0:T(8,128)(2,1)S(1)}, u32[]{:S(2)}, u32[]{:S(2)}) collective-permute-start(bf16[8,16,512]{2,1,0:T(8,128)(2,1)S(1)} %get-tuple-element.47), channel_id=1, source_target_pairs={{0,2},{1,3},{2,0},{3,1},{4,6},{5,7},{6,4},{7,5},{8,10},{9,11},{10,... | collective-permute-start | bytes 393224 | tf_op jit(solution)/shard_map/second_stage/ppermute | solution.py:33
  131.8 4.1 %collective-permute-start.15 = (bf16[8,16,512]{2,1,0:T(8,128)(2,1)S(1)}, bf16[8,16,512]{2,1,0:T(8,128)(2,1)S(1)}, u32[]{:S(2)}, u32[]{:S(2)}) collective-permute-start(bf16[8,16,512]{2,1,0:T(8,128)(2,1)S(1)} %get-tuple-element.48), channel_id=1, source_target_pairs={{0,3},{1,0},{2,1},{3,2},{4,7},{5,4},{6,5},{7,6},{8,11},{9,8},{10,9... | collective-permute-start | bytes 393224 | tf_op jit(solution)/shard_map/second_stage/ppermute | solution.py:33
  195.1 10.5 %collective-permute-start.16 = (bf16[4096,512]{1,0:T(8,128)(2,1)}, bf16[4096,512]{1,0:T(8,128)(2,1)S(1)}, u32[]{:S(2)}, u32[]{:S(2)}) collective-permute-start(bf16[4096,512]{1,0:T(8,128)(2,1)} %all-gather.2.cloned.1.call-done.weight), channel_id=1, source_target_pairs={{0,64},{64,0},{1,65},{65,1},{2,66},{66,2},{3,67},{67,3},{4,68},{68... | collective-permute-start | bytes 12582920 | tf_op jit(solution)/shard_map/input_grad/ppermute | solution.py:33
  195.8 14.8 %collective-permute-start.17 = (bf16[16,32,512]{2,1,0:T(8,128)(2,1)S(1)}, bf16[16,32,512]{2,1,0:T(8,128)(2,1)S(1)}, u32[]{:S(2)}, u32[]{:S(2)}) collective-permute-start(bf16[16,32,512]{2,1,0:T(8,128)(2,1)S(1)} %all_to_all.11.rest_0_), channel_id=1, source_target_pairs={{0,1},{1,2},{2,3},{3,0},{4,5},{5,6},{6,7},{7,4},{8,9},{9,10},{10,1... | collective-permute-start | bytes 1572872 | tf_op jit(solution)/shard_map/fresh_weights/ppermute | solution.py:33
  196.9 25.7 %collective-permute-start.18 = (bf16[16,32,512]{2,1,0:T(8,128)(2,1)S(1)}, bf16[16,32,512]{2,1,0:T(8,128)(2,1)S(1)}, u32[]{:S(2)}, u32[]{:S(2)}) collective-permute-start(bf16[16,32,512]{2,1,0:T(8,128)(2,1)S(1)} %all_to_all.11.rest_0_), channel_id=1, source_target_pairs={{0,2},{1,3},{2,0},{3,1},{4,6},{5,7},{6,4},{7,5},{8,10},{9,11},{10,... | collective-permute-start | bytes 1572872 | tf_op jit(solution)/shard_map/fresh_weights/ppermute | solution.py:33
  199.4 23.3 %collective-permute-start.19 = (bf16[16,32,512]{2,1,0:T(8,128)(2,1)S(1)}, bf16[16,32,512]{2,1,0:T(8,128)(2,1)S(1)}, u32[]{:S(2)}, u32[]{:S(2)}) collective-permute-start(bf16[16,32,512]{2,1,0:T(8,128)(2,1)S(1)} %all_to_all.11.rest_0_), channel_id=1, source_target_pairs={{0,3},{1,0},{2,1},{3,2},{4,7},{5,4},{6,5},{7,6},{8,11},{9,8},{10,9... | collective-permute-start | bytes 1572872 | tf_op jit(solution)/shard_map/fresh_weights/ppermute | solution.py:33
Sparse Core Ops, SparseCore 0:
  115.5 79.4 all-gather.1

commit v4 on v3

--- a/solution.py
+++ b/solution.py
@@ -31,6 +31,15 @@
 
 def send(value, axis, step):
     return lax.ppermute(value, ("yl", "yh") if axis == "y" else axis, shift(axis, step))
+
+
+def cross(value):
+    pairs = []
+    for y in range(NY):
+        for c in range(NC):
+            to = (y + 1 + 2 * c) % NY
+            pairs.append(tuple(((n % NYL) * NC + c) * NYH + n // NYL for n in (y, to)))
+    return lax.ppermute(value, ("yl", "c", "yh"), pairs)
 
 
 def vmem():
@@ -65,7 +74,7 @@
             num_scalar_prefetch=1,
             grid=(1,),
             in_specs=[pl.BlockSpec(memory_space=pl.ANY)],
-            out_specs=[pl.BlockSpec(memory_space=pl.ANY)] * 2,
+            out_specs=[vmem(), vmem()],
             scratch_shapes=[pltpu.SemaphoreType.DMA((2,))],
         ),
         out_shape=[shape, shape],
@@ -83,7 +92,7 @@
 
 
 def own_partials(place, tokens, key, rows):
-    cut = min(512, rows)
+    cut = min(1024, rows)
     steps = rows // cut
     return pl.pallas_call(
         own_kernel,
@@ -146,15 +155,19 @@
     )(place, far_order, near_order, own, far, near, key)
 
 
-def input_grad_kernel(place, key, weight, *rest):
+def input_grad_kernel(place, key, first, second, *rest):
     out = rest[-1]
-    out[...] = lax.dot_general(
-        key[...], weight[...], (((1,), (1,)), ((), ())), preferred_element_type=jnp.float32
-    ).astype(out.dtype)
-
-
-def input_grad_of(place, key, weight, width, before=None):
-    cut = weight.shape[0] // 4
+    for n, weight in enumerate((first, second)):
+
+        @pl.when(lax.div(pl.program_id(0), 2) == n)
+        def _(weight=weight):
+            out[...] = lax.dot_general(
+                key[...], weight[...], (((1,), (1,)), ((), ())), preferred_element_type=jnp.float32
+            ).astype(out.dtype)
+
+
+def input_grad_of(place, key, first, second, width, before=None):
+    cut = first.shape[0] // 2
     extra = [] if before is None else [before]
     return pl.pallas_call(
         input_grad_kernel,
@@ -163,43 +176,57 @@
             grid=(4,),
             in_specs=[
                 spec(key.shape, lambda i, place: (0, 0)),
-                spec((cut, key.shape[1]), lambda i, place: (i, 0)),
+                spec((cut, key.shape[1]), lambda i, place: (jnp.minimum(i, 1), 0)),
+                spec((cut, key.shape[1]), lambda i, place: (jnp.maximum(i - 2, 0), 0)),
             ]
             + [pl.BlockSpec(memory_space=pl.ANY)] * len(extra),
             out_specs=spec(
                 (key.shape[0], cut),
-                lambda i, place: (0, (lax.div(i, 2) * NC + place[0]) * 2 + lax.rem(i, 2)),
+                lambda i, place: (0, place[lax.div(i, 2)] * 2 + lax.rem(i, 2)),
             ),
         ),
         out_shape=jax.ShapeDtypeStruct((key.shape[0], width), jnp.bfloat16),
-        input_output_aliases={3: 0} if extra else {},
-        compiler_params=params(10),
-    )(place, key, weight, *extra)
-
-
-def place_kernel(place, order, *rest):
-    parts, out = rest[:-1], rest[-1]
+        input_output_aliases={4: 0} if extra else {},
+        compiler_params=params(12),
+    )(place, key, first, second, *extra)
+
+
+def rows_kernel(steps, place, order, *rest):
+    parts, out, sems = rest[: len(steps)], rest[-2], rest[-1]
     x = place[0]
     block_rows = parts[0].shape[1]
-    for k in range(NX):
+    copies = []
+    for i, k in enumerate(steps):
         from_x = lax.rem(x + NX - k, NX)
         for n in range(NZ * NYH):
             start = pl.multiple_of(order[0, n * NX + from_x] * block_rows, block_rows)
-            out[pl.ds(start, block_rows), :] = parts[k][n]
-
-
-def put_in_rows(place, order, parts, rows):
-    return pl.pallas_call(
-        place_kernel,
+            copies.append(
+                pltpu.make_async_copy(
+                    parts[i].at[n], out.at[pl.ds(start, block_rows), :], sems.at[i, n]
+                )
+            )
+    for copy in copies:
+        copy.start()
+    for copy in copies:
+        copy.wait()
+
+
+def put_in_rows(place, order, parts, rows, before=None):
+    steps, values = tuple(parts), list(parts.values())
+    extra = [] if before is None else [before]
+    return pl.pallas_call(
+        functools.partial(rows_kernel, steps),
         grid_spec=pltpu.PrefetchScalarGridSpec(
             num_scalar_prefetch=2,
             grid=(1,),
-            in_specs=[vmem()] * len(parts),
-            out_specs=vmem(),
-        ),
-        out_shape=jax.ShapeDtypeStruct((rows, parts[0].shape[2]), parts[0].dtype),
-        compiler_params=params(8),
-    )(place, order, *parts)
+            in_specs=[vmem()] * len(values) + [pl.BlockSpec(memory_space=pl.ANY)] * len(extra),
+            out_specs=pl.BlockSpec(memory_space=pl.ANY),
+            scratch_shapes=[pltpu.SemaphoreType.DMA((len(steps), NZ * NYH))],
+        ),
+        out_shape=jax.ShapeDtypeStruct((rows, values[0].shape[2]), values[0].dtype),
+        input_output_aliases={2 + len(values): 0} if extra else {},
+        compiler_params=params(6),
+    )(place, order, *values, *extra)
 
 
 def f32(value):
@@ -240,22 +267,29 @@
         values = [total_of([part[n] for part in parts]) for n in range(parts[0].shape[0])]
         return values[:1] + [value.astype(jnp.bfloat16) for value in values[1:]]
 
+    def exchange(over_x, over_y):
+        steps = [("x", 1), ("y", 1), ("y", 2), ("y", 3), ("x", 3), ("x", 2)]
+        values = [send((over_x if axis == "x" else over_y)[n], axis, n) for axis, n in steps]
+        got = dict(zip(steps, lax.optimization_barrier(values)))
+        got_x = [over_x[0]] + [got["x", k] for k in range(1, NX)]
+        got_y = [over_y[0]] + [got["y", j] for j in range(1, NY)]
+        return got_x, got_y
+
     with jax.named_scope("first_stage"):
-        second = sums(by_y[:1] + [send(by_y[j], "y", j) for j in (1, 3, 2)])
-        first = sums(by_x[:1] + [send(by_x[k], "x", k) for k in (1, 3, 2)])
+        first, second = (sums(got) for got in exchange(by_x, by_y))
+
+    with jax.named_scope("second_stage"):
+        second_half, first_half = (total_of(got) for got in exchange(second, first))
+        blocks = jnp.concatenate([first_half, second_half], axis=1)
 
     with jax.named_scope("weights"):
-        held, first, second = lax.optimization_barrier((key_weight, first, second))
-        column = lax.all_gather(held, "yl", axis=0, tiled=True)
-
-    with jax.named_scope("second_stage"):
-        second_half = total_of(second[:1] + [send(second[k], "x", k) for k in range(1, NX)])
-        first_half = total_of(first[:1] + [send(first[j], "y", j) for j in range(1, NY)])
+        core = send(key_weight, "c", 1)
+        held, blocks = lax.optimization_barrier((key_weight, blocks))
+        other = cross(held)
 
     with jax.named_scope("third_stage"):
-        blocks = jnp.concatenate([first_half, second_half], axis=1)
         parts = lax.all_to_all(blocks, "z", 0, 0, tiled=True)
-        own_block = jnp.sum(parts, axis=0)
+        own_block = total_of([parts[n] for n in range(NZ)])
 
     with jax.named_scope("adam"):
         devices = NYL * NC * NZ * NYH * NX
@@ -273,20 +307,22 @@
             master_new.astype(jnp.bfloat16), (NZ * NYH,) + master_new.shape
         )
         plane = lax.all_to_all(fresh, ("z", "yh"), 0, 0, tiled=True)
-        parts = [plane] + [send(plane, "x", k) for k in range(1, NX)]
+        parts = {k: send(plane, "x", k) for k in (1, 3, 2)}
 
     with jax.named_scope("input_grad"):
-        column, _ = lax.optimization_barrier((column, plane))
-        other = send(column, "c", 1)
-        core = jnp.stack([c]).astype(jnp.int32)
-        held = pltpu.with_memory_space_constraint(column, pltpu.HBM)
-        input_grad = input_grad_of(core, key_cotangent, held, width)
-        input_grad = input_grad_of(1 - core, key_cotangent, other, width, input_grad)
+        place = jnp.stack([here + c, here + 1 - c]).astype(jnp.int32)
+        input_grad = input_grad_of(place, key_cotangent, key_weight, core, width)
+        other, _ = lax.optimization_barrier((other, plane))
+        other_core = send(other, "c", 1)
+        place = jnp.stack([there + c, there + 1 - c]).astype(jnp.int32)
+        input_grad = input_grad_of(place, key_cotangent, other, other_core, width, input_grad)
 
     with jax.named_scope("rows"):
-        input_grad, *parts = lax.optimization_barrier((input_grad, *parts))
+        last = {2: parts.pop(2)}
+        parts, input_grad = lax.optimization_barrier(({0: plane} | parts, input_grad))
         place = jnp.stack([x]).astype(jnp.int32)
         weight_new = put_in_rows(place, writer, parts, rows_here)
+        weight_new = put_in_rows(place, writer, last, rows_here, weight_new)
     return (input_grad, master_new, moment_one, moment_two, weight_new)
 
 

time: 232 us -> 133 us (0.57)
  Pallas kernels: 83.9 us -> 23.9 us
  blocking collectives: 36.5 us -> 0 us
  between operations: 14.2 us -> 0.95 us
  starting transfers between devices: 35.1 us -> 47.3 us
  waiting for transfers between devices: 59.9 us -> 56.9 us
    pallas_call x1, Pallas kernels: 65.2 us -> 3.42 us  [columns_of(): pl.pallas_call(columns_kernel, grid_spec=pltpu.PrefetchScalarGridSpec(num...]
    all_to_all x2 -> x0, blocking collectives: 36.5 us -> none  [the longest x1 20.4 us: on_device(): parts = lax.all_to_all(blocks, 'z', 0, 0, tiled=True)]
    all_gather x1 -> x0, waiting for transfers between devices: 21.7 us -> none  [on_device(): column = lax.all_gather(held, 'yl', axis=0, tiled=True)]
    all_to_all x0 -> x2, waiting for transfers between devices: none -> 21 us  [the longest x1 13 us: on_device(): parts = lax.all_to_all(blocks, 'z', 0, 0, tiled=True)]
    all_to_all x0 -> x2, starting transfers between devices: none -> 12.2 us  [the longest x1 8.64 us: on_device(): parts = lax.all_to_all(blocks, 'z', 0, 0, tiled=True)]
    ppermute x20 -> x21, waiting for transfers between devices: 38.1 us -> 35.9 us  [send(): lax.ppermute(value, ('yl', 'yh') if axis == 'y' else axis, shift(axis, st...]
    ppermute x20 -> x21, starting transfers between devices: 35 us -> 35 us  [send(): lax.ppermute(value, ('yl', 'yh') if axis == 'y' else axis, shift(axis, st...]
  transfers between devices with their start and end apart: 21 -> 24, of which waited for: 9 -> 12; matrix products, arithmetic and copies ran while one was open for 1% -> 2% of each run, Pallas kernels for 6% -> 13%
where the time goes in v4:
time: 133 us
  waiting for transfers between devices  56.9 us (43%)
  starting transfers between devices  47.3 us (36%)
  Pallas kernels  23.9 us (18%)
  other arithmetic  2.83 us (2%)
    ppermute x21, waiting for transfers between devices, send(): lax.ppermute(value, ('yl', 'yh') if axis == 'y' else axis, shift(axis, st...  35.9 us
    ppermute x21, starting transfers between devices, send(): lax.ppermute(value, ('yl', 'yh') if axis == 'y' else axis, shift(axis, st...  35 us
    all_to_all x1, waiting for transfers between devices, on_device(): parts = lax.all_to_all(blocks, 'z', 0, 0, tiled=True)  13 us
    pallas_call x2, Pallas kernels, input_grad_of(): pl.pallas_call(input_grad_kernel, grid_spec=pltpu.PrefetchScalarGridSpec(...  10.4 us
    all_to_all x1, starting transfers between devices, on_device(): parts = lax.all_to_all(blocks, 'z', 0, 0, tiled=True)  8.64 us
    all_to_all x1, waiting for transfers between devices, on_device(): plane = lax.all_to_all(fresh, ('z', 'yh'), 0, 0, tiled=True)  8.07 us
    pallas_call x1, Pallas kernels, own_partials(): pl.pallas_call(own_kernel, grid_spec=pltpu.PrefetchScalarGridSpec(num_sca...  4.14 us
    all_to_all x1, starting transfers between devices, on_device(): plane = lax.all_to_all(fresh, ('z', 'yh'), 0, 0, tiled=True)  3.57 us
  transfers between devices with their start and end apart: 24, of which 12 were waited for; matrix products, arithmetic and copies ran while one was open for 2% of the time, Pallas kernels for 13%

profile of v4, /device:TPU:1, one launch (start us, length us, event | category | flops | bytes accessed | tf_op | source)
XLA Modules:
  0.0 132.7 jit_solution(7612327379790411908)
XLA Ops:
  0.6 0.1 pad_add_fusion.2.place
  0.7 3.4 %core_swap.4 = (bf16[256,2048]{1,0:T(8,128)(2,1)}, bf16[256,2048]{1,0:T(8,128)(2,1)}) custom-call(s32[2]{0:T(128)S(1)} %pad_add_fusion.2.place, bf16[256,8192]{1,0:T(8,128)(2,1)} %tokens.1), custom_call_target="tpu_custom_call" | custom-call | tf_op jit(solution)/shard_map/core_swap/pallas_call | solution.py:71
  4.1 3.3 %collective-permute-start.1 = (bf16[256,2048]{1,0:T(8,128)(2,1)}, bf16[256,2048]{1,0:T(8,128)(2,1)S(1)}, u32[]{:S(2)}, u32[]{:S(2)}) collective-permute-start(bf16[256,2048]{1,0:T(8,128)(2,1)} %get-tuple-element.34), channel_id=1, source_target_pairs={{0,64},{64,0},{1,65},{65,1},{2,66},{66,2},{3,67},{67,3},{4,68},{68... | collective-permute-start | bytes 3145736 | tf_op jit(solution)/shard_map/core_swap/ppermute | solution.py:33
  7.5 0.1 collective-permute-start.2
  7.6 0.4 collective-permute-start.3
  8.0 0.0 collective-permute-start
  8.0 0.1 pad_add_fusion.1.place
  8.1 0.1 pad_add_fusion.place
  8.1 4.1 %core_swap.3.own = bf16[2,2048,512]{2,1,0:T(8,128)(2,1)S(1)} custom-call(s32[2]{0:T(128)S(1)} %pad_add_fusion.1.place, bf16[256,8192]{1,0:T(8,128)(2,1)} %tokens.1, bf16[256,512]{1,0:T(8,128)(2,1)S(1)} %copy-done), custom_call_target="tpu_custom_call" | custom-call | tf_op jit(solution)/shard_map/core_swap/pallas_call | solution.py:97
  12.3 0.0 collective-permute-done.far_order
  12.3 0.0 collective-permute-done.3.key
  12.3 0.0 collective-permute-done.1.far
  12.3 0.0 collective-permute-done.2.near
  12.3 2.4 %core_swap.5 = (f32[4,8,16,512]{3,2,1,0:T(8,128)S(1)}, bf16[4,8,16,512]{3,2,1,0:T(8,128)(2,1)S(1)}, bf16[4,8,16,512]{3,2,1,0:T(8,128)(2,1)S(1)}, bf16[4,8,16,512...) custom-call(s32[2]{0:T(128)S(1)} %pad_add_fusion.place, ...), custom_call_target="tpu_custom_call" | custom-call | tf_op jit(solution)/shard_map/core_swap/pallas_call | solution.py:144
  14.7 0.9 collective-permute-start.4
  15.6 0.8 collective-permute-start.5
  16.4 2.3 %collective-permute-start.6 = (bf16[4,8,16,512]{3,2,1,0:T(8,128)(2,1)S(1)}, bf16[4,8,16,512]{3,2,1,0:T(8,128)(2,1)S(1)}, u32[]{:S(2)}, u32[]{:S(2)}) collective-permute-start(bf16[4,8,16,512]{3,2,1,0:T(8,128)(2,1)S(1)} %get-tuple-element.39), channel_id=1, source_target_pairs={{0,4},{128,132},{4,0},{132,128},{1,5},{129,133},{5,1},{133,129},{2... | collective-permute-start | bytes 1572872 | tf_op jit(solution)/shard_map/first_stage/ppermute | solution.py:33
  18.7 1.6 %collective-permute-start.7 = (bf16[4,8,16,512]{3,2,1,0:T(8,128)(2,1)S(1)}, bf16[4,8,16,512]{3,2,1,0:T(8,128)(2,1)S(1)}, u32[]{:S(2)}, u32[]{:S(2)}) collective-permute-start(bf16[4,8,16,512]{3,2,1,0:T(8,128)(2,1)S(1)} %get-tuple-element.40), channel_id=1, source_target_pairs={{0,132},{128,0},{4,128},{132,4},{1,133},{129,1},{5,129},{133,5},{2... | collective-permute-start | bytes 1572872 | tf_op jit(solution)/shard_map/first_stage/ppermute | solution.py:33
  20.3 1.5 %collective-permute-start.8 = (bf16[4,8,16,512]{3,2,1,0:T(8,128)(2,1)S(1)}, bf16[4,8,16,512]{3,2,1,0:T(8,128)(2,1)S(1)}, u32[]{:S(2)}, u32[]{:S(2)}) collective-permute-start(bf16[4,8,16,512]{3,2,1,0:T(8,128)(2,1)S(1)} %get-tuple-element.41), channel_id=1, source_target_pairs={{0,3},{1,0},{2,1},{3,2},{4,7},{5,4},{6,5},{7,6},{8,11},{9,8},{10,9... | collective-permute-start | bytes 1572872 | tf_op jit(solution)/shard_map/first_stage/ppermute | solution.py:33
  21.7 7.8 %collective-permute-done.4 = bf16[4,8,16,512]{3,2,1,0:T(8,128)(2,1)S(1)} collective-permute-done((bf16[4,8,16,512]{3,2,1,0:T(8,128)(2,1)S(1)}, bf16[4,8,16,512]{3,2,1,0:T(8,128)(2,1)S(1)}, u32[]{:S(2)}, u32[]{:S(2)}) %collective-permute-start.4) | collective-permute-done | bytes 524320 | tf_op jit(solution)/shard_map/first_stage/ppermute | solution.py:33
  29.5 0.8 collective-permute-start.9
  30.3 0.0 collective-permute-done.5
  30.3 11.0 %collective-permute-done.6 = bf16[4,8,16,512]{3,2,1,0:T(8,128)(2,1)S(1)} collective-permute-done((bf16[4,8,16,512]{3,2,1,0:T(8,128)(2,1)S(1)}, bf16[4,8,16,512]{3,2,1,0:T(8,128)(2,1)S(1)}, u32[]{:S(2)}, u32[]{:S(2)}) %collective-permute-start.6) | collective-permute-done | bytes 524320 | tf_op jit(solution)/shard_map/first_stage/ppermute | solution.py:33
  41.3 0.2 collective-permute-done.7
  41.4 2.1 %collective-permute-done.9 = bf16[4,8,16,512]{3,2,1,0:T(8,128)(2,1)S(1)} collective-permute-done((bf16[4,8,16,512]{3,2,1,0:T(8,128)(2,1)S(1)}, bf16[4,8,16,512]{3,2,1,0:T(8,128)(2,1)S(1)}, u32[]{:S(2)}, u32[]{:S(2)}) %collective-permute-start.9) | collective-permute-done | bytes 524320 | tf_op jit(solution)/shard_map/first_stage/ppermute | solution.py:33
  43.6 0.3 fusion.7
  43.9 0.9 collective-permute-start.11
  44.8 1.7 %collective-permute-start.12 = (bf16[8,16,512]{2,1,0:T(8,128)(2,1)S(1)}, bf16[8,16,512]{2,1,0:T(8,128)(2,1)S(1)}, u32[]{:S(2)}, u32[]{:S(2)}) collective-permute-start(bf16[8,16,512]{2,1,0:T(8,128)(2,1)S(1)} %get-tuple-element.71), channel_id=1, source_target_pairs={{0,4},{128,132},{4,0},{132,128},{1,5},{129,133},{5,1},{133,129},{2... | collective-permute-start | bytes 393224 | tf_op jit(solution)/shard_map/second_stage/ppermute | solution.py:33
  46.4 1.1 collective-permute-start.13
  47.6 0.3 fusion.9
  47.9 1.8 %collective-permute-start.10 = (bf16[8,16,512]{2,1,0:T(8,128)(2,1)S(1)}, bf16[8,16,512]{2,1,0:T(8,128)(2,1)S(1)}, u32[]{:S(2)}, u32[]{:S(2)}) collective-permute-start(bf16[8,16,512]{2,1,0:T(8,128)(2,1)S(1)} %get-tuple-element.69), channel_id=1, source_target_pairs={{0,1},{1,2},{2,3},{3,0},{4,5},{5,6},{6,7},{7,4},{8,9},{9,10},{10,1... | collective-permute-start | bytes 393224 | tf_op jit(solution)/shard_map/second_stage/ppermute | solution.py:33
  49.7 0.9 collective-permute-start.14
  50.6 0.0 collective-permute-done.11
  50.6 0.0 copy-start.5
  50.6 1.2 collective-permute-start.15
  51.8 0.0 collective-permute-done.12
  51.8 0.0 collective-permute-done.13
  51.9 1.4 %collective-permute-done.10 = bf16[8,16,512]{2,1,0:T(8,128)(2,1)S(1)} collective-permute-done((bf16[8,16,512]{2,1,0:T(8,128)(2,1)S(1)}, bf16[8,16,512]{2,1,0:T(8,128)(2,1)S(1)}, u32[]{:S(2)}, u32[]{:S(2)}) %collective-permute-start.10) | collective-permute-done | bytes 131104 | tf_op jit(solution)/shard_map/second_stage/ppermute | solution.py:33
  53.3 0.5 collective-permute-done.14
  53.8 2.8 %collective-permute-done.15 = bf16[8,16,512]{2,1,0:T(8,128)(2,1)S(1)} collective-permute-done((bf16[8,16,512]{2,1,0:T(8,128)(2,1)S(1)}, bf16[8,16,512]{2,1,0:T(8,128)(2,1)S(1)}, u32[]{:S(2)}, u32[]{:S(2)}) %collective-permute-start.15) | collective-permute-done | bytes 131104 | tf_op jit(solution)/shard_map/second_stage/ppermute | solution.py:33
  56.5 0.3 fusion.1
  56.8 0.8 pad_maximum_fusion
  57.7 8.6 %all-to-all-start = ((f32[8,32,512]{2,1,0:T(8,128)}), f32[8,32,512]{2,1,0:T(8,128)S(1)}, u32[]{:S(2)}, u32[]{:S(2)}) async-start(f32[8,32,512]{2,1,0:T(8,128)} %pad_maximum_fusion), calls=%async_computation | async-start | bytes 1048576 | tf_op jit(solution)/shard_map/third_stage/all_to_all | solution.py:291
  66.3 0.1 collective-permute-start.18
  66.4 13.0 %all-to-all-done = f32[8,32,512]{2,1,0:T(8,128)S(1)} async-done(((f32[8,32,512]{2,1,0:T(8,128)}), f32[8,32,512]{2,1,0:T(8,128)S(1)}, u32[]{:S(2)}, u32[]{:S(2)}) %all-to-all-start) | async-done | bytes 524320 | tf_op jit(solution)/shard_map/third_stage/all_to_all | solution.py:291
  79.4 0.7 fusion.10
  80.1 0.8 broadcast_in_dim.3
  81.0 3.6 %all-to-all-start.1 = ((bf16[16,32,512]{2,1,0:T(8,128)(2,1)}), bf16[16,32,512]{2,1,0:T(8,128)(2,1)S(1)}, u32[]{:S(2)}, u32[]{:S(2)}) async-start(bf16[16,32,512]{2,1,0:T(8,128)(2,1)} %broadcast_in_dim.3), calls=%async_computation.1 | async-start | bytes 1048576 | tf_op jit(solution)/shard_map/fresh_weights/all_to_all | solution.py:309
  84.6 5.5 %collective-permute-start.20 = (bf16[2048,512]{1,0:T(8,128)(2,1)S(1)}, bf16[2048,512]{1,0:T(8,128)(2,1)}, u32[]{:S(2)}, u32[]{:S(2)}) collective-permute-start(bf16[2048,512]{1,0:T(8,128)(2,1)S(1)} %copy-done.1), channel_id=1, source_target_pairs={{0,64},{64,0},{1,65},{65,1},{2,66},{66,2},{3,67},{67,3},{4,68},{68... | collective-permute-start | bytes 6291464 | tf_op jit(solution)/shard_map/weights/ppermute | solution.py:33
  90.0 8.1 %all-to-all-done.1.rest_0_ = bf16[16,32,512]{2,1,0:T(8,128)(2,1)S(1)} async-done(((bf16[16,32,512]{2,1,0:T(8,128)(2,1)}), bf16[16,32,512]{2,1,0:T(8,128)(2,1)S(1)}, u32[]{:S(2)}, u32[]{:S(2)}) %all-to-all-start.1) | async-done | bytes 524320 | tf_op jit(solution)/shard_map/fresh_weights/all_to_all | solution.py:309
  98.1 0.0 collective-permute-done.18.first
  98.1 6.5 %collective-permute-start.19 = (bf16[2048,512]{1,0:T(8,128)(2,1)}, bf16[2048,512]{1,0:T(8,128)(2,1)S(1)}, u32[]{:S(2)}, u32[]{:S(2)}) collective-permute-start(bf16[2048,512]{1,0:T(8,128)(2,1)} %collective-permute-done.18.first), channel_id=1, source_target_pairs={{0,64},{64,0},{1,65},{65,1},{2,66},{66,2},{3,67},{67,3},{4,68},{68... | collective-permute-start | bytes 6291464 | tf_op jit(solution)/shard_map/input_grad/ppermute | solution.py:33
  104.6 2.0 %collective-permute-start.16 = (bf16[16,32,512]{2,1,0:T(8,128)(2,1)S(1)}, bf16[16,32,512]{2,1,0:T(8,128)(2,1)S(1)}, u32[]{:S(2)}, u32[]{:S(2)}) collective-permute-start(bf16[16,32,512]{2,1,0:T(8,128)(2,1)S(1)} %all-to-all-done.1.rest_0_), channel_id=1, source_target_pairs={{0,1},{1,2},{2,3},{3,0},{4,5},{5,6},{6,7},{7,4},{8,9},{9,10},{10,1... | collective-permute-start | bytes 1572872 | tf_op jit(solution)/shard_map/fresh_weights/ppermute | solution.py:33
  106.5 0.7 collective-permute-start.17
  107.2 1.1 collective-permute-start.21
  108.3 0.1 pad_add_fusion.4.place
  108.4 0.1 pad_add_fusion.3.place
  108.5 5.5 %input_grad.2.rest_0_ = bf16[256,8192]{1,0:T(8,128)(2,1)} custom-call(s32[2]{0:T(128)S(1)} %pad_add_fusion.4.place, bf16[256,512]{1,0:T(8,128)(2,1)S(1)} %copy-done, bf16[2048,512]{1,0:T(8,128)(2,1)S(1)} %copy-done.1, bf16[2048,512]{1,0:T(8,128)(2,1)} %collective-permute-done.20.second), custom_call_target="tpu_custom_call" | custom-call | tf_op jit(solution)/shard_map/input_grad/pallas_call | solution.py:172
  114.0 4.8 %input_grad.3 = bf16[256,8192]{1,0:T(8,128)(2,1)} custom-call(s32[2]{0:T(128)S(1)} %pad_add_fusion.3.place, bf16[256,512]{1,0:T(8,128)(2,1)S(1)} %copy-done, bf16[2048,512]{1,0:T(8,128)(2,1)} %collective-permute-done.18.first, bf16[2048,512]{1,0:T(8,128)(2,1)S(1)} %collective-permute-done.19.second, ...), custom_call_target="tpu_custom_call", output_to_operand_aliasing={{}: (4, {})} | custom-call | tf_op jit(solution)/shard_map/input_grad/pallas_call | solution.py:172
  118.9 0.5 collective-permute-done.16.rest_1_
  119.3 0.4 collective-permute-done.17.rest_2_
  119.8 2.1 %rows.2.rest_1_ = bf16[2048,512]{1,0:T(8,128)(2,1)} custom-call(s32[1]{0:T(128)} %bitcast.place, s32[1,64]{1,0:T(1,128)S(1)} %copy-done.2, bf16[16,32,512]{2,1,0:T(8,128)(2,1)S(1)} %all-to-all-done.1.rest_0_, bf16[16,32,512]{2,1,0:T(8,128)(2,1)S(1)} %collective-permute-done.16.rest_1_, bf16[16,32,512]{2,1,0:T(8,128)(2,1)S(1)} %collective-permute-done.17.rest_2_), custom_call_target="tpu_custom_call" | custom-call | tf_op jit(solution)/shard_map/rows/pallas_call | solution.py:217
  121.9 9.2 %collective-permute-done.21.rest_0_ = bf16[16,32,512]{2,1,0:T(8,128)(2,1)S(1)} collective-permute-done((bf16[16,32,512]{2,1,0:T(8,128)(2,1)S(1)}, bf16[16,32,512]{2,1,0:T(8,128)(2,1)S(1)}, u32[]{:S(2)}, u32[]{:S(2)}) %collective-permute-start.21) | collective-permute-done | bytes 524320 | tf_op jit(solution)/shard_map/fresh_weights/ppermute | solution.py:33
  131.1 1.5 %rows.3 = bf16[2048,512]{1,0:T(8,128)(2,1)} custom-call(s32[1]{0:T(128)} %bitcast.place, s32[1,64]{1,0:T(1,128)S(1)} %copy-done.2, bf16[16,32,512]{2,1,0:T(8,128)(2,1)S(1)} %collective-permute-done.21.rest_0_, bf16[2048,512]{1,0:T(8,128)(2,1)} %rows.2.rest_1_), custom_call_target="tpu_custom_call", output_to_operand_aliasing={{}: (3, {})} | custom-call | tf_op jit(solution)/shard_map/rows/pallas_call | solution.py:217
  (14 shorter events, 0.0 us)
Async XLA Ops:
  0.7 6.9 %copy-start = (bf16[256,512]{1,0:T(8,128)(2,1)S(1)}, bf16[256,512]{1,0:T(8,128)(2,1)}, u32[]{:S(2)}) copy-start(bf16[256,512]{1,0:T(8,128)(2,1)} %key.5) | copy-start | bytes 786436
  0.7 7.3 %copy-start.2 = (s32[1,64]{1,0:T(1,128)S(1)}, s32[1,64]{1,0:T(1,128)}, u32[]{:S(2)}) copy-start(s32[1,64]{1,0:T(1,128)} %order.3) | copy-start | bytes 772
  4.1 8.2 %collective-permute-start.1 = (bf16[256,2048]{1,0:T(8,128)(2,1)}, bf16[256,2048]{1,0:T(8,128)(2,1)S(1)}, u32[]{:S(2)}, u32[]{:S(2)}) collective-permute-start(bf16[256,2048]{1,0:T(8,128)(2,1)} %get-tuple-element.34), channel_id=1, source_target_pairs={{0,64},{64,0},{1,65},{65,1},{2,66},{66,2},{3,67},{67,3},{4,68},{68... | collective-permute-start | bytes 3145736 | tf_op jit(solution)/shard_map/core_swap/ppermute | solution.py:33
  7.5 4.9 %collective-permute-start.2 = (bf16[256,2048]{1,0:T(8,128)(2,1)}, bf16[256,2048]{1,0:T(8,128)(2,1)S(1)}, u32[]{:S(2)}, u32[]{:S(2)}) collective-permute-start(bf16[256,2048]{1,0:T(8,128)(2,1)} %get-tuple-element.35), channel_id=1, source_target_pairs={{0,64},{64,0},{1,65},{65,1},{2,66},{66,2},{3,67},{67,3},{4,68},{68... | collective-permute-start | bytes 3145736 | tf_op jit(solution)/shard_map/core_swap/ppermute | solution.py:33
  7.6 4.7 %collective-permute-start.3 = (bf16[256,512]{1,0:T(8,128)(2,1)S(1)}, bf16[256,512]{1,0:T(8,128)(2,1)S(1)}, u32[]{:S(2)}, u32[]{:S(2)}) collective-permute-start(bf16[256,512]{1,0:T(8,128)(2,1)S(1)} %copy-done), channel_id=1, source_target_pairs={{0,64},{64,0},{1,65},{65,1},{2,66},{66,2},{3,67},{67,3},{4,68},{68... | collective-permute-start | bytes 786440 | tf_op jit(solution)/shard_map/core_swap/ppermute | solution.py:33
  8.0 4.3 %collective-permute-start = (s32[1,64]{1,0:T(1,128)S(1)}, s32[1,64]{1,0:T(1,128)S(1)}, u32[]{:S(2)}, u32[]{:S(2)}) collective-permute-start(s32[1,64]{1,0:T(1,128)S(1)} %copy-done.2), channel_id=1, source_target_pairs={{0,128},{128,0},{1,129},{129,1},{2,130},{130,2},{3,131},{131,3},{4... | collective-permute-start | bytes 776 | tf_op jit(solution)/shard_map/core_swap/ppermute | solution.py:33
  14.7 14.8 %collective-permute-start.4 = (bf16[4,8,16,512]{3,2,1,0:T(8,128)(2,1)S(1)}, bf16[4,8,16,512]{3,2,1,0:T(8,128)(2,1)S(1)}, u32[]{:S(2)}, u32[]{:S(2)}) collective-permute-start(bf16[4,8,16,512]{3,2,1,0:T(8,128)(2,1)S(1)} %get-tuple-element.37), channel_id=1, source_target_pairs={{0,1},{1,2},{2,3},{3,0},{4,5},{5,6},{6,7},{7,4},{8,9},{9,10},{10,1... | collective-permute-start | bytes 1572872 | tf_op jit(solution)/shard_map/first_stage/ppermute | solution.py:33
  15.6 14.7 %collective-permute-start.5 = (bf16[4,8,16,512]{3,2,1,0:T(8,128)(2,1)S(1)}, bf16[4,8,16,512]{3,2,1,0:T(8,128)(2,1)S(1)}, u32[]{:S(2)}, u32[]{:S(2)}) collective-permute-start(bf16[4,8,16,512]{3,2,1,0:T(8,128)(2,1)S(1)} %get-tuple-element.38), channel_id=1, source_target_pairs={{0,128},{128,4},{4,132},{132,0},{1,129},{129,5},{5,133},{133,1},{2... | collective-permute-start | bytes 1572872 | tf_op jit(solution)/shard_map/first_stage/ppermute | solution.py:33
  16.4 24.9 %collective-permute-start.6 = (bf16[4,8,16,512]{3,2,1,0:T(8,128)(2,1)S(1)}, bf16[4,8,16,512]{3,2,1,0:T(8,128)(2,1)S(1)}, u32[]{:S(2)}, u32[]{:S(2)}) collective-permute-start(bf16[4,8,16,512]{3,2,1,0:T(8,128)(2,1)S(1)} %get-tuple-element.39), channel_id=1, source_target_pairs={{0,4},{128,132},{4,0},{132,128},{1,5},{129,133},{5,1},{133,129},{2... | collective-permute-start | bytes 1572872 | tf_op jit(solution)/shard_map/first_stage/ppermute | solution.py:33
  18.7 22.8 %collective-permute-start.7 = (bf16[4,8,16,512]{3,2,1,0:T(8,128)(2,1)S(1)}, bf16[4,8,16,512]{3,2,1,0:T(8,128)(2,1)S(1)}, u32[]{:S(2)}, u32[]{:S(2)}) collective-permute-start(bf16[4,8,16,512]{3,2,1,0:T(8,128)(2,1)S(1)} %get-tuple-element.40), channel_id=1, source_target_pairs={{0,132},{128,0},{4,128},{132,4},{1,133},{129,1},{5,129},{133,5},{2... | collective-permute-start | bytes 1572872 | tf_op jit(solution)/shard_map/first_stage/ppermute | solution.py:33
  20.3 21.2 %collective-permute-start.8 = (bf16[4,8,16,512]{3,2,1,0:T(8,128)(2,1)S(1)}, bf16[4,8,16,512]{3,2,1,0:T(8,128)(2,1)S(1)}, u32[]{:S(2)}, u32[]{:S(2)}) collective-permute-start(bf16[4,8,16,512]{3,2,1,0:T(8,128)(2,1)S(1)} %get-tuple-element.41), channel_id=1, source_target_pairs={{0,3},{1,0},{2,1},{3,2},{4,7},{5,4},{6,5},{7,6},{8,11},{9,8},{10,9... | collective-permute-start | bytes 1572872 | tf_op jit(solution)/shard_map/first_stage/ppermute | solution.py:33
  29.5 14.1 %collective-permute-start.9 = (bf16[4,8,16,512]{3,2,1,0:T(8,128)(2,1)S(1)}, bf16[4,8,16,512]{3,2,1,0:T(8,128)(2,1)S(1)}, u32[]{:S(2)}, u32[]{:S(2)}) collective-permute-start(bf16[4,8,16,512]{3,2,1,0:T(8,128)(2,1)S(1)} %get-tuple-element.42), channel_id=1, source_target_pairs={{0,2},{1,3},{2,0},{3,1},{4,6},{5,7},{6,4},{7,5},{8,10},{9,11},{10,... | collective-permute-start | bytes 1572872 | tf_op jit(solution)/shard_map/first_stage/ppermute | solution.py:33
  43.9 6.8 %collective-permute-start.11 = (bf16[8,16,512]{2,1,0:T(8,128)(2,1)S(1)}, bf16[8,16,512]{2,1,0:T(8,128)(2,1)S(1)}, u32[]{:S(2)}, u32[]{:S(2)}) collective-permute-start(bf16[8,16,512]{2,1,0:T(8,128)(2,1)S(1)} %get-tuple-element.72), channel_id=1, source_target_pairs={{0,128},{128,4},{4,132},{132,0},{1,129},{129,5},{5,133},{133,1},{2... | collective-permute-start | bytes 393224 | tf_op jit(solution)/shard_map/second_stage/ppermute | solution.py:33
  44.8 7.1 %collective-permute-start.12 = (bf16[8,16,512]{2,1,0:T(8,128)(2,1)S(1)}, bf16[8,16,512]{2,1,0:T(8,128)(2,1)S(1)}, u32[]{:S(2)}, u32[]{:S(2)}) collective-permute-start(bf16[8,16,512]{2,1,0:T(8,128)(2,1)S(1)} %get-tuple-element.71), channel_id=1, source_target_pairs={{0,4},{128,132},{4,0},{132,128},{1,5},{129,133},{5,1},{133,129},{2... | collective-permute-start | bytes 393224 | tf_op jit(solution)/shard_map/second_stage/ppermute | solution.py:33
  46.4 5.4 %collective-permute-start.13 = (bf16[8,16,512]{2,1,0:T(8,128)(2,1)S(1)}, bf16[8,16,512]{2,1,0:T(8,128)(2,1)S(1)}, u32[]{:S(2)}, u32[]{:S(2)}) collective-permute-start(bf16[8,16,512]{2,1,0:T(8,128)(2,1)S(1)} %get-tuple-element.70), channel_id=1, source_target_pairs={{0,132},{128,0},{4,128},{132,4},{1,133},{129,1},{5,129},{133,5},{2... | collective-permute-start | bytes 393224 | tf_op jit(solution)/shard_map/second_stage/ppermute | solution.py:33
  47.9 5.4 %collective-permute-start.10 = (bf16[8,16,512]{2,1,0:T(8,128)(2,1)S(1)}, bf16[8,16,512]{2,1,0:T(8,128)(2,1)S(1)}, u32[]{:S(2)}, u32[]{:S(2)}) collective-permute-start(bf16[8,16,512]{2,1,0:T(8,128)(2,1)S(1)} %get-tuple-element.69), channel_id=1, source_target_pairs={{0,1},{1,2},{2,3},{3,0},{4,5},{5,6},{6,7},{7,4},{8,9},{9,10},{10,1... | collective-permute-start | bytes 393224 | tf_op jit(solution)/shard_map/second_stage/ppermute | solution.py:33
  49.7 4.1 %collective-permute-start.14 = (bf16[8,16,512]{2,1,0:T(8,128)(2,1)S(1)}, bf16[8,16,512]{2,1,0:T(8,128)(2,1)S(1)}, u32[]{:S(2)}, u32[]{:S(2)}) collective-permute-start(bf16[8,16,512]{2,1,0:T(8,128)(2,1)S(1)} %get-tuple-element.68), channel_id=1, source_target_pairs={{0,3},{1,0},{2,1},{3,2},{4,7},{5,4},{6,5},{7,6},{8,11},{9,8},{10,9... | collective-permute-start | bytes 393224 | tf_op jit(solution)/shard_map/second_stage/ppermute | solution.py:33
  50.6 15.7 %copy-start.1 = (bf16[2048,512]{1,0:T(8,128)(2,1)S(1)}, bf16[2048,512]{1,0:T(8,128)(2,1)}, u32[]{:S(2)}) copy-start(bf16[2048,512]{1,0:T(8,128)(2,1)} %first.1) | copy-start | bytes 6291460
  50.6 28.8 %copy-start.3 = (f32[32,512]{1,0:T(8,128)S(1)}, f32[32,512]{1,0:T(8,128)}, u32[]{:S(2)}) copy-start(f32[32,512]{1,0:T(8,128)} %param.10) | copy-start | bytes 196612
  50.6 28.8 %copy-start.4 = (f32[32,512]{1,0:T(8,128)S(1)}, f32[32,512]{1,0:T(8,128)}, u32[]{:S(2)}) copy-start(f32[32,512]{1,0:T(8,128)} %param.11) | copy-start | bytes 196612
  50.6 28.8 %copy-start.5 = (f32[32,512]{1,0:T(8,128)S(1)}, f32[32,512]{1,0:T(8,128)}, u32[]{:S(2)}) copy-start(f32[32,512]{1,0:T(8,128)} %param.12) | copy-start | bytes 196612
  50.6 5.9 %collective-permute-start.15 = (bf16[8,16,512]{2,1,0:T(8,128)(2,1)S(1)}, bf16[8,16,512]{2,1,0:T(8,128)(2,1)S(1)}, u32[]{:S(2)}, u32[]{:S(2)}) collective-permute-start(bf16[8,16,512]{2,1,0:T(8,128)(2,1)S(1)} %get-tuple-element.67), channel_id=1, source_target_pairs={{0,2},{1,3},{2,0},{3,1},{4,6},{5,7},{6,4},{7,5},{8,10},{9,11},{10,... | collective-permute-start | bytes 393224 | tf_op jit(solution)/shard_map/second_stage/ppermute | solution.py:33
  57.7 21.7 %all-to-all-start = ((f32[8,32,512]{2,1,0:T(8,128)}), f32[8,32,512]{2,1,0:T(8,128)S(1)}, u32[]{:S(2)}, u32[]{:S(2)}) async-start(f32[8,32,512]{2,1,0:T(8,128)} %pad_maximum_fusion), calls=%async_computation | async-start | bytes 1048576 | tf_op jit(solution)/shard_map/third_stage/all_to_all | solution.py:291
  66.3 31.8 %collective-permute-start.18 = (bf16[2048,512]{1,0:T(8,128)(2,1)S(1)}, bf16[2048,512]{1,0:T(8,128)(2,1)}, u32[]{:S(2)}, u32[]{:S(2)}) collective-permute-start(bf16[2048,512]{1,0:T(8,128)(2,1)S(1)} %copy-done.1), channel_id=1, source_target_pairs={{0,128},{64,196},{128,4},{192,64},{4,132},{68,192},{132,0},{196,68... | collective-permute-start | bytes 6291464 | tf_op jit(solution)/shard_map/weights/ppermute | solution.py:42
  81.0 17.1 %all-to-all-start.1 = ((bf16[16,32,512]{2,1,0:T(8,128)(2,1)}), bf16[16,32,512]{2,1,0:T(8,128)(2,1)S(1)}, u32[]{:S(2)}, u32[]{:S(2)}) async-start(bf16[16,32,512]{2,1,0:T(8,128)(2,1)} %broadcast_in_dim.3), calls=%async_computation.1 | async-start | bytes 1048576 | tf_op jit(solution)/shard_map/fresh_weights/all_to_all | solution.py:309
  84.6 23.9 %collective-permute-start.20 = (bf16[2048,512]{1,0:T(8,128)(2,1)S(1)}, bf16[2048,512]{1,0:T(8,128)(2,1)}, u32[]{:S(2)}, u32[]{:S(2)}) collective-permute-start(bf16[2048,512]{1,0:T(8,128)(2,1)S(1)} %copy-done.1), channel_id=1, source_target_pairs={{0,64},{64,0},{1,65},{65,1},{2,66},{66,2},{3,67},{67,3},{4,68},{68... | collective-permute-start | bytes 6291464 | tf_op jit(solution)/shard_map/weights/ppermute | solution.py:33
  98.1 15.9 %collective-permute-start.19 = (bf16[2048,512]{1,0:T(8,128)(2,1)}, bf16[2048,512]{1,0:T(8,128)(2,1)S(1)}, u32[]{:S(2)}, u32[]{:S(2)}) collective-permute-start(bf16[2048,512]{1,0:T(8,128)(2,1)} %collective-permute-done.18.first), channel_id=1, source_target_pairs={{0,64},{64,0},{1,65},{65,1},{2,66},{66,2},{3,67},{67,3},{4,68},{68... | collective-permute-start | bytes 6291464 | tf_op jit(solution)/shard_map/input_grad/ppermute | solution.py:33
  104.6 14.8 %collective-permute-start.16 = (bf16[16,32,512]{2,1,0:T(8,128)(2,1)S(1)}, bf16[16,32,512]{2,1,0:T(8,128)(2,1)S(1)}, u32[]{:S(2)}, u32[]{:S(2)}) collective-permute-start(bf16[16,32,512]{2,1,0:T(8,128)(2,1)S(1)} %all-to-all-done.1.rest_0_), channel_id=1, source_target_pairs={{0,1},{1,2},{2,3},{3,0},{4,5},{5,6},{6,7},{7,4},{8,9},{9,10},{10,1... | collective-permute-start | bytes 1572872 | tf_op jit(solution)/shard_map/fresh_weights/ppermute | solution.py:33
  106.5 13.2 %collective-permute-start.17 = (bf16[16,32,512]{2,1,0:T(8,128)(2,1)S(1)}, bf16[16,32,512]{2,1,0:T(8,128)(2,1)S(1)}, u32[]{:S(2)}, u32[]{:S(2)}) collective-permute-start(bf16[16,32,512]{2,1,0:T(8,128)(2,1)S(1)} %all-to-all-done.1.rest_0_), channel_id=1, source_target_pairs={{0,3},{1,0},{2,1},{3,2},{4,7},{5,4},{6,5},{7,6},{8,11},{9,8},{10,9... | collective-permute-start | bytes 1572872 | tf_op jit(solution)/shard_map/fresh_weights/ppermute | solution.py:33
  107.2 23.8 %collective-permute-start.21 = (bf16[16,32,512]{2,1,0:T(8,128)(2,1)S(1)}, bf16[16,32,512]{2,1,0:T(8,128)(2,1)S(1)}, u32[]{:S(2)}, u32[]{:S(2)}) collective-permute-start(bf16[16,32,512]{2,1,0:T(8,128)(2,1)S(1)} %all-to-all-done.1.rest_0_), channel_id=1, source_target_pairs={{0,2},{1,3},{2,0},{3,1},{4,6},{5,7},{6,4},{7,5},{8,10},{9,11},{10,... | collective-permute-start | bytes 1572872 | tf_op jit(solution)/shard_map/fresh_weights/ppermute | solution.py:33

commit v5 on v4

--- a/solution.py
+++ b/solution.py
@@ -194,26 +194,32 @@
 def rows_kernel(steps, place, order, *rest):
     parts, out, sems = rest[: len(steps)], rest[-2], rest[-1]
     x = place[0]
-    block_rows = parts[0].shape[1]
+    block_rows = parts[0].shape[-2]
     copies = []
-    for i, k in enumerate(steps):
-        from_x = lax.rem(x + NX - k, NX)
+    for part, k in zip(parts, steps):
         for n in range(NZ * NYH):
-            start = pl.multiple_of(order[0, n * NX + from_x] * block_rows, block_rows)
-            copies.append(
-                pltpu.make_async_copy(
-                    parts[i].at[n], out.at[pl.ds(start, block_rows), :], sems.at[i, n]
+            for back in range(NX) if k is None else (k,):
+                from_x = lax.rem(x + NX - back, NX)
+                start = pl.multiple_of(order[0, n * NX + from_x] * block_rows, block_rows)
+                width = part.shape[-1]
+                first = out.shape[1] - width if k is None else 0
+                copies.append(
+                    pltpu.make_async_copy(
+                        part.at[n, back] if k is None else part.at[n],
+                        out.at[pl.ds(start, block_rows), first : first + width],
+                        sems.at[len(copies)],
+                    )
                 )
-            )
     for copy in copies:
         copy.start()
     for copy in copies:
         copy.wait()
 
 
-def put_in_rows(place, order, parts, rows, before=None):
+def put_in_rows(place, order, parts, shape, before=None):
     steps, values = tuple(parts), list(parts.values())
     extra = [] if before is None else [before]
+    count = sum(NZ * NYH * (NX if k is None else 1) for k in steps)
     return pl.pallas_call(
         functools.partial(rows_kernel, steps),
         grid_spec=pltpu.PrefetchScalarGridSpec(
@@ -221,9 +227,9 @@
             grid=(1,),
             in_specs=[vmem()] * len(values) + [pl.BlockSpec(memory_space=pl.ANY)] * len(extra),
             out_specs=pl.BlockSpec(memory_space=pl.ANY),
-            scratch_shapes=[pltpu.SemaphoreType.DMA((len(steps), NZ * NYH))],
-        ),
-        out_shape=jax.ShapeDtypeStruct((rows, values[0].shape[2]), values[0].dtype),
+            scratch_shapes=[pltpu.SemaphoreType.DMA((count,))],
+        ),
+        out_shape=jax.ShapeDtypeStruct(shape, values[0].dtype),
         input_output_aliases={2 + len(values): 0} if extra else {},
         compiler_params=params(6),
     )(place, order, *values, *extra)
@@ -244,7 +250,8 @@
     tokens_in, key_cotangent, key_weight, master_store, first_moment, second_moment, writer
 ):
     yl, c, _, yh, x = (lax.axis_index(name) for name in AXES)
-    tok_rows, width = tokens_in.shape
+    tok_rows, depth = tokens_in.shape
+    width = key_weight.shape[1]
     rows_here = key_weight.shape[0]
     block_rows = master_store.shape[0]
 
@@ -280,7 +287,7 @@
 
     with jax.named_scope("second_stage"):
         second_half, first_half = (total_of(got) for got in exchange(second, first))
-        blocks = jnp.concatenate([first_half, second_half], axis=1)
+        blocks = jnp.concatenate([first_half, second_half], axis=1).astype(jnp.bfloat16)
 
     with jax.named_scope("weights"):
         core = send(key_weight, "c", 1)
@@ -303,26 +310,35 @@
         )
 
     with jax.named_scope("fresh_weights"):
-        fresh = jnp.broadcast_to(
-            master_new.astype(jnp.bfloat16), (NZ * NYH,) + master_new.shape
-        )
-        plane = lax.all_to_all(fresh, ("z", "yh"), 0, 0, tiled=True)
+        fresh = master_new.astype(jnp.bfloat16)
+        most = width - width // 4
+
+        def to_plane(value):
+            value = jnp.broadcast_to(value, (NZ * NYH,) + value.shape)
+            return lax.all_to_all(value, ("z", "yh"), 0, 0, tiled=True)
+
+        plane = to_plane(fresh[:, :most])
+        line = fresh[:, most:]
+        line = jnp.stack([line] + [send(line, "x", k) for k in range(1, NX)])
+        plane, line = lax.optimization_barrier((plane, line))
         parts = {k: send(plane, "x", k) for k in (1, 3, 2)}
+        last_columns = to_plane(line)
 
     with jax.named_scope("input_grad"):
         place = jnp.stack([here + c, here + 1 - c]).astype(jnp.int32)
-        input_grad = input_grad_of(place, key_cotangent, key_weight, core, width)
+        input_grad = input_grad_of(place, key_cotangent, key_weight, core, depth)
         other, _ = lax.optimization_barrier((other, plane))
         other_core = send(other, "c", 1)
         place = jnp.stack([there + c, there + 1 - c]).astype(jnp.int32)
-        input_grad = input_grad_of(place, key_cotangent, other, other_core, width, input_grad)
+        input_grad = input_grad_of(place, key_cotangent, other, other_core, depth, input_grad)
 
     with jax.named_scope("rows"):
-        last = {2: parts.pop(2)}
-        parts, input_grad = lax.optimization_barrier(({0: plane} | parts, input_grad))
+        near_x, near_back, input_grad = lax.optimization_barrier((parts[1], parts[3], input_grad))
         place = jnp.stack([x]).astype(jnp.int32)
-        weight_new = put_in_rows(place, writer, parts, rows_here)
-        weight_new = put_in_rows(place, writer, last, rows_here, weight_new)
+        shape = key_weight.shape
+        weight_new = None
+        for group in ({0: plane, 1: near_x, 3: near_back}, {None: last_columns}, {2: parts[2]}):
+            weight_new = put_in_rows(place, writer, group, shape, weight_new)
     return (input_grad, master_new, moment_one, moment_two, weight_new)
 
 

time: 133 us -> 131 us (0.985)
  the two profiles are of different devices: /device:TPU:1 before, /device:TPU:30 now
where the time goes in v5:
time: 131 us
  waiting for transfers between devices  41.4 us (32%)
  starting transfers between devices  38.1 us (29%)
  Pallas kernels  27.8 us (21%)
  blocking collectives  18.7 us (14%)
  other arithmetic  1.98 us (2%)
  local copies, waits for them, and re-layouts  1.72 us (1%)
    ppermute x24, waiting for transfers between devices, send(): lax.ppermute(value, ('yl', 'yh') if axis == 'y' else axis, shift(axis, st...  37.9 us
    ppermute x24, starting transfers between devices, send(): lax.ppermute(value, ('yl', 'yh') if axis == 'y' else axis, shift(axis, st...  23.1 us
    all_to_all x1, blocking collectives, on_device(): parts = lax.all_to_all(blocks, 'z', 0, 0, tiled=True)  18.7 us
    pallas_call x2, Pallas kernels, input_grad_of(): pl.pallas_call(input_grad_kernel, grid_spec=pltpu.PrefetchScalarGridSpec(...  11.4 us
    all_to_all x2, starting transfers between devices, to_plane(): return lax.all_to_all(value, ('z', 'yh'), 0, 0, tiled=True)  11.3 us
    pallas_call x3, Pallas kernels, put_in_rows(): pl.pallas_call(functools.partial(rows_kernel, steps), grid_spec=pltpu.Pre...  6.32 us
    pallas_call x1, Pallas kernels, own_partials(): pl.pallas_call(own_kernel, grid_spec=pltpu.PrefetchScalarGridSpec(num_sca...  4.18 us
    ppermute x1, starting transfers between devices, cross(): return lax.ppermute(value, ('yl', 'c', 'yh'), pairs)  3.74 us
  transfers between devices with their start and end apart: 27, of which 14 were waited for; matrix products, arithmetic and copies ran while one was open for 2% of the time, Pallas kernels for 15%

profile of v5, /device:TPU:30, one launch (start us, length us, event | category | flops | bytes accessed | tf_op | source)
XLA Modules:
  0.0 130.7 jit_solution(4324064774417010145)
XLA Ops:
  0.6 0.1 pad_add_fusion.2.place
  0.7 3.4 %core_swap.4 = (bf16[256,2048]{1,0:T(8,128)(2,1)}, bf16[256,2048]{1,0:T(8,128)(2,1)}) custom-call(s32[2]{0:T(128)S(1)} %pad_add_fusion.2.place, bf16[256,8192]{1,0:T(8,128)(2,1)} %tokens.1), custom_call_target="tpu_custom_call" | custom-call | tf_op jit(solution)/shard_map/core_swap/pallas_call | solution.py:71
  4.1 0.1 collective-permute-start.1
  4.2 0.5 collective-permute-start.2
  4.7 0.1 collective-permute-start.3
  4.9 0.7 collective-permute-start
  5.6 0.1 pad_add_fusion.1.place
  5.7 0.1 pad_add_fusion.place
  5.7 4.2 %core_swap.3.own = bf16[2,2048,512]{2,1,0:T(8,128)(2,1)S(1)} custom-call(s32[2]{0:T(128)S(1)} %pad_add_fusion.1.place, bf16[256,8192]{1,0:T(8,128)(2,1)} %tokens.1, bf16[256,512]{1,0:T(8,128)(2,1)S(1)} %copy-done), custom_call_target="tpu_custom_call" | custom-call | tf_op jit(solution)/shard_map/core_swap/pallas_call | solution.py:97
  9.9 0.0 collective-permute-done.far_order
  9.9 0.0 collective-permute-done.3.key
  10.0 2.4 %core_swap.5 = (f32[4,8,16,512]{3,2,1,0:T(8,128)S(1)}, bf16[4,8,16,512]{3,2,1,0:T(8,128)(2,1)S(1)}, bf16[4,8,16,512]{3,2,1,0:T(8,128)(2,1)S(1)}, bf16[4,8,16,512...) custom-call(s32[2]{0:T(128)S(1)} %pad_add_fusion.place, ...), custom_call_target="tpu_custom_call" | custom-call | tf_op jit(solution)/shard_map/core_swap/pallas_call | solution.py:144
  12.4 0.6 collective-permute-start.4
  13.0 1.2 collective-permute-start.5
  14.2 2.1 %collective-permute-start.6 = (bf16[4,8,16,512]{3,2,1,0:T(8,128)(2,1)S(1)}, bf16[4,8,16,512]{3,2,1,0:T(8,128)(2,1)S(1)}, u32[]{:S(2)}, u32[]{:S(2)}) collective-permute-start(bf16[4,8,16,512]{3,2,1,0:T(8,128)(2,1)S(1)} %get-tuple-element.40), channel_id=1, source_target_pairs={{0,4},{128,132},{4,0},{132,128},{1,5},{129,133},{5,1},{133,129},{2... | collective-permute-start | bytes 1572872 | tf_op jit(solution)/shard_map/first_stage/ppermute | solution.py:33
  16.3 0.7 collective-permute-start.7
  17.1 0.8 collective-permute-start.8
  17.9 8.6 %collective-permute-done.4 = bf16[4,8,16,512]{3,2,1,0:T(8,128)(2,1)S(1)} collective-permute-done((bf16[4,8,16,512]{3,2,1,0:T(8,128)(2,1)S(1)}, bf16[4,8,16,512]{3,2,1,0:T(8,128)(2,1)S(1)}, u32[]{:S(2)}, u32[]{:S(2)}) %collective-permute-start.4) | collective-permute-done | bytes 524320 | tf_op jit(solution)/shard_map/first_stage/ppermute | solution.py:33
  26.5 1.4 %collective-permute-start.9 = (bf16[4,8,16,512]{3,2,1,0:T(8,128)(2,1)S(1)}, bf16[4,8,16,512]{3,2,1,0:T(8,128)(2,1)S(1)}, u32[]{:S(2)}, u32[]{:S(2)}) collective-permute-start(bf16[4,8,16,512]{3,2,1,0:T(8,128)(2,1)S(1)} %get-tuple-element.43), channel_id=1, source_target_pairs={{0,2},{1,3},{2,0},{3,1},{4,6},{5,7},{6,4},{7,5},{8,10},{9,11},{10,... | collective-permute-start | bytes 1572872 | tf_op jit(solution)/shard_map/first_stage/ppermute | solution.py:33
  27.9 2.7 %collective-permute-done.6 = bf16[4,8,16,512]{3,2,1,0:T(8,128)(2,1)S(1)} collective-permute-done((bf16[4,8,16,512]{3,2,1,0:T(8,128)(2,1)S(1)}, bf16[4,8,16,512]{3,2,1,0:T(8,128)(2,1)S(1)}, u32[]{:S(2)}, u32[]{:S(2)}) %collective-permute-start.6) | collective-permute-done | bytes 524320 | tf_op jit(solution)/shard_map/first_stage/ppermute | solution.py:33
  30.6 10.1 %collective-permute-done.7 = bf16[4,8,16,512]{3,2,1,0:T(8,128)(2,1)S(1)} collective-permute-done((bf16[4,8,16,512]{3,2,1,0:T(8,128)(2,1)S(1)}, bf16[4,8,16,512]{3,2,1,0:T(8,128)(2,1)S(1)}, u32[]{:S(2)}, u32[]{:S(2)}) %collective-permute-start.7) | collective-permute-done | bytes 524320 | tf_op jit(solution)/shard_map/first_stage/ppermute | solution.py:33
  40.6 1.7 %collective-permute-done.8 = bf16[4,8,16,512]{3,2,1,0:T(8,128)(2,1)S(1)} collective-permute-done((bf16[4,8,16,512]{3,2,1,0:T(8,128)(2,1)S(1)}, bf16[4,8,16,512]{3,2,1,0:T(8,128)(2,1)S(1)}, u32[]{:S(2)}, u32[]{:S(2)}) %collective-permute-start.8) | collective-permute-done | bytes 524320 | tf_op jit(solution)/shard_map/first_stage/ppermute | solution.py:33
  42.4 0.3 fusion.9
  42.7 2.6 %collective-permute-start.11 = (bf16[8,16,512]{2,1,0:T(8,128)(2,1)S(1)}, bf16[8,16,512]{2,1,0:T(8,128)(2,1)S(1)}, u32[]{:S(2)}, u32[]{:S(2)}) collective-permute-start(bf16[8,16,512]{2,1,0:T(8,128)(2,1)S(1)} %get-tuple-element.74), channel_id=1, source_target_pairs={{0,128},{128,4},{4,132},{132,0},{1,129},{129,5},{5,133},{133,1},{2... | collective-permute-start | bytes 393224 | tf_op jit(solution)/shard_map/second_stage/ppermute | solution.py:33
  45.2 0.5 collective-permute-start.12
  45.7 0.5 collective-permute-start.13
  46.2 0.3 fusion.11
  46.5 0.0 copy-start.3
  46.5 0.0 copy-start.4
  46.5 0.0 copy-start.5
  46.5 1.1 collective-permute-start.10
  47.7 1.0 collective-permute-start.14
  48.6 0.5 collective-permute-done.11
  49.1 1.9 %collective-permute-start.15 = (bf16[8,16,512]{2,1,0:T(8,128)(2,1)S(1)}, bf16[8,16,512]{2,1,0:T(8,128)(2,1)S(1)}, u32[]{:S(2)}, u32[]{:S(2)}) collective-permute-start(bf16[8,16,512]{2,1,0:T(8,128)(2,1)S(1)} %get-tuple-element.69), channel_id=1, source_target_pairs={{0,2},{1,3},{2,0},{3,1},{4,6},{5,7},{6,4},{7,5},{8,10},{9,11},{10,... | collective-permute-start | bytes 393224 | tf_op jit(solution)/shard_map/second_stage/ppermute | solution.py:33
  51.0 0.8 collective-permute-done.12
  51.8 1.3 collective-permute-done.13
  53.1 0.7 collective-permute-done.14
  53.8 1.8 %collective-permute-done.15 = bf16[8,16,512]{2,1,0:T(8,128)(2,1)S(1)} collective-permute-done((bf16[8,16,512]{2,1,0:T(8,128)(2,1)S(1)}, bf16[8,16,512]{2,1,0:T(8,128)(2,1)S(1)}, u32[]{:S(2)}, u32[]{:S(2)}) %collective-permute-start.15) | collective-permute-done | bytes 131104 | tf_op jit(solution)/shard_map/second_stage/ppermute | solution.py:33
  55.6 0.3 fusion.2
  56.0 3.7 %collective-permute-start.21 = (bf16[2048,512]{1,0:T(8,128)(2,1)S(1)}, bf16[2048,512]{1,0:T(8,128)(2,1)}, u32[]{:S(2)}, u32[]{:S(2)}) collective-permute-start(bf16[2048,512]{1,0:T(8,128)(2,1)S(1)} %copy-done.1), channel_id=1, source_target_pairs={{0,128},{64,196},{128,4},{192,64},{4,132},{68,192},{132,0},{196,68... | collective-permute-start | bytes 6291464 | tf_op jit(solution)/shard_map/weights/ppermute | solution.py:42
  59.7 18.7 %all_to_all.15 = bf16[8,32,512]{2,1,0:T(8,128)(2,1)S(1)} all-to-all(bf16[8,32,512]{2,1,0:T(8,128)(2,1)S(1)} %pad_maximum_fusion), channel_id=1, replica_groups=mesh['yl'=2,'c'=2,'z'=8,'yh'=2,'x'=4] {'z'}, dimensions={0} | all-to-all | bytes 524288 | tf_op jit(solution)/shard_map/third_stage/all_to_all | solution.py:298
  78.4 0.7 fusion.12
  79.2 0.8 broadcast_in_dim.6
  80.0 4.8 %all-to-all-start.1 = ((bf16[16,32,384]{2,1,0:T(8,128)(2,1)}), bf16[16,32,384]{2,1,0:T(8,128)(2,1)S(1)}, u32[]{:S(2)}, u32[]{:S(2)}) async-start(bf16[16,32,384]{2,1,0:T(8,128)(2,1)} %broadcast_in_dim.6), calls=%async_computation.1 | async-start | bytes 786432 | tf_op jit(solution)/shard_map/fresh_weights/all_to_all | solution.py:318
  84.8 0.7 collective-permute-start.16
  85.4 1.4 %collective-permute-start.17 = (bf16[32,128]{1,0:T(8,128)(2,1)S(1)}, bf16[32,128]{1,0:T(8,128)(2,1)S(1)}, u32[]{:S(2)}, u32[]{:S(2)}) collective-permute-start(bf16[32,128]{1,0:T(8,128)(2,1)S(1)} %get-tuple-element.76), channel_id=1, source_target_pairs={{0,2},{1,3},{2,0},{3,1},{4,6},{5,7},{6,4},{7,5},{8,10},{9,11},{10,... | collective-permute-start | bytes 24584 | tf_op jit(solution)/shard_map/fresh_weights/ppermute | solution.py:33
  86.8 1.3 %collective-permute-start.18 = (bf16[32,128]{1,0:T(8,128)(2,1)S(1)}, bf16[32,128]{1,0:T(8,128)(2,1)S(1)}, u32[]{:S(2)}, u32[]{:S(2)}) collective-permute-start(bf16[32,128]{1,0:T(8,128)(2,1)S(1)} %get-tuple-element.76), channel_id=1, source_target_pairs={{0,3},{1,0},{2,1},{3,2},{4,7},{5,4},{6,5},{7,6},{8,11},{9,8},{10,9... | collective-permute-start | bytes 24584 | tf_op jit(solution)/shard_map/fresh_weights/ppermute | solution.py:33
  88.2 0.4 collective-permute-done.16
  88.5 2.1 %collective-permute-done.17 = bf16[32,128]{1,0:T(8,128)(2,1)S(1)} collective-permute-done((bf16[32,128]{1,0:T(8,128)(2,1)S(1)}, bf16[32,128]{1,0:T(8,128)(2,1)S(1)}, u32[]{:S(2)}, u32[]{:S(2)}) %collective-permute-start.17) | collective-permute-done | bytes 8224 | tf_op jit(solution)/shard_map/fresh_weights/ppermute | solution.py:33
  90.6 1.1 collective-permute-done.18
  91.7 3.5 %all-to-all-done.1.rest_0_ = bf16[16,32,384]{2,1,0:T(8,128)(2,1)S(1)} async-done(((bf16[16,32,384]{2,1,0:T(8,128)(2,1)}), bf16[16,32,384]{2,1,0:T(8,128)(2,1)S(1)}, u32[]{:S(2)}, u32[]{:S(2)}) %all-to-all-start.1) | async-done | bytes 393248 | tf_op jit(solution)/shard_map/fresh_weights/all_to_all | solution.py:318
  95.2 0.9 broadcast_in_dim.7
  96.1 6.4 %all-to-all-start.2 = ((bf16[16,4,32,128]{3,2,1,0:T(8,128)(2,1)}), bf16[16,4,32,128]{3,2,1,0:T(8,128)(2,1)S(1)}, u32[]{:S(2)}, u32[]{:S(2)}) async-start(bf16[16,4,32,128]{3,2,1,0:T(8,128)(2,1)} %broadcast_in_dim.7), calls=%async_computation.2 | async-start | bytes 1048576 | tf_op jit(solution)/shard_map/fresh_weights/all_to_all | solution.py:318
  102.6 1.3 %collective-permute-start.19 = (bf16[16,32,384]{2,1,0:T(8,128)(2,1)S(1)}, bf16[16,32,384]{2,1,0:T(8,128)(2,1)S(1)}, u32[]{:S(2)}, u32[]{:S(2)}) collective-permute-start(bf16[16,32,384]{2,1,0:T(8,128)(2,1)S(1)} %all-to-all-done.1.rest_0_), channel_id=1, source_target_pairs={{0,1},{1,2},{2,3},{3,0},{4,5},{5,6},{6,7},{7,4},{8,9},{9,10},{10,1... | collective-permute-start | bytes 1179656 | tf_op jit(solution)/shard_map/fresh_weights/ppermute | solution.py:33
  103.9 0.7 collective-permute-start.20
  104.6 1.9 %collective-permute-start.24 = (bf16[16,32,384]{2,1,0:T(8,128)(2,1)S(1)}, bf16[16,32,384]{2,1,0:T(8,128)(2,1)}, u32[]{:S(2)}, u32[]{:S(2)}) collective-permute-start(bf16[16,32,384]{2,1,0:T(8,128)(2,1)S(1)} %all-to-all-done.1.rest_0_), channel_id=1, source_target_pairs={{0,2},{1,3},{2,0},{3,1},{4,6},{5,7},{6,4},{7,5},{8,10},{9,11},{10,... | collective-permute-start | bytes 1179656 | tf_op jit(solution)/shard_map/fresh_weights/ppermute | solution.py:33
  106.4 0.1 pad_add_fusion.4.place
  106.5 0.1 pad_add_fusion.3.place
  106.6 5.5 %input_grad.2.rest_0_ = bf16[256,8192]{1,0:T(8,128)(2,1)} custom-call(s32[2]{0:T(128)S(1)} %pad_add_fusion.4.place, bf16[256,512]{1,0:T(8,128)(2,1)S(1)} %copy-done, bf16[2048,512]{1,0:T(8,128)(2,1)S(1)} %copy-done.1, bf16[2048,512]{1,0:T(8,128)(2,1)} %collective-permute-done.23.second), custom_call_target="tpu_custom_call" | custom-call | tf_op jit(solution)/shard_map/input_grad/pallas_call | solution.py:172
  112.1 5.9 %input_grad.3 = bf16[256,8192]{1,0:T(8,128)(2,1)} custom-call(s32[2]{0:T(128)S(1)} %pad_add_fusion.3.place, bf16[256,512]{1,0:T(8,128)(2,1)S(1)} %copy-done, bf16[2048,512]{1,0:T(8,128)(2,1)} %collective-permute-done.21.first, bf16[2048,512]{1,0:T(8,128)(2,1)} %collective-permute-done.22.second, ...), custom_call_target="tpu_custom_call", output_to_operand_aliasing={{}: (4, {})} | custom-call | tf_op jit(solution)/shard_map/input_grad/pallas_call | solution.py:172
  118.0 6.2 %collective-permute-done.20.rest_2_ = bf16[16,32,384]{2,1,0:T(8,128)(2,1)S(1)} collective-permute-done((bf16[16,32,384]{2,1,0:T(8,128)(2,1)S(1)}, bf16[16,32,384]{2,1,0:T(8,128)(2,1)S(1)}, u32[]{:S(2)}, u32[]{:S(2)}) %collective-permute-start.20) | collective-permute-done | bytes 393248 | tf_op jit(solution)/shard_map/fresh_weights/ppermute | solution.py:33
  124.2 2.0 %rows.3.rest_1_ = bf16[2048,512]{1,0:T(8,128)(2,1)} custom-call(s32[1]{0:T(128)} %bitcast.place, s32[1,64]{1,0:T(1,128)S(1)} %copy-done.2, bf16[16,32,384]{2,1,0:T(8,128)(2,1)S(1)} %all-to-all-done.1.rest_0_, bf16[16,32,384]{2,1,0:T(8,128)(2,1)S(1)} %collective-permute-done.19.rest_1_, bf16[16,32,384]{2,1,0:T(8,128)(2,1)S(1)} %collective-permute-done.20.rest_2_), custom_call_target="tpu_custom_call" | custom-call | tf_op jit(solution)/shard_map/rows/pallas_call | solution.py:223
  126.2 2.0 %rows.4.rest_1_ = bf16[2048,512]{1,0:T(8,128)(2,1)} custom-call(s32[1]{0:T(128)} %bitcast.place, s32[1,64]{1,0:T(1,128)S(1)} %copy-done.2, bf16[16,4,32,128]{3,2,1,0:T(8,128)(2,1)S(1)} %all-to-all-done.2.rest_0_, bf16[2048,512]{1,0:T(8,128)(2,1)} %rows.3.rest_1_), custom_call_target="tpu_custom_call", output_to_operand_aliasing={{}: (3, {})} | custom-call | tf_op jit(solution)/shard_map/rows/pallas_call | solution.py:223
  128.1 2.4 %rows.5 = bf16[2048,512]{1,0:T(8,128)(2,1)} custom-call(s32[1]{0:T(128)} %bitcast.place, s32[1,64]{1,0:T(1,128)S(1)} %copy-done.2, bf16[16,32,384]{2,1,0:T(8,128)(2,1)} %collective-permute-done.24.rest_0_, bf16[2048,512]{1,0:T(8,128)(2,1)} %rows.4.rest_1_), custom_call_target="tpu_custom_call", output_to_operand_aliasing={{}: (3, {})} | custom-call | tf_op jit(solution)/shard_map/rows/pallas_call | solution.py:223
  (26 shorter events, 0.1 us)
Async XLA Ops:
  0.7 4.0 %copy-start = (bf16[256,512]{1,0:T(8,128)(2,1)S(1)}, bf16[256,512]{1,0:T(8,128)(2,1)}, u32[]{:S(2)}) copy-start(bf16[256,512]{1,0:T(8,128)(2,1)} %key.5) | copy-start | bytes 786436
  0.7 4.1 %copy-start.2 = (s32[1,64]{1,0:T(1,128)S(1)}, s32[1,64]{1,0:T(1,128)}, u32[]{:S(2)}) copy-start(s32[1,64]{1,0:T(1,128)} %order.5) | copy-start | bytes 772
  4.1 5.8 %collective-permute-start.1 = (bf16[256,2048]{1,0:T(8,128)(2,1)}, bf16[256,2048]{1,0:T(8,128)(2,1)S(1)}, u32[]{:S(2)}, u32[]{:S(2)}) collective-permute-start(bf16[256,2048]{1,0:T(8,128)(2,1)} %get-tuple-element.35), channel_id=1, source_target_pairs={{0,64},{64,0},{1,65},{65,1},{2,66},{66,2},{3,67},{67,3},{4,68},{68... | collective-permute-start | bytes 3145736 | tf_op jit(solution)/shard_map/core_swap/ppermute | solution.py:33
  4.2 5.7 %collective-permute-start.2 = (bf16[256,2048]{1,0:T(8,128)(2,1)}, bf16[256,2048]{1,0:T(8,128)(2,1)S(1)}, u32[]{:S(2)}, u32[]{:S(2)}) collective-permute-start(bf16[256,2048]{1,0:T(8,128)(2,1)} %get-tuple-element.36), channel_id=1, source_target_pairs={{0,64},{64,0},{1,65},{65,1},{2,66},{66,2},{3,67},{67,3},{4,68},{68... | collective-permute-start | bytes 3145736 | tf_op jit(solution)/shard_map/core_swap/ppermute | solution.py:33
  4.7 5.2 %collective-permute-start.3 = (bf16[256,512]{1,0:T(8,128)(2,1)S(1)}, bf16[256,512]{1,0:T(8,128)(2,1)S(1)}, u32[]{:S(2)}, u32[]{:S(2)}) collective-permute-start(bf16[256,512]{1,0:T(8,128)(2,1)S(1)} %copy-done), channel_id=1, source_target_pairs={{0,64},{64,0},{1,65},{65,1},{2,66},{66,2},{3,67},{67,3},{4,68},{68... | collective-permute-start | bytes 786440 | tf_op jit(solution)/shard_map/core_swap/ppermute | solution.py:33
  4.9 5.1 %collective-permute-start = (s32[1,64]{1,0:T(1,128)S(1)}, s32[1,64]{1,0:T(1,128)S(1)}, u32[]{:S(2)}, u32[]{:S(2)}) collective-permute-start(s32[1,64]{1,0:T(1,128)S(1)} %copy-done.2), channel_id=1, source_target_pairs={{0,128},{128,0},{1,129},{129,1},{2,130},{130,2},{3,131},{131,3},{4... | collective-permute-start | bytes 776 | tf_op jit(solution)/shard_map/core_swap/ppermute | solution.py:33
  12.4 14.1 %collective-permute-start.4 = (bf16[4,8,16,512]{3,2,1,0:T(8,128)(2,1)S(1)}, bf16[4,8,16,512]{3,2,1,0:T(8,128)(2,1)S(1)}, u32[]{:S(2)}, u32[]{:S(2)}) collective-permute-start(bf16[4,8,16,512]{3,2,1,0:T(8,128)(2,1)S(1)} %get-tuple-element.38), channel_id=1, source_target_pairs={{0,1},{1,2},{2,3},{3,0},{4,5},{5,6},{6,7},{7,4},{8,9},{9,10},{10,1... | collective-permute-start | bytes 1572872 | tf_op jit(solution)/shard_map/first_stage/ppermute | solution.py:33
  13.0 14.9 %collective-permute-start.5 = (bf16[4,8,16,512]{3,2,1,0:T(8,128)(2,1)S(1)}, bf16[4,8,16,512]{3,2,1,0:T(8,128)(2,1)S(1)}, u32[]{:S(2)}, u32[]{:S(2)}) collective-permute-start(bf16[4,8,16,512]{3,2,1,0:T(8,128)(2,1)S(1)} %get-tuple-element.39), channel_id=1, source_target_pairs={{0,128},{128,4},{4,132},{132,0},{1,129},{129,5},{5,133},{133,1},{2... | collective-permute-start | bytes 1572872 | tf_op jit(solution)/shard_map/first_stage/ppermute | solution.py:33
  14.2 16.4 %collective-permute-start.6 = (bf16[4,8,16,512]{3,2,1,0:T(8,128)(2,1)S(1)}, bf16[4,8,16,512]{3,2,1,0:T(8,128)(2,1)S(1)}, u32[]{:S(2)}, u32[]{:S(2)}) collective-permute-start(bf16[4,8,16,512]{3,2,1,0:T(8,128)(2,1)S(1)} %get-tuple-element.40), channel_id=1, source_target_pairs={{0,4},{128,132},{4,0},{132,128},{1,5},{129,133},{5,1},{133,129},{2... | collective-permute-start | bytes 1572872 | tf_op jit(solution)/shard_map/first_stage/ppermute | solution.py:33
  16.3 24.3 %collective-permute-start.7 = (bf16[4,8,16,512]{3,2,1,0:T(8,128)(2,1)S(1)}, bf16[4,8,16,512]{3,2,1,0:T(8,128)(2,1)S(1)}, u32[]{:S(2)}, u32[]{:S(2)}) collective-permute-start(bf16[4,8,16,512]{3,2,1,0:T(8,128)(2,1)S(1)} %get-tuple-element.41), channel_id=1, source_target_pairs={{0,132},{128,0},{4,128},{132,4},{1,133},{129,1},{5,129},{133,5},{2... | collective-permute-start | bytes 1572872 | tf_op jit(solution)/shard_map/first_stage/ppermute | solution.py:33
  17.1 25.3 %collective-permute-start.8 = (bf16[4,8,16,512]{3,2,1,0:T(8,128)(2,1)S(1)}, bf16[4,8,16,512]{3,2,1,0:T(8,128)(2,1)S(1)}, u32[]{:S(2)}, u32[]{:S(2)}) collective-permute-start(bf16[4,8,16,512]{3,2,1,0:T(8,128)(2,1)S(1)} %get-tuple-element.42), channel_id=1, source_target_pairs={{0,3},{1,0},{2,1},{3,2},{4,7},{5,4},{6,5},{7,6},{8,11},{9,8},{10,9... | collective-permute-start | bytes 1572872 | tf_op jit(solution)/shard_map/first_stage/ppermute | solution.py:33
  26.5 15.9 %collective-permute-start.9 = (bf16[4,8,16,512]{3,2,1,0:T(8,128)(2,1)S(1)}, bf16[4,8,16,512]{3,2,1,0:T(8,128)(2,1)S(1)}, u32[]{:S(2)}, u32[]{:S(2)}) collective-permute-start(bf16[4,8,16,512]{3,2,1,0:T(8,128)(2,1)S(1)} %get-tuple-element.43), channel_id=1, source_target_pairs={{0,2},{1,3},{2,0},{3,1},{4,6},{5,7},{6,4},{7,5},{8,10},{9,11},{10,... | collective-permute-start | bytes 1572872 | tf_op jit(solution)/shard_map/first_stage/ppermute | solution.py:33
  42.7 6.5 %collective-permute-start.11 = (bf16[8,16,512]{2,1,0:T(8,128)(2,1)S(1)}, bf16[8,16,512]{2,1,0:T(8,128)(2,1)S(1)}, u32[]{:S(2)}, u32[]{:S(2)}) collective-permute-start(bf16[8,16,512]{2,1,0:T(8,128)(2,1)S(1)} %get-tuple-element.74), channel_id=1, source_target_pairs={{0,128},{128,4},{4,132},{132,0},{1,129},{129,5},{5,133},{133,1},{2... | collective-permute-start | bytes 393224 | tf_op jit(solution)/shard_map/second_stage/ppermute | solution.py:33
  45.2 6.6 %collective-permute-start.12 = (bf16[8,16,512]{2,1,0:T(8,128)(2,1)S(1)}, bf16[8,16,512]{2,1,0:T(8,128)(2,1)S(1)}, u32[]{:S(2)}, u32[]{:S(2)}) collective-permute-start(bf16[8,16,512]{2,1,0:T(8,128)(2,1)S(1)} %get-tuple-element.73), channel_id=1, source_target_pairs={{0,4},{128,132},{4,0},{132,128},{1,5},{129,133},{5,1},{133,129},{2... | collective-permute-start | bytes 393224 | tf_op jit(solution)/shard_map/second_stage/ppermute | solution.py:33
  45.7 7.4 %collective-permute-start.13 = (bf16[8,16,512]{2,1,0:T(8,128)(2,1)S(1)}, bf16[8,16,512]{2,1,0:T(8,128)(2,1)S(1)}, u32[]{:S(2)}, u32[]{:S(2)}) collective-permute-start(bf16[8,16,512]{2,1,0:T(8,128)(2,1)S(1)} %get-tuple-element.72), channel_id=1, source_target_pairs={{0,132},{128,0},{4,128},{132,4},{1,133},{129,1},{5,129},{133,5},{2... | collective-permute-start | bytes 393224 | tf_op jit(solution)/shard_map/second_stage/ppermute | solution.py:33
  46.2 9.7 %copy-start.1 = (bf16[2048,512]{1,0:T(8,128)(2,1)S(1)}, bf16[2048,512]{1,0:T(8,128)(2,1)}, u32[]{:S(2)}) copy-start(bf16[2048,512]{1,0:T(8,128)(2,1)} %first.1) | copy-start | bytes 6291460
  46.5 31.9 %copy-start.3 = (f32[32,512]{1,0:T(8,128)S(1)}, f32[32,512]{1,0:T(8,128)}, u32[]{:S(2)}) copy-start(f32[32,512]{1,0:T(8,128)} %param.10) | copy-start | bytes 196612
  46.5 31.9 %copy-start.4 = (f32[32,512]{1,0:T(8,128)S(1)}, f32[32,512]{1,0:T(8,128)}, u32[]{:S(2)}) copy-start(f32[32,512]{1,0:T(8,128)} %param.11) | copy-start | bytes 196612
  46.5 31.9 %copy-start.5 = (f32[32,512]{1,0:T(8,128)S(1)}, f32[32,512]{1,0:T(8,128)}, u32[]{:S(2)}) copy-start(f32[32,512]{1,0:T(8,128)} %param.12) | copy-start | bytes 196612
  46.5 6.6 %collective-permute-start.10 = (bf16[8,16,512]{2,1,0:T(8,128)(2,1)S(1)}, bf16[8,16,512]{2,1,0:T(8,128)(2,1)S(1)}, u32[]{:S(2)}, u32[]{:S(2)}) collective-permute-start(bf16[8,16,512]{2,1,0:T(8,128)(2,1)S(1)} %get-tuple-element.71), channel_id=1, source_target_pairs={{0,1},{1,2},{2,3},{3,0},{4,5},{5,6},{6,7},{7,4},{8,9},{9,10},{10,1... | collective-permute-start | bytes 393224 | tf_op jit(solution)/shard_map/second_stage/ppermute | solution.py:33
  47.7 6.2 %collective-permute-start.14 = (bf16[8,16,512]{2,1,0:T(8,128)(2,1)S(1)}, bf16[8,16,512]{2,1,0:T(8,128)(2,1)S(1)}, u32[]{:S(2)}, u32[]{:S(2)}) collective-permute-start(bf16[8,16,512]{2,1,0:T(8,128)(2,1)S(1)} %get-tuple-element.70), channel_id=1, source_target_pairs={{0,3},{1,0},{2,1},{3,2},{4,7},{5,4},{6,5},{7,6},{8,11},{9,8},{10,9... | collective-permute-start | bytes 393224 | tf_op jit(solution)/shard_map/second_stage/ppermute | solution.py:33
  49.1 6.5 %collective-permute-start.15 = (bf16[8,16,512]{2,1,0:T(8,128)(2,1)S(1)}, bf16[8,16,512]{2,1,0:T(8,128)(2,1)S(1)}, u32[]{:S(2)}, u32[]{:S(2)}) collective-permute-start(bf16[8,16,512]{2,1,0:T(8,128)(2,1)S(1)} %get-tuple-element.69), channel_id=1, source_target_pairs={{0,2},{1,3},{2,0},{3,1},{4,6},{5,7},{6,4},{7,5},{8,10},{9,11},{10,... | collective-permute-start | bytes 393224 | tf_op jit(solution)/shard_map/second_stage/ppermute | solution.py:33
  56.0 39.2 %collective-permute-start.21 = (bf16[2048,512]{1,0:T(8,128)(2,1)S(1)}, bf16[2048,512]{1,0:T(8,128)(2,1)}, u32[]{:S(2)}, u32[]{:S(2)}) collective-permute-start(bf16[2048,512]{1,0:T(8,128)(2,1)S(1)} %copy-done.1), channel_id=1, source_target_pairs={{0,128},{64,196},{128,4},{192,64},{4,132},{68,192},{132,0},{196,68... | collective-permute-start | bytes 6291464 | tf_op jit(solution)/shard_map/weights/ppermute | solution.py:42
  80.0 15.2 %all-to-all-start.1 = ((bf16[16,32,384]{2,1,0:T(8,128)(2,1)}), bf16[16,32,384]{2,1,0:T(8,128)(2,1)S(1)}, u32[]{:S(2)}, u32[]{:S(2)}) async-start(bf16[16,32,384]{2,1,0:T(8,128)(2,1)} %broadcast_in_dim.6), calls=%async_computation.1 | async-start | bytes 786432 | tf_op jit(solution)/shard_map/fresh_weights/all_to_all | solution.py:318
  84.8 3.7 %collective-permute-start.16 = (bf16[32,128]{1,0:T(8,128)(2,1)S(1)}, bf16[32,128]{1,0:T(8,128)(2,1)S(1)}, u32[]{:S(2)}, u32[]{:S(2)}) collective-permute-start(bf16[32,128]{1,0:T(8,128)(2,1)S(1)} %get-tuple-element.76), channel_id=1, source_target_pairs={{0,1},{1,2},{2,3},{3,0},{4,5},{5,6},{6,7},{7,4},{8,9},{9,10},{10,1... | collective-permute-start | bytes 24584 | tf_op jit(solution)/shard_map/fresh_weights/ppermute | solution.py:33
  85.4 5.2 %collective-permute-start.17 = (bf16[32,128]{1,0:T(8,128)(2,1)S(1)}, bf16[32,128]{1,0:T(8,128)(2,1)S(1)}, u32[]{:S(2)}, u32[]{:S(2)}) collective-permute-start(bf16[32,128]{1,0:T(8,128)(2,1)S(1)} %get-tuple-element.76), channel_id=1, source_target_pairs={{0,2},{1,3},{2,0},{3,1},{4,6},{5,7},{6,4},{7,5},{8,10},{9,11},{10,... | collective-permute-start | bytes 24584 | tf_op jit(solution)/shard_map/fresh_weights/ppermute | solution.py:33
  86.8 4.9 %collective-permute-start.18 = (bf16[32,128]{1,0:T(8,128)(2,1)S(1)}, bf16[32,128]{1,0:T(8,128)(2,1)S(1)}, u32[]{:S(2)}, u32[]{:S(2)}) collective-permute-start(bf16[32,128]{1,0:T(8,128)(2,1)S(1)} %get-tuple-element.76), channel_id=1, source_target_pairs={{0,3},{1,0},{2,1},{3,2},{4,7},{5,4},{6,5},{7,6},{8,11},{9,8},{10,9... | collective-permute-start | bytes 24584 | tf_op jit(solution)/shard_map/fresh_weights/ppermute | solution.py:33
  88.1 18.4 %collective-permute-start.23 = (bf16[2048,512]{1,0:T(8,128)(2,1)S(1)}, bf16[2048,512]{1,0:T(8,128)(2,1)}, u32[]{:S(2)}, u32[]{:S(2)}) collective-permute-start(bf16[2048,512]{1,0:T(8,128)(2,1)S(1)} %copy-done.1), channel_id=1, source_target_pairs={{0,64},{64,0},{1,65},{65,1},{2,66},{66,2},{3,67},{67,3},{4,68},{68... | collective-permute-start | bytes 6291464 | tf_op jit(solution)/shard_map/weights/ppermute | solution.py:33
  95.2 16.9 %collective-permute-start.22 = (bf16[2048,512]{1,0:T(8,128)(2,1)}, bf16[2048,512]{1,0:T(8,128)(2,1)}, u32[]{:S(2)}, u32[]{:S(2)}) collective-permute-start(bf16[2048,512]{1,0:T(8,128)(2,1)} %collective-permute-done.21.first), channel_id=1, source_target_pairs={{0,64},{64,0},{1,65},{65,1},{2,66},{66,2},{3,67},{67,3},{4,68},{68... | collective-permute-start | bytes 6291464 | tf_op jit(solution)/shard_map/input_grad/ppermute | solution.py:33
  96.1 30.0 %all-to-all-start.2 = ((bf16[16,4,32,128]{3,2,1,0:T(8,128)(2,1)}), bf16[16,4,32,128]{3,2,1,0:T(8,128)(2,1)S(1)}, u32[]{:S(2)}, u32[]{:S(2)}) async-start(bf16[16,4,32,128]{3,2,1,0:T(8,128)(2,1)} %broadcast_in_dim.7), calls=%async_computation.2 | async-start | bytes 1048576 | tf_op jit(solution)/shard_map/fresh_weights/all_to_all | solution.py:318
  102.6 15.5 %collective-permute-start.19 = (bf16[16,32,384]{2,1,0:T(8,128)(2,1)S(1)}, bf16[16,32,384]{2,1,0:T(8,128)(2,1)S(1)}, u32[]{:S(2)}, u32[]{:S(2)}) collective-permute-start(bf16[16,32,384]{2,1,0:T(8,128)(2,1)S(1)} %all-to-all-done.1.rest_0_), channel_id=1, source_target_pairs={{0,1},{1,2},{2,3},{3,0},{4,5},{5,6},{6,7},{7,4},{8,9},{9,10},{10,1... | collective-permute-start | bytes 1179656 | tf_op jit(solution)/shard_map/fresh_weights/ppermute | solution.py:33
  103.9 20.3 %collective-permute-start.20 = (bf16[16,32,384]{2,1,0:T(8,128)(2,1)S(1)}, bf16[16,32,384]{2,1,0:T(8,128)(2,1)S(1)}, u32[]{:S(2)}, u32[]{:S(2)}) collective-permute-start(bf16[16,32,384]{2,1,0:T(8,128)(2,1)S(1)} %all-to-all-done.1.rest_0_), channel_id=1, source_target_pairs={{0,3},{1,0},{2,1},{3,2},{4,7},{5,4},{6,5},{7,6},{8,11},{9,8},{10,9... | collective-permute-start | bytes 1179656 | tf_op jit(solution)/shard_map/fresh_weights/ppermute | solution.py:33
  104.6 23.5 %collective-permute-start.24 = (bf16[16,32,384]{2,1,0:T(8,128)(2,1)S(1)}, bf16[16,32,384]{2,1,0:T(8,128)(2,1)}, u32[]{:S(2)}, u32[]{:S(2)}) collective-permute-start(bf16[16,32,384]{2,1,0:T(8,128)(2,1)S(1)} %all-to-all-done.1.rest_0_), channel_id=1, source_target_pairs={{0,2},{1,3},{2,0},{3,1},{4,6},{5,7},{6,4},{7,5},{8,10},{9,11},{10,... | collective-permute-start | bytes 1179656 | tf_op jit(solution)/shard_map/fresh_weights/ppermute | solution.py:33

commit v6 on v4

--- a/solution.py
+++ b/solution.py
@@ -155,9 +155,9 @@
     )(place, far_order, near_order, own, far, near, key)
 
 
-def input_grad_kernel(place, key, first, second, *rest):
+def input_grad_kernel(count, place, key, *rest):
     out = rest[-1]
-    for n, weight in enumerate((first, second)):
+    for n, weight in enumerate(rest[:count]):
 
         @pl.when(lax.div(pl.program_id(0), 2) == n)
         def _(weight=weight):
@@ -166,19 +166,20 @@
             ).astype(out.dtype)
 
 
-def input_grad_of(place, key, first, second, width, before=None):
-    cut = first.shape[0] // 2
+def input_grad_of(place, key, weights, width, before=None):
+    count, cut = len(weights), weights[0].shape[0] // 2
     extra = [] if before is None else [before]
-    return pl.pallas_call(
-        input_grad_kernel,
+
+    def rows_of(n):
+        return spec((cut, key.shape[1]), lambda i, place: (jnp.clip(i - 2 * n, 0, 1), 0))
+
+    return pl.pallas_call(
+        functools.partial(input_grad_kernel, count),
         grid_spec=pltpu.PrefetchScalarGridSpec(
             num_scalar_prefetch=1,
-            grid=(4,),
-            in_specs=[
-                spec(key.shape, lambda i, place: (0, 0)),
-                spec((cut, key.shape[1]), lambda i, place: (jnp.minimum(i, 1), 0)),
-                spec((cut, key.shape[1]), lambda i, place: (jnp.maximum(i - 2, 0), 0)),
-            ]
+            grid=(2 * count,),
+            in_specs=[spec(key.shape, lambda i, place: (0, 0))]
+            + [rows_of(n) for n in range(count)]
             + [pl.BlockSpec(memory_space=pl.ANY)] * len(extra),
             out_specs=spec(
                 (key.shape[0], cut),
@@ -186,9 +187,9 @@
             ),
         ),
         out_shape=jax.ShapeDtypeStruct((key.shape[0], width), jnp.bfloat16),
-        input_output_aliases={4: 0} if extra else {},
+        input_output_aliases={2 + count: 0} if extra else {},
         compiler_params=params(12),
-    )(place, key, first, second, *extra)
+    )(place, key, *weights, *extra)
 
 
 def rows_kernel(steps, place, order, *rest):
@@ -196,13 +197,14 @@
     x = place[0]
     block_rows = parts[0].shape[1]
     copies = []
-    for i, k in enumerate(steps):
+    for part, (k, first) in zip(parts, steps):
         from_x = lax.rem(x + NX - k, NX)
-        for n in range(NZ * NYH):
-            start = pl.multiple_of(order[0, n * NX + from_x] * block_rows, block_rows)
+        for n in range(part.shape[0]):
+            block = order[0, (first + n) * NX + from_x]
+            start = pl.multiple_of(block * block_rows, block_rows)
             copies.append(
                 pltpu.make_async_copy(
-                    parts[i].at[n], out.at[pl.ds(start, block_rows), :], sems.at[i, n]
+                    part.at[n], out.at[pl.ds(start, block_rows), :], sems.at[len(copies)]
                 )
             )
     for copy in copies:
@@ -211,7 +213,7 @@
         copy.wait()
 
 
-def put_in_rows(place, order, parts, rows, before=None):
+def put_in_rows(place, order, parts, shape, before=None):
     steps, values = tuple(parts), list(parts.values())
     extra = [] if before is None else [before]
     return pl.pallas_call(
@@ -221,9 +223,9 @@
             grid=(1,),
             in_specs=[vmem()] * len(values) + [pl.BlockSpec(memory_space=pl.ANY)] * len(extra),
             out_specs=pl.BlockSpec(memory_space=pl.ANY),
-            scratch_shapes=[pltpu.SemaphoreType.DMA((len(steps), NZ * NYH))],
-        ),
-        out_shape=jax.ShapeDtypeStruct((rows, values[0].shape[2]), values[0].dtype),
+            scratch_shapes=[pltpu.SemaphoreType.DMA((sum(v.shape[0] for v in values),))],
+        ),
+        out_shape=jax.ShapeDtypeStruct(shape, values[0].dtype),
         input_output_aliases={2 + len(values): 0} if extra else {},
         compiler_params=params(6),
     )(place, order, *values, *extra)
@@ -244,7 +246,8 @@
     tokens_in, key_cotangent, key_weight, master_store, first_moment, second_moment, writer
 ):
     yl, c, _, yh, x = (lax.axis_index(name) for name in AXES)
-    tok_rows, width = tokens_in.shape
+    tok_rows, depth = tokens_in.shape
+    width = key_weight.shape[1]
     rows_here = key_weight.shape[0]
     block_rows = master_store.shape[0]
 
@@ -280,15 +283,20 @@
 
     with jax.named_scope("second_stage"):
         second_half, first_half = (total_of(got) for got in exchange(second, first))
-        blocks = jnp.concatenate([first_half, second_half], axis=1)
+        blocks = jnp.concatenate([first_half, second_half], axis=1).astype(jnp.bfloat16)
 
     with jax.named_scope("weights"):
         core = send(key_weight, "c", 1)
         held, blocks = lax.optimization_barrier((key_weight, blocks))
         other = cross(held)
 
+    with jax.named_scope("input_grad"):
+        place = jnp.stack([here + c, here + 1 - c]).astype(jnp.int32)
+        input_grad = input_grad_of(place, key_cotangent, [key_weight, core], depth)
+
     with jax.named_scope("third_stage"):
         parts = lax.all_to_all(blocks, "z", 0, 0, tiled=True)
+        parts, input_grad = lax.optimization_barrier((parts, input_grad))
         own_block = total_of([parts[n] for n in range(NZ)])
 
     with jax.named_scope("adam"):
@@ -303,26 +311,32 @@
         )
 
     with jax.named_scope("fresh_weights"):
-        fresh = jnp.broadcast_to(
-            master_new.astype(jnp.bfloat16), (NZ * NYH,) + master_new.shape
-        )
+        fresh = master_new.astype(jnp.bfloat16)
+        fresh = jnp.broadcast_to(fresh, (NZ * NYH,) + fresh.shape)
         plane = lax.all_to_all(fresh, ("z", "yh"), 0, 0, tiled=True)
-        parts = {k: send(plane, "x", k) for k in (1, 3, 2)}
+        half = NZ * NYH // 2
+        low, high = plane[:half], plane[half:]
+        parts = {(1, 0): send(low, "x", 1), (3, half): send(high, "x", 3)}
+        parts |= {(1, half): send(high, "x", 1), (3, 0): send(low, "x", 3)}
+        last = {
+            (2, 0): send(parts[1, 0], "x", 1),
+            (2, half): send(parts[3, half], "x", 3),
+        }
 
     with jax.named_scope("input_grad"):
-        place = jnp.stack([here + c, here + 1 - c]).astype(jnp.int32)
-        input_grad = input_grad_of(place, key_cotangent, key_weight, core, width)
         other, _ = lax.optimization_barrier((other, plane))
         other_core = send(other, "c", 1)
         place = jnp.stack([there + c, there + 1 - c]).astype(jnp.int32)
-        input_grad = input_grad_of(place, key_cotangent, other, other_core, width, input_grad)
+        input_grad = input_grad_of(
+            place, key_cotangent, [other, other_core], depth, input_grad
+        )
 
     with jax.named_scope("rows"):
-        last = {2: parts.pop(2)}
-        parts, input_grad = lax.optimization_barrier(({0: plane} | parts, input_grad))
+        *values, input_grad = lax.optimization_barrier((*parts.values(), input_grad))
+        parts = {(0, 0): plane} | dict(zip(parts, values))
         place = jnp.stack([x]).astype(jnp.int32)
-        weight_new = put_in_rows(place, writer, parts, rows_here)
-        weight_new = put_in_rows(place, writer, last, rows_here, weight_new)
+        weight_new = put_in_rows(place, writer, parts, key_weight.shape)
+        weight_new = put_in_rows(place, writer, last, key_weight.shape, weight_new)
     return (input_grad, master_new, moment_one, moment_two, weight_new)
 
 

time: 133 us -> 126 us (0.947)
  waiting for transfers between devices: 56.9 us -> 32.8 us
  blocking collectives: 0 us -> 16.3 us
    all_to_all x0 -> x1, blocking collectives: none -> 16.3 us  [on_device(): plane = lax.all_to_all(fresh, ('z', 'yh'), 0, 0, tiled=True)]
    all_to_all x1, waiting for transfers between devices: 13 us -> 3.8 us  [on_device(): parts = lax.all_to_all(blocks, 'z', 0, 0, tiled=True)]
    all_to_all x1 -> x0, waiting for transfers between devices: 8.07 us -> none  [on_device(): plane = lax.all_to_all(fresh, ('z', 'yh'), 0, 0, tiled=True)]
    ppermute x21 -> x24, waiting for transfers between devices: 35.9 us -> 29 us  [send(): lax.ppermute(value, ('yl', 'yh') if axis == 'y' else axis, shift(axis, st...]
    ppermute x21 -> x24, starting transfers between devices: 35 us -> 38.6 us  [send(): lax.ppermute(value, ('yl', 'yh') if axis == 'y' else axis, shift(axis, st...]
    all_to_all x1 -> x0, starting transfers between devices: 3.57 us -> none  [on_device(): plane = lax.all_to_all(fresh, ('z', 'yh'), 0, 0, tiled=True)]
  transfers between devices with their start and end apart: 24 -> 26, of which waited for: 12 -> 10; matrix products, arithmetic and copies ran while one was open for 2% -> 2% of each run, Pallas kernels for 13% -> 13%
where the time goes in v6:
time: 126 us; the launch traced here: 125 us
  starting transfers between devices  47 us (37%)
  waiting for transfers between devices  32.8 us (26%)
  Pallas kernels  25.1 us (20%)
  blocking collectives  16.3 us (13%)
  other arithmetic  2.72 us (2%)
    ppermute x24, starting transfers between devices, send(): lax.ppermute(value, ('yl', 'yh') if axis == 'y' else axis, shift(axis, st...  38.6 us
    ppermute x24, waiting for transfers between devices, send(): lax.ppermute(value, ('yl', 'yh') if axis == 'y' else axis, shift(axis, st...  29 us
    all_to_all x1, blocking collectives, on_device(): plane = lax.all_to_all(fresh, ('z', 'yh'), 0, 0, tiled=True)  16.3 us
    pallas_call x2, Pallas kernels, input_grad_of(): pl.pallas_call(functools.partial(input_grad_kernel, count), grid_spec=plt...  10.4 us
    all_to_all x1, starting transfers between devices, on_device(): parts = lax.all_to_all(blocks, 'z', 0, 0, tiled=True)  8.19 us
    pallas_call x1, Pallas kernels, own_partials(): pl.pallas_call(own_kernel, grid_spec=pltpu.PrefetchScalarGridSpec(num_sca...  4.14 us
    all_to_all x1, waiting for transfers between devices, on_device(): parts = lax.all_to_all(blocks, 'z', 0, 0, tiled=True)  3.8 us
    pallas_call x1, Pallas kernels, both_cores(): pl.pallas_call(both_cores_kernel, grid_spec=pltpu.PrefetchScalarGridSpec(...  3.65 us
  transfers between devices with their start and end apart: 26, of which 10 were waited for; matrix products, arithmetic and copies ran while one was open for 2% of the time, Pallas kernels for 13%

profile of v6, /device:TPU:1, one launch (start us, length us, event | category | flops | bytes accessed | tf_op | source)
XLA Modules:
  0.0 125.0 jit_solution(8584405494663018713)
XLA Ops:
  0.6 0.1 pad_add_fusion.2.place
  0.7 3.4 %core_swap.4 = (bf16[256,2048]{1,0:T(8,128)(2,1)}, bf16[256,2048]{1,0:T(8,128)(2,1)}) custom-call(s32[2]{0:T(128)S(1)} %pad_add_fusion.2.place, bf16[256,8192]{1,0:T(8,128)(2,1)} %tokens.1), custom_call_target="tpu_custom_call" | custom-call | tf_op jit(solution)/shard_map/core_swap/pallas_call | solution.py:71
  4.1 3.3 %collective-permute-start.1 = (bf16[256,2048]{1,0:T(8,128)(2,1)}, bf16[256,2048]{1,0:T(8,128)(2,1)S(1)}, u32[]{:S(2)}, u32[]{:S(2)}) collective-permute-start(bf16[256,2048]{1,0:T(8,128)(2,1)} %get-tuple-element.37), channel_id=1, source_target_pairs={{0,64},{64,0},{1,65},{65,1},{2,66},{66,2},{3,67},{67,3},{4,68},{68... | collective-permute-start | bytes 3145736 | tf_op jit(solution)/shard_map/core_swap/ppermute | solution.py:33
  7.5 0.1 collective-permute-start.2
  7.6 0.4 collective-permute-start.3
  8.0 0.0 collective-permute-start
  8.0 0.1 pad_add_fusion.1.place
  8.1 0.1 pad_add_fusion.place
  8.1 4.1 %core_swap.3.own = bf16[2,2048,512]{2,1,0:T(8,128)(2,1)S(1)} custom-call(s32[2]{0:T(128)S(1)} %pad_add_fusion.1.place, bf16[256,8192]{1,0:T(8,128)(2,1)} %tokens.1, bf16[256,512]{1,0:T(8,128)(2,1)S(1)} %copy-done), custom_call_target="tpu_custom_call" | custom-call | tf_op jit(solution)/shard_map/core_swap/pallas_call | solution.py:97
  12.3 0.0 copy-start.1
  12.3 0.0 collective-permute-done.far_order
  12.3 0.0 collective-permute-done.1.far
  12.3 0.0 collective-permute-done.2.near
  12.3 3.7 %core_swap.5 = (f32[4,8,16,512]{3,2,1,0:T(8,128)S(1)}, bf16[4,8,16,512]{3,2,1,0:T(8,128)(2,1)S(1)}, bf16[4,8,16,512]{3,2,1,0:T(8,128)(2,1)S(1)}, bf16[4,8,16,512...) custom-call(s32[2]{0:T(128)S(1)} %pad_add_fusion.place, ...), custom_call_target="tpu_custom_call" | custom-call | tf_op jit(solution)/shard_map/core_swap/pallas_call | solution.py:144
  16.0 0.9 collective-permute-start.4
  16.9 0.8 collective-permute-start.5
  17.7 2.3 %collective-permute-start.6 = (bf16[4,8,16,512]{3,2,1,0:T(8,128)(2,1)S(1)}, bf16[4,8,16,512]{3,2,1,0:T(8,128)(2,1)S(1)}, u32[]{:S(2)}, u32[]{:S(2)}) collective-permute-start(bf16[4,8,16,512]{3,2,1,0:T(8,128)(2,1)S(1)} %get-tuple-element.42), channel_id=1, source_target_pairs={{0,4},{128,132},{4,0},{132,128},{1,5},{129,133},{5,1},{133,129},{2... | collective-permute-start | bytes 1572872 | tf_op jit(solution)/shard_map/first_stage/ppermute | solution.py:33
  20.0 1.6 %collective-permute-start.7 = (bf16[4,8,16,512]{3,2,1,0:T(8,128)(2,1)S(1)}, bf16[4,8,16,512]{3,2,1,0:T(8,128)(2,1)S(1)}, u32[]{:S(2)}, u32[]{:S(2)}) collective-permute-start(bf16[4,8,16,512]{3,2,1,0:T(8,128)(2,1)S(1)} %get-tuple-element.43), channel_id=1, source_target_pairs={{0,132},{128,0},{4,128},{132,4},{1,133},{129,1},{5,129},{133,5},{2... | collective-permute-start | bytes 1572872 | tf_op jit(solution)/shard_map/first_stage/ppermute | solution.py:33
  21.6 1.5 %collective-permute-start.8 = (bf16[4,8,16,512]{3,2,1,0:T(8,128)(2,1)S(1)}, bf16[4,8,16,512]{3,2,1,0:T(8,128)(2,1)S(1)}, u32[]{:S(2)}, u32[]{:S(2)}) collective-permute-start(bf16[4,8,16,512]{3,2,1,0:T(8,128)(2,1)S(1)} %get-tuple-element.44), channel_id=1, source_target_pairs={{0,3},{1,0},{2,1},{3,2},{4,7},{5,4},{6,5},{7,6},{8,11},{9,8},{10,9... | collective-permute-start | bytes 1572872 | tf_op jit(solution)/shard_map/first_stage/ppermute | solution.py:33
  23.0 7.8 %collective-permute-done.4 = bf16[4,8,16,512]{3,2,1,0:T(8,128)(2,1)S(1)} collective-permute-done((bf16[4,8,16,512]{3,2,1,0:T(8,128)(2,1)S(1)}, bf16[4,8,16,512]{3,2,1,0:T(8,128)(2,1)S(1)}, u32[]{:S(2)}, u32[]{:S(2)}) %collective-permute-start.4) | collective-permute-done | bytes 524320 | tf_op jit(solution)/shard_map/first_stage/ppermute | solution.py:33
  30.8 0.8 collective-permute-start.9
  31.6 0.0 collective-permute-done.5
  31.6 1.6 %collective-permute-start.16 = (bf16[2048,512]{1,0:T(8,128)(2,1)S(1)}, bf16[2048,512]{1,0:T(8,128)(2,1)}, u32[]{:S(2)}, u32[]{:S(2)}) collective-permute-start(bf16[2048,512]{1,0:T(8,128)(2,1)S(1)} %copy-done.1), channel_id=1, source_target_pairs={{0,64},{64,0},{1,65},{65,1},{2,66},{66,2},{3,67},{67,3},{4,68},{68... | collective-permute-start | bytes 6291464 | tf_op jit(solution)/shard_map/weights/ppermute | solution.py:33
  33.1 9.4 %collective-permute-done.6 = bf16[4,8,16,512]{3,2,1,0:T(8,128)(2,1)S(1)} collective-permute-done((bf16[4,8,16,512]{3,2,1,0:T(8,128)(2,1)S(1)}, bf16[4,8,16,512]{3,2,1,0:T(8,128)(2,1)S(1)}, u32[]{:S(2)}, u32[]{:S(2)}) %collective-permute-start.6) | collective-permute-done | bytes 524320 | tf_op jit(solution)/shard_map/first_stage/ppermute | solution.py:33
  42.6 0.2 collective-permute-done.7
  42.7 0.0 collective-permute-done.8
  42.7 2.1 %collective-permute-done.9 = bf16[4,8,16,512]{3,2,1,0:T(8,128)(2,1)S(1)} collective-permute-done((bf16[4,8,16,512]{3,2,1,0:T(8,128)(2,1)S(1)}, bf16[4,8,16,512]{3,2,1,0:T(8,128)(2,1)S(1)}, u32[]{:S(2)}, u32[]{:S(2)}) %collective-permute-start.9) | collective-permute-done | bytes 524320 | tf_op jit(solution)/shard_map/first_stage/ppermute | solution.py:33
  44.9 0.3 fusion.9
  45.2 0.9 collective-permute-start.11
  46.0 1.7 %collective-permute-start.12 = (bf16[8,16,512]{2,1,0:T(8,128)(2,1)S(1)}, bf16[8,16,512]{2,1,0:T(8,128)(2,1)S(1)}, u32[]{:S(2)}, u32[]{:S(2)}) collective-permute-start(bf16[8,16,512]{2,1,0:T(8,128)(2,1)S(1)} %get-tuple-element.77), channel_id=1, source_target_pairs={{0,4},{128,132},{4,0},{132,128},{1,5},{129,133},{5,1},{133,129},{2... | collective-permute-start | bytes 393224 | tf_op jit(solution)/shard_map/second_stage/ppermute | solution.py:33
  47.7 1.1 collective-permute-start.13
  48.8 0.3 fusion.11
  49.1 2.0 %collective-permute-start.10 = (bf16[8,16,512]{2,1,0:T(8,128)(2,1)S(1)}, bf16[8,16,512]{2,1,0:T(8,128)(2,1)S(1)}, u32[]{:S(2)}, u32[]{:S(2)}) collective-permute-start(bf16[8,16,512]{2,1,0:T(8,128)(2,1)S(1)} %get-tuple-element.75), channel_id=1, source_target_pairs={{0,1},{1,2},{2,3},{3,0},{4,5},{5,6},{6,7},{7,4},{8,9},{9,10},{10,1... | collective-permute-start | bytes 393224 | tf_op jit(solution)/shard_map/second_stage/ppermute | solution.py:33
  51.1 0.1 collective-permute-done.11
  51.2 2.8 %collective-permute-start.14 = (bf16[8,16,512]{2,1,0:T(8,128)(2,1)S(1)}, bf16[8,16,512]{2,1,0:T(8,128)(2,1)S(1)}, u32[]{:S(2)}, u32[]{:S(2)}) collective-permute-start(bf16[8,16,512]{2,1,0:T(8,128)(2,1)S(1)} %get-tuple-element.74), channel_id=1, source_target_pairs={{0,3},{1,0},{2,1},{3,2},{4,7},{5,4},{6,5},{7,6},{8,11},{9,8},{10,9... | collective-permute-start | bytes 393224 | tf_op jit(solution)/shard_map/second_stage/ppermute | solution.py:33
  54.0 1.8 %collective-permute-start.15 = (bf16[8,16,512]{2,1,0:T(8,128)(2,1)S(1)}, bf16[8,16,512]{2,1,0:T(8,128)(2,1)S(1)}, u32[]{:S(2)}, u32[]{:S(2)}) collective-permute-start(bf16[8,16,512]{2,1,0:T(8,128)(2,1)S(1)} %get-tuple-element.73), channel_id=1, source_target_pairs={{0,2},{1,3},{2,0},{3,1},{4,6},{5,7},{6,4},{7,5},{8,10},{9,11},{10,... | collective-permute-start | bytes 393224 | tf_op jit(solution)/shard_map/second_stage/ppermute | solution.py:33
  55.8 1.5 %collective-permute-done.14 = bf16[8,16,512]{2,1,0:T(8,128)(2,1)S(1)} collective-permute-done((bf16[8,16,512]{2,1,0:T(8,128)(2,1)S(1)}, bf16[8,16,512]{2,1,0:T(8,128)(2,1)S(1)}, u32[]{:S(2)}, u32[]{:S(2)}) %collective-permute-start.14) | collective-permute-done | bytes 131104 | tf_op jit(solution)/shard_map/second_stage/ppermute | solution.py:33
  57.3 2.6 %collective-permute-done.15 = bf16[8,16,512]{2,1,0:T(8,128)(2,1)S(1)} collective-permute-done((bf16[8,16,512]{2,1,0:T(8,128)(2,1)S(1)}, bf16[8,16,512]{2,1,0:T(8,128)(2,1)S(1)}, u32[]{:S(2)}, u32[]{:S(2)}) %collective-permute-start.15) | collective-permute-done | bytes 131104 | tf_op jit(solution)/shard_map/second_stage/ppermute | solution.py:33
  59.9 0.3 fusion.2
  60.2 0.7 pad_maximum_fusion
  60.9 0.2 collective-permute-start.21
  61.1 8.2 %all-to-all-start = ((bf16[8,32,512]{2,1,0:T(8,128)(2,1)}), bf16[8,32,512]{2,1,0:T(8,128)(2,1)S(1)}, u32[]{:S(2)}, u32[]{:S(2)}) async-start(bf16[8,32,512]{2,1,0:T(8,128)(2,1)} %pad_maximum_fusion), calls=%async_computation | async-start | bytes 524288 | tf_op jit(solution)/shard_map/third_stage/all_to_all | solution.py:298
  69.3 0.1 pad_add_fusion.3.place
  69.4 0.0 collective-permute-done.16.rest_1_
  69.4 5.5 %input_grad.2.rest_2_ = bf16[256,8192]{1,0:T(8,128)(2,1)} custom-call(s32[2]{0:T(128)S(1)} %pad_add_fusion.3.place, bf16[256,512]{1,0:T(8,128)(2,1)S(1)} %copy-done, bf16[2048,512]{1,0:T(8,128)(2,1)S(1)} %copy-done.1, bf16[2048,512]{1,0:T(8,128)(2,1)} %collective-permute-done.16.rest_1_), custom_call_target="tpu_custom_call" | custom-call | tf_op jit(solution)/shard_map/input_grad/pallas_call | solution.py:176
  75.0 3.8 %all-to-all-done = bf16[8,32,512]{2,1,0:T(8,128)(2,1)S(1)} async-done(((bf16[8,32,512]{2,1,0:T(8,128)(2,1)}), bf16[8,32,512]{2,1,0:T(8,128)(2,1)S(1)}, u32[]{:S(2)}, u32[]{:S(2)}) %all-to-all-start) | async-done | bytes 262176 | tf_op jit(solution)/shard_map/third_stage/all_to_all | solution.py:298
  78.8 0.7 fusion.12
  79.5 16.3 %all_to_all.10.rest_0_ = bf16[16,32,512]{2,1,0:T(8,128)(2,1)S(1)} all-to-all(bf16[16,32,512]{2,1,0:T(8,128)(2,1)S(1)} %broadcast_in_dim.3), channel_id=1, replica_groups=mesh['yl'=2,'c'=2,'z'=8,'yh'=2,'x'=4] {'z','yh'}, dimensions={0} | all-to-all | bytes 1048576 | tf_op jit(solution)/shard_map/fresh_weights/all_to_all | solution.py:316
  95.8 0.0 collective-permute-done.21.rest_0_
  95.8 7.0 %collective-permute-start.22 = (bf16[2048,512]{1,0:T(8,128)(2,1)}, bf16[2048,512]{1,0:T(8,128)(2,1)S(1)}, u32[]{:S(2)}, u32[]{:S(2)}) collective-permute-start(bf16[2048,512]{1,0:T(8,128)(2,1)} %collective-permute-done.21.rest_0_), channel_id=1, source_target_pairs={{0,64},{64,0},{1,65},{65,1},{2,66},{66,2},{3,67},{67,3},{4,68},{68... | collective-permute-start | bytes 6291464 | tf_op jit(solution)/shard_map/input_grad/ppermute | solution.py:33
  102.9 1.6 %collective-permute-start.17 = (bf16[8,32,512]{2,1,0:T(8,128)(2,1)S(1)}, bf16[8,32,512]{2,1,0:T(8,128)(2,1)S(1)}, u32[]{:S(2)}, u32[]{:S(2)}) collective-permute-start(bf16[8,32,512]{2,1,0:T(8,128)(2,1)S(1)} %get-tuple-element.80), channel_id=1, source_target_pairs={{0,1},{1,2},{2,3},{3,0},{4,5},{5,6},{6,7},{7,4},{8,9},{9,10},{10,1... | collective-permute-start | bytes 786440 | tf_op jit(solution)/shard_map/fresh_weights/ppermute | solution.py:33
  104.5 1.1 collective-permute-start.18
  105.6 0.3 collective-permute-start.19
  106.0 2.3 %collective-permute-start.20 = (bf16[8,32,512]{2,1,0:T(8,128)(2,1)S(1)}, bf16[8,32,512]{2,1,0:T(8,128)(2,1)S(1)}, u32[]{:S(2)}, u32[]{:S(2)}) collective-permute-start(bf16[8,32,512]{2,1,0:T(8,128)(2,1)S(1)} %get-tuple-element.80), channel_id=1, source_target_pairs={{0,3},{1,0},{2,1},{3,2},{4,7},{5,4},{6,5},{7,6},{8,11},{9,8},{10,9... | collective-permute-start | bytes 786440 | tf_op jit(solution)/shard_map/fresh_weights/ppermute | solution.py:33
  108.3 3.8 %collective-permute-done.17.rest_1_ = bf16[8,32,512]{2,1,0:T(8,128)(2,1)S(1)} collective-permute-done((bf16[8,32,512]{2,1,0:T(8,128)(2,1)S(1)}, bf16[8,32,512]{2,1,0:T(8,128)(2,1)S(1)}, u32[]{:S(2)}, u32[]{:S(2)}) %collective-permute-start.17) | collective-permute-done | bytes 262176 | tf_op jit(solution)/shard_map/fresh_weights/ppermute | solution.py:33
  112.1 0.3 collective-permute-start.23
  112.4 2.3 %collective-permute-start.24 = (bf16[8,32,512]{2,1,0:T(8,128)(2,1)S(1)}, bf16[8,32,512]{2,1,0:T(8,128)(2,1)S(1)}, u32[]{:S(2)}, u32[]{:S(2)}) collective-permute-start(bf16[8,32,512]{2,1,0:T(8,128)(2,1)S(1)} %collective-permute-done.18.rest_2_), channel_id=1, source_target_pairs={{0,3},{1,0},{2,1},{3,2},{4,7},{5,4},{6,5},{7,6},{8,11},{9,8},{10,9... | collective-permute-start | bytes 786440 | tf_op jit(solution)/shard_map/fresh_weights/ppermute | solution.py:33
  114.8 0.1 pad_add_fusion.4.place
  114.9 0.0 collective-permute-done.22.rest_1_
  114.9 4.8 %input_grad.3 = bf16[256,8192]{1,0:T(8,128)(2,1)} custom-call(s32[2]{0:T(128)S(1)} %pad_add_fusion.4.place, bf16[256,512]{1,0:T(8,128)(2,1)S(1)} %copy-done, bf16[2048,512]{1,0:T(8,128)(2,1)} %collective-permute-done.21.rest_0_, bf16[2048,512]{1,0:T(8,128)(2,1)S(1)} %collective-permute-done.22.rest_1_, ...), custom_call_target="tpu_custom_call", output_to_operand_aliasing={{}: (4, {})} | custom-call | tf_op jit(solution)/shard_map/input_grad/pallas_call | solution.py:176
  119.7 2.1 %rows.2.rest_2_ = bf16[2048,512]{1,0:T(8,128)(2,1)} custom-call(s32[1]{0:T(128)} %bitcast.place, s32[1,64]{1,0:T(1,128)S(1)} %copy-done.2, bf16[16,32,512]{2,1,0:T(8,128)(2,1)S(1)} %all_to_all.10.rest_0_, bf16[8,32,512]{2,1,0:T(8,128)(2,1)S(1)} %collective-permute-done.17.rest_1_, bf16[8,32,512]{2,1,0:T(8,128)(2,1)S(1)} %collective-permute-done.18.rest_2_, ...), custom_call_target="tpu_custom_call" | custom-call | tf_op jit(solution)/shard_map/rows/pallas_call | solution.py:219
  121.8 1.5 %collective-permute-done.23.rest_0_ = bf16[8,32,512]{2,1,0:T(8,128)(2,1)S(1)} collective-permute-done((bf16[8,32,512]{2,1,0:T(8,128)(2,1)S(1)}, bf16[8,32,512]{2,1,0:T(8,128)(2,1)S(1)}, u32[]{:S(2)}, u32[]{:S(2)}) %collective-permute-start.23) | collective-permute-done | bytes 262176 | tf_op jit(solution)/shard_map/fresh_weights/ppermute | solution.py:33
  123.3 0.0 collective-permute-done.24.rest_1_
  123.3 1.5 %rows.3 = bf16[2048,512]{1,0:T(8,128)(2,1)} custom-call(s32[1]{0:T(128)} %bitcast.place, s32[1,64]{1,0:T(1,128)S(1)} %copy-done.2, bf16[8,32,512]{2,1,0:T(8,128)(2,1)S(1)} %collective-permute-done.23.rest_0_, bf16[8,32,512]{2,1,0:T(8,128)(2,1)S(1)} %collective-permute-done.24.rest_1_, bf16[2048,512]{1,0:T(8,128)(2,1)} %rows.2.rest_2_), custom_call_target="tpu_custom_call", output_to_operand_aliasing={{}: (4, {})} | custom-call | tf_op jit(solution)/shard_map/rows/pallas_call | solution.py:219
  (20 shorter events, 0.1 us)
Async XLA Ops:
  0.7 6.9 %copy-start = (bf16[256,512]{1,0:T(8,128)(2,1)S(1)}, bf16[256,512]{1,0:T(8,128)(2,1)}, u32[]{:S(2)}) copy-start(bf16[256,512]{1,0:T(8,128)(2,1)} %key.5) | copy-start | bytes 786436
  0.7 7.3 %copy-start.2 = (s32[1,64]{1,0:T(1,128)S(1)}, s32[1,64]{1,0:T(1,128)}, u32[]{:S(2)}) copy-start(s32[1,64]{1,0:T(1,128)} %order.3) | copy-start | bytes 772
  4.1 8.2 %collective-permute-start.1 = (bf16[256,2048]{1,0:T(8,128)(2,1)}, bf16[256,2048]{1,0:T(8,128)(2,1)S(1)}, u32[]{:S(2)}, u32[]{:S(2)}) collective-permute-start(bf16[256,2048]{1,0:T(8,128)(2,1)} %get-tuple-element.37), channel_id=1, source_target_pairs={{0,64},{64,0},{1,65},{65,1},{2,66},{66,2},{3,67},{67,3},{4,68},{68... | collective-permute-start | bytes 3145736 | tf_op jit(solution)/shard_map/core_swap/ppermute | solution.py:33
  7.5 4.9 %collective-permute-start.2 = (bf16[256,2048]{1,0:T(8,128)(2,1)}, bf16[256,2048]{1,0:T(8,128)(2,1)}, u32[]{:S(2)}, u32[]{:S(2)}) collective-permute-start(bf16[256,2048]{1,0:T(8,128)(2,1)} %get-tuple-element.38), channel_id=1, source_target_pairs={{0,64},{64,0},{1,65},{65,1},{2,66},{66,2},{3,67},{67,3},{4,68},{68... | collective-permute-start | bytes 3145736 | tf_op jit(solution)/shard_map/core_swap/ppermute | solution.py:33
  7.6 4.7 %collective-permute-start.3 = (bf16[256,512]{1,0:T(8,128)(2,1)S(1)}, bf16[256,512]{1,0:T(8,128)(2,1)}, u32[]{:S(2)}, u32[]{:S(2)}) collective-permute-start(bf16[256,512]{1,0:T(8,128)(2,1)S(1)} %copy-done), channel_id=1, source_target_pairs={{0,64},{64,0},{1,65},{65,1},{2,66},{66,2},{3,67},{67,3},{4,68},{68... | collective-permute-start | bytes 786440 | tf_op jit(solution)/shard_map/core_swap/ppermute | solution.py:33
  8.0 4.3 %collective-permute-start = (s32[1,64]{1,0:T(1,128)S(1)}, s32[1,64]{1,0:T(1,128)S(1)}, u32[]{:S(2)}, u32[]{:S(2)}) collective-permute-start(s32[1,64]{1,0:T(1,128)S(1)} %copy-done.2), channel_id=1, source_target_pairs={{0,128},{128,0},{1,129},{129,1},{2,130},{130,2},{3,131},{131,3},{4... | collective-permute-start | bytes 776 | tf_op jit(solution)/shard_map/core_swap/ppermute | solution.py:33
  12.3 19.3 %copy-start.1 = (bf16[2048,512]{1,0:T(8,128)(2,1)S(1)}, bf16[2048,512]{1,0:T(8,128)(2,1)}, u32[]{:S(2)}) copy-start(bf16[2048,512]{1,0:T(8,128)(2,1)} %rest_0_.1) | copy-start | bytes 6291460
  16.0 14.8 %collective-permute-start.4 = (bf16[4,8,16,512]{3,2,1,0:T(8,128)(2,1)S(1)}, bf16[4,8,16,512]{3,2,1,0:T(8,128)(2,1)S(1)}, u32[]{:S(2)}, u32[]{:S(2)}) collective-permute-start(bf16[4,8,16,512]{3,2,1,0:T(8,128)(2,1)S(1)} %get-tuple-element.40), channel_id=1, source_target_pairs={{0,1},{1,2},{2,3},{3,0},{4,5},{5,6},{6,7},{7,4},{8,9},{9,10},{10,1... | collective-permute-start | bytes 1572872 | tf_op jit(solution)/shard_map/first_stage/ppermute | solution.py:33
  16.9 14.7 %collective-permute-start.5 = (bf16[4,8,16,512]{3,2,1,0:T(8,128)(2,1)S(1)}, bf16[4,8,16,512]{3,2,1,0:T(8,128)(2,1)S(1)}, u32[]{:S(2)}, u32[]{:S(2)}) collective-permute-start(bf16[4,8,16,512]{3,2,1,0:T(8,128)(2,1)S(1)} %get-tuple-element.41), channel_id=1, source_target_pairs={{0,128},{128,4},{4,132},{132,0},{1,129},{129,5},{5,133},{133,1},{2... | collective-permute-start | bytes 1572872 | tf_op jit(solution)/shard_map/first_stage/ppermute | solution.py:33
  17.7 24.9 %collective-permute-start.6 = (bf16[4,8,16,512]{3,2,1,0:T(8,128)(2,1)S(1)}, bf16[4,8,16,512]{3,2,1,0:T(8,128)(2,1)S(1)}, u32[]{:S(2)}, u32[]{:S(2)}) collective-permute-start(bf16[4,8,16,512]{3,2,1,0:T(8,128)(2,1)S(1)} %get-tuple-element.42), channel_id=1, source_target_pairs={{0,4},{128,132},{4,0},{132,128},{1,5},{129,133},{5,1},{133,129},{2... | collective-permute-start | bytes 1572872 | tf_op jit(solution)/shard_map/first_stage/ppermute | solution.py:33
  20.0 22.8 %collective-permute-start.7 = (bf16[4,8,16,512]{3,2,1,0:T(8,128)(2,1)S(1)}, bf16[4,8,16,512]{3,2,1,0:T(8,128)(2,1)S(1)}, u32[]{:S(2)}, u32[]{:S(2)}) collective-permute-start(bf16[4,8,16,512]{3,2,1,0:T(8,128)(2,1)S(1)} %get-tuple-element.43), channel_id=1, source_target_pairs={{0,132},{128,0},{4,128},{132,4},{1,133},{129,1},{5,129},{133,5},{2... | collective-permute-start | bytes 1572872 | tf_op jit(solution)/shard_map/first_stage/ppermute | solution.py:33
  21.6 21.2 %collective-permute-start.8 = (bf16[4,8,16,512]{3,2,1,0:T(8,128)(2,1)S(1)}, bf16[4,8,16,512]{3,2,1,0:T(8,128)(2,1)S(1)}, u32[]{:S(2)}, u32[]{:S(2)}) collective-permute-start(bf16[4,8,16,512]{3,2,1,0:T(8,128)(2,1)S(1)} %get-tuple-element.44), channel_id=1, source_target_pairs={{0,3},{1,0},{2,1},{3,2},{4,7},{5,4},{6,5},{7,6},{8,11},{9,8},{10,9... | collective-permute-start | bytes 1572872 | tf_op jit(solution)/shard_map/first_stage/ppermute | solution.py:33
  30.8 14.1 %collective-permute-start.9 = (bf16[4,8,16,512]{3,2,1,0:T(8,128)(2,1)S(1)}, bf16[4,8,16,512]{3,2,1,0:T(8,128)(2,1)S(1)}, u32[]{:S(2)}, u32[]{:S(2)}) collective-permute-start(bf16[4,8,16,512]{3,2,1,0:T(8,128)(2,1)S(1)} %get-tuple-element.45), channel_id=1, source_target_pairs={{0,2},{1,3},{2,0},{3,1},{4,6},{5,7},{6,4},{7,5},{8,10},{9,11},{10,... | collective-permute-start | bytes 1572872 | tf_op jit(solution)/shard_map/first_stage/ppermute | solution.py:33
  31.6 37.8 %collective-permute-start.16 = (bf16[2048,512]{1,0:T(8,128)(2,1)S(1)}, bf16[2048,512]{1,0:T(8,128)(2,1)}, u32[]{:S(2)}, u32[]{:S(2)}) collective-permute-start(bf16[2048,512]{1,0:T(8,128)(2,1)S(1)} %copy-done.1), channel_id=1, source_target_pairs={{0,64},{64,0},{1,65},{65,1},{2,66},{66,2},{3,67},{67,3},{4,68},{68... | collective-permute-start | bytes 6291464 | tf_op jit(solution)/shard_map/weights/ppermute | solution.py:33
  45.2 6.0 %collective-permute-start.11 = (bf16[8,16,512]{2,1,0:T(8,128)(2,1)S(1)}, bf16[8,16,512]{2,1,0:T(8,128)(2,1)S(1)}, u32[]{:S(2)}, u32[]{:S(2)}) collective-permute-start(bf16[8,16,512]{2,1,0:T(8,128)(2,1)S(1)} %get-tuple-element.78), channel_id=1, source_target_pairs={{0,128},{128,4},{4,132},{132,0},{1,129},{129,5},{5,133},{133,1},{2... | collective-permute-start | bytes 393224 | tf_op jit(solution)/shard_map/second_stage/ppermute | solution.py:33
  46.0 7.9 %collective-permute-start.12 = (bf16[8,16,512]{2,1,0:T(8,128)(2,1)S(1)}, bf16[8,16,512]{2,1,0:T(8,128)(2,1)S(1)}, u32[]{:S(2)}, u32[]{:S(2)}) collective-permute-start(bf16[8,16,512]{2,1,0:T(8,128)(2,1)S(1)} %get-tuple-element.77), channel_id=1, source_target_pairs={{0,4},{128,132},{4,0},{132,128},{1,5},{129,133},{5,1},{133,129},{2... | collective-permute-start | bytes 393224 | tf_op jit(solution)/shard_map/second_stage/ppermute | solution.py:33
  47.7 8.1 %collective-permute-start.13 = (bf16[8,16,512]{2,1,0:T(8,128)(2,1)S(1)}, bf16[8,16,512]{2,1,0:T(8,128)(2,1)S(1)}, u32[]{:S(2)}, u32[]{:S(2)}) collective-permute-start(bf16[8,16,512]{2,1,0:T(8,128)(2,1)S(1)} %get-tuple-element.76), channel_id=1, source_target_pairs={{0,132},{128,0},{4,128},{132,4},{1,133},{129,1},{5,129},{133,5},{2... | collective-permute-start | bytes 393224 | tf_op jit(solution)/shard_map/second_stage/ppermute | solution.py:33
  49.1 6.7 %collective-permute-start.10 = (bf16[8,16,512]{2,1,0:T(8,128)(2,1)S(1)}, bf16[8,16,512]{2,1,0:T(8,128)(2,1)S(1)}, u32[]{:S(2)}, u32[]{:S(2)}) collective-permute-start(bf16[8,16,512]{2,1,0:T(8,128)(2,1)S(1)} %get-tuple-element.75), channel_id=1, source_target_pairs={{0,1},{1,2},{2,3},{3,0},{4,5},{5,6},{6,7},{7,4},{8,9},{9,10},{10,1... | collective-permute-start | bytes 393224 | tf_op jit(solution)/shard_map/second_stage/ppermute | solution.py:33
  51.2 6.1 %collective-permute-start.14 = (bf16[8,16,512]{2,1,0:T(8,128)(2,1)S(1)}, bf16[8,16,512]{2,1,0:T(8,128)(2,1)S(1)}, u32[]{:S(2)}, u32[]{:S(2)}) collective-permute-start(bf16[8,16,512]{2,1,0:T(8,128)(2,1)S(1)} %get-tuple-element.74), channel_id=1, source_target_pairs={{0,3},{1,0},{2,1},{3,2},{4,7},{5,4},{6,5},{7,6},{8,11},{9,8},{10,9... | collective-permute-start | bytes 393224 | tf_op jit(solution)/shard_map/second_stage/ppermute | solution.py:33
  54.0 5.9 %collective-permute-start.15 = (bf16[8,16,512]{2,1,0:T(8,128)(2,1)S(1)}, bf16[8,16,512]{2,1,0:T(8,128)(2,1)S(1)}, u32[]{:S(2)}, u32[]{:S(2)}) collective-permute-start(bf16[8,16,512]{2,1,0:T(8,128)(2,1)S(1)} %get-tuple-element.73), channel_id=1, source_target_pairs={{0,2},{1,3},{2,0},{3,1},{4,6},{5,7},{6,4},{7,5},{8,10},{9,11},{10,... | collective-permute-start | bytes 393224 | tf_op jit(solution)/shard_map/second_stage/ppermute | solution.py:33
  60.9 34.9 %collective-permute-start.21 = (bf16[2048,512]{1,0:T(8,128)(2,1)S(1)}, bf16[2048,512]{1,0:T(8,128)(2,1)}, u32[]{:S(2)}, u32[]{:S(2)}) collective-permute-start(bf16[2048,512]{1,0:T(8,128)(2,1)S(1)} %copy-done.1), channel_id=1, source_target_pairs={{0,128},{64,196},{128,4},{192,64},{4,132},{68,192},{132,0},{196,68... | collective-permute-start | bytes 6291464 | tf_op jit(solution)/shard_map/weights/ppermute | solution.py:42
  61.1 17.6 %all-to-all-start = ((bf16[8,32,512]{2,1,0:T(8,128)(2,1)}), bf16[8,32,512]{2,1,0:T(8,128)(2,1)S(1)}, u32[]{:S(2)}, u32[]{:S(2)}) async-start(bf16[8,32,512]{2,1,0:T(8,128)(2,1)} %pad_maximum_fusion), calls=%async_computation | async-start | bytes 524288 | tf_op jit(solution)/shard_map/third_stage/all_to_all | solution.py:298
  69.4 9.4 %copy-start.3 = (f32[32,512]{1,0:T(8,128)S(1)}, f32[32,512]{1,0:T(8,128)}, u32[]{:S(2)}) copy-start(f32[32,512]{1,0:T(8,128)} %param.10) | copy-start | bytes 196612
  69.4 9.4 %copy-start.4 = (f32[32,512]{1,0:T(8,128)S(1)}, f32[32,512]{1,0:T(8,128)}, u32[]{:S(2)}) copy-start(f32[32,512]{1,0:T(8,128)} %param.11) | copy-start | bytes 196612
  69.4 9.4 %copy-start.5 = (f32[32,512]{1,0:T(8,128)S(1)}, f32[32,512]{1,0:T(8,128)}, u32[]{:S(2)}) copy-start(f32[32,512]{1,0:T(8,128)} %param.12) | copy-start | bytes 196612
  95.8 19.0 %collective-permute-start.22 = (bf16[2048,512]{1,0:T(8,128)(2,1)}, bf16[2048,512]{1,0:T(8,128)(2,1)S(1)}, u32[]{:S(2)}, u32[]{:S(2)}) collective-permute-start(bf16[2048,512]{1,0:T(8,128)(2,1)} %collective-permute-done.21.rest_0_), channel_id=1, source_target_pairs={{0,64},{64,0},{1,65},{65,1},{2,66},{66,2},{3,67},{67,3},{4,68},{68... | collective-permute-start | bytes 6291464 | tf_op jit(solution)/shard_map/input_grad/ppermute | solution.py:33
  102.9 9.2 %collective-permute-start.17 = (bf16[8,32,512]{2,1,0:T(8,128)(2,1)S(1)}, bf16[8,32,512]{2,1,0:T(8,128)(2,1)S(1)}, u32[]{:S(2)}, u32[]{:S(2)}) collective-permute-start(bf16[8,32,512]{2,1,0:T(8,128)(2,1)S(1)} %get-tuple-element.80), channel_id=1, source_target_pairs={{0,1},{1,2},{2,3},{3,0},{4,5},{5,6},{6,7},{7,4},{8,9},{9,10},{10,1... | collective-permute-start | bytes 786440 | tf_op jit(solution)/shard_map/fresh_weights/ppermute | solution.py:33
  104.5 7.9 %collective-permute-start.18 = (bf16[8,32,512]{2,1,0:T(8,128)(2,1)S(1)}, bf16[8,32,512]{2,1,0:T(8,128)(2,1)S(1)}, u32[]{:S(2)}, u32[]{:S(2)}) collective-permute-start(bf16[8,32,512]{2,1,0:T(8,128)(2,1)S(1)} %get-tuple-element.79), channel_id=1, source_target_pairs={{0,3},{1,0},{2,1},{3,2},{4,7},{5,4},{6,5},{7,6},{8,11},{9,8},{10,9... | collective-permute-start | bytes 786440 | tf_op jit(solution)/shard_map/fresh_weights/ppermute | solution.py:33
  105.6 14.1 %collective-permute-start.19 = (bf16[8,32,512]{2,1,0:T(8,128)(2,1)S(1)}, bf16[8,32,512]{2,1,0:T(8,128)(2,1)S(1)}, u32[]{:S(2)}, u32[]{:S(2)}) collective-permute-start(bf16[8,32,512]{2,1,0:T(8,128)(2,1)S(1)} %get-tuple-element.79), channel_id=1, source_target_pairs={{0,1},{1,2},{2,3},{3,0},{4,5},{5,6},{6,7},{7,4},{8,9},{9,10},{10,1... | collective-permute-start | bytes 786440 | tf_op jit(solution)/shard_map/fresh_weights/ppermute | solution.py:33
  106.0 13.7 %collective-permute-start.20 = (bf16[8,32,512]{2,1,0:T(8,128)(2,1)S(1)}, bf16[8,32,512]{2,1,0:T(8,128)(2,1)S(1)}, u32[]{:S(2)}, u32[]{:S(2)}) collective-permute-start(bf16[8,32,512]{2,1,0:T(8,128)(2,1)S(1)} %get-tuple-element.80), channel_id=1, source_target_pairs={{0,3},{1,0},{2,1},{3,2},{4,7},{5,4},{6,5},{7,6},{8,11},{9,8},{10,9... | collective-permute-start | bytes 786440 | tf_op jit(solution)/shard_map/fresh_weights/ppermute | solution.py:33
  112.1 11.2 %collective-permute-start.23 = (bf16[8,32,512]{2,1,0:T(8,128)(2,1)S(1)}, bf16[8,32,512]{2,1,0:T(8,128)(2,1)S(1)}, u32[]{:S(2)}, u32[]{:S(2)}) collective-permute-start(bf16[8,32,512]{2,1,0:T(8,128)(2,1)S(1)} %collective-permute-done.17.rest_1_), channel_id=1, source_target_pairs={{0,1},{1,2},{2,3},{3,0},{4,5},{5,6},{6,7},{7,4},{8,9},{9,10},{10,1... | collective-permute-start | bytes 786440 | tf_op jit(solution)/shard_map/fresh_weights/ppermute | solution.py:33
  112.4 10.9 %collective-permute-start.24 = (bf16[8,32,512]{2,1,0:T(8,128)(2,1)S(1)}, bf16[8,32,512]{2,1,0:T(8,128)(2,1)S(1)}, u32[]{:S(2)}, u32[]{:S(2)}) collective-permute-start(bf16[8,32,512]{2,1,0:T(8,128)(2,1)S(1)} %collective-permute-done.18.rest_2_), channel_id=1, source_target_pairs={{0,3},{1,0},{2,1},{3,2},{4,7},{5,4},{6,5},{7,6},{8,11},{9,8},{10,9... | collective-permute-start | bytes 786440 | tf_op jit(solution)/shard_map/fresh_weights/ppermute | solution.py:33

commit v7 on v6

--- a/solution.py
+++ b/solution.py
@@ -54,28 +54,46 @@
     return pltpu.CompilerParams(vmem_limit_bytes=mib * MIB)
 
 
-def columns_kernel(place, tokens, far, near, sems):
-    copies = []
+def columns_kernel(place, tokens, far, near, held, sems):
+    rows, pieces = held.shape[2], sems.shape[2]
+    cut = held.shape[1] // pieces
+    inward, outward = [], []
     for n, out in enumerate((far, near)):
-        rows = out.shape[1]
         start = pl.multiple_of(place[n] * rows, rows)
-        copies.append(pltpu.make_async_copy(tokens.at[:, pl.ds(start, rows)], out, sems.at[n]))
-    for copy in copies:
+        for i in range(pieces):
+            here = pl.ds(i * cut, cut)
+            inward.append(
+                pltpu.make_async_copy(
+                    tokens.at[here, pl.ds(start, rows)], held.at[n, here, :], sems.at[0, n, i]
+                )
+            )
+            outward.append(
+                pltpu.make_async_copy(held.at[n, here, :], out.at[here, :], sems.at[1, n, i])
+            )
+    for copy in inward:
         copy.start()
-    for copy in copies:
+    for copy, after in zip(inward, outward):
         copy.wait()
+        after.start()
+    for copy in outward:
+        copy.wait()
 
 
 def columns_of(place, tokens, rows):
-    shape = jax.ShapeDtypeStruct((tokens.shape[0], rows), tokens.dtype)
+    count = tokens.shape[0]
+    pieces = 4 if count % 64 == 0 else 1
+    shape = jax.ShapeDtypeStruct((count, rows), tokens.dtype)
     return pl.pallas_call(
         columns_kernel,
         grid_spec=pltpu.PrefetchScalarGridSpec(
             num_scalar_prefetch=1,
             grid=(1,),
             in_specs=[pl.BlockSpec(memory_space=pl.ANY)],
-            out_specs=[vmem(), vmem()],
-            scratch_shapes=[pltpu.SemaphoreType.DMA((2,))],
+            out_specs=[pl.BlockSpec(memory_space=pl.ANY)] * 2,
+            scratch_shapes=[
+                pltpu.VMEM((2, count, rows), tokens.dtype),
+                pltpu.SemaphoreType.DMA((2, 2, pieces)),
+            ],
         ),
         out_shape=[shape, shape],
         compiler_params=params(6),
@@ -286,13 +304,11 @@
         blocks = jnp.concatenate([first_half, second_half], axis=1).astype(jnp.bfloat16)
 
     with jax.named_scope("weights"):
-        core = send(key_weight, "c", 1)
         held, blocks = lax.optimization_barrier((key_weight, blocks))
+        core = send(held, "c", 1)
         other = cross(held)
-
-    with jax.named_scope("input_grad"):
         place = jnp.stack([here + c, here + 1 - c]).astype(jnp.int32)
-        input_grad = input_grad_of(place, key_cotangent, [key_weight, core], depth)
+        input_grad = input_grad_of(place, key_cotangent, [held, core], depth)
 
     with jax.named_scope("third_stage"):
         parts = lax.all_to_all(blocks, "z", 0, 0, tiled=True)

time: 126 us -> 130 us (1.032)
  waiting for transfers between devices: 32.8 us -> 55 us
  blocking collectives: 16.3 us -> 0 us
  Pallas kernels: 25.1 us -> 23.4 us
    all_to_all x0 -> x1, waiting for transfers between devices: none -> 17.5 us  [on_device(): plane = lax.all_to_all(fresh, ('z', 'yh'), 0, 0, tiled=True)]
    all_to_all x1 -> x0, blocking collectives: 16.3 us -> none  [on_device(): plane = lax.all_to_all(fresh, ('z', 'yh'), 0, 0, tiled=True)]
    ppermute x24, starting transfers between devices: 38.6 us -> 34.6 us  [send(): lax.ppermute(value, ('yl', 'yh') if axis == 'y' else axis, shift(axis, st...]
    all_to_all x0 -> x1, starting transfers between devices: none -> 3.57 us  [on_device(): plane = lax.all_to_all(fresh, ('z', 'yh'), 0, 0, tiled=True)]
    all_to_all x1, waiting for transfers between devices: 3.8 us -> 6.64 us  [on_device(): parts = lax.all_to_all(blocks, 'z', 0, 0, tiled=True)]
    ppermute x24, waiting for transfers between devices: 29 us -> 30.8 us  [send(): lax.ppermute(value, ('yl', 'yh') if axis == 'y' else axis, shift(axis, st...]
  transfers between devices with their start and end apart: 26 -> 27, of which waited for: 10 -> 12; matrix products, arithmetic and copies ran while one was open for 2% -> 2% of each run, Pallas kernels for 13% -> 13%
where the time goes in v7:
time: 130 us; the launch traced here: 129 us
  waiting for transfers between devices  55 us (42%)
  starting transfers between devices  46.4 us (36%)
  Pallas kernels  23.4 us (18%)
  other arithmetic  2.72 us (2%)
    ppermute x24, starting transfers between devices, send(): lax.ppermute(value, ('yl', 'yh') if axis == 'y' else axis, shift(axis, st...  34.6 us
    ppermute x24, waiting for transfers between devices, send(): lax.ppermute(value, ('yl', 'yh') if axis == 'y' else axis, shift(axis, st...  30.8 us
    all_to_all x1, waiting for transfers between devices, on_device(): plane = lax.all_to_all(fresh, ('z', 'yh'), 0, 0, tiled=True)  17.5 us
    pallas_call x2, Pallas kernels, input_grad_of(): pl.pallas_call(functools.partial(input_grad_kernel, count), grid_spec=plt...  10.4 us
    all_to_all x1, starting transfers between devices, on_device(): parts = lax.all_to_all(blocks, 'z', 0, 0, tiled=True)  7.7 us
    all_to_all x1, waiting for transfers between devices, on_device(): parts = lax.all_to_all(blocks, 'z', 0, 0, tiled=True)  6.64 us
    pallas_call x1, Pallas kernels, own_partials(): pl.pallas_call(own_kernel, grid_spec=pltpu.PrefetchScalarGridSpec(num_sca...  4.14 us
    all_to_all x1, starting transfers between devices, on_device(): plane = lax.all_to_all(fresh, ('z', 'yh'), 0, 0, tiled=True)  3.57 us
  transfers between devices with their start and end apart: 27, of which 12 were waited for; matrix products, arithmetic and copies ran while one was open for 2% of the time, Pallas kernels for 13%

profile of v7, /device:TPU:1, one launch (start us, length us, event | category | flops | bytes accessed | tf_op | source)
XLA Modules:
  0.0 129.3 jit_solution(6382827500457874669)
XLA Ops:
  0.6 0.1 pad_add_fusion.2.place
  0.7 2.9 %core_swap.4 = (bf16[256,2048]{1,0:T(8,128)(2,1)}, bf16[256,2048]{1,0:T(8,128)(2,1)}) custom-call(s32[2]{0:T(128)S(1)} %pad_add_fusion.2.place, bf16[256,8192]{1,0:T(8,128)(2,1)} %tokens.1), custom_call_target="tpu_custom_call" | custom-call | tf_op jit(solution)/shard_map/core_swap/pallas_call | solution.py:86
  3.7 3.3 %collective-permute-start.1 = (bf16[256,2048]{1,0:T(8,128)(2,1)}, bf16[256,2048]{1,0:T(8,128)(2,1)S(1)}, u32[]{:S(2)}, u32[]{:S(2)}) collective-permute-start(bf16[256,2048]{1,0:T(8,128)(2,1)} %get-tuple-element.37), channel_id=1, source_target_pairs={{0,64},{64,0},{1,65},{65,1},{2,66},{66,2},{3,67},{67,3},{4,68},{68... | collective-permute-start | bytes 3145736 | tf_op jit(solution)/shard_map/core_swap/ppermute | solution.py:33
  7.0 0.1 collective-permute-start.2
  7.1 0.4 collective-permute-start.3
  7.5 0.0 collective-permute-start
  7.5 0.1 pad_add_fusion.1.place
  7.6 0.1 pad_add_fusion.place
  7.7 4.1 %core_swap.3.own = bf16[2,2048,512]{2,1,0:T(8,128)(2,1)S(1)} custom-call(s32[2]{0:T(128)S(1)} %pad_add_fusion.1.place, bf16[256,8192]{1,0:T(8,128)(2,1)} %tokens.1, bf16[256,512]{1,0:T(8,128)(2,1)S(1)} %copy-done), custom_call_target="tpu_custom_call" | custom-call | tf_op jit(solution)/shard_map/core_swap/pallas_call | solution.py:115
  11.8 0.0 collective-permute-done.far_order
  11.8 0.0 collective-permute-done.1.far
  11.8 0.0 collective-permute-done.2.near
  11.9 2.4 %core_swap.5 = (f32[4,8,16,512]{3,2,1,0:T(8,128)S(1)}, bf16[4,8,16,512]{3,2,1,0:T(8,128)(2,1)S(1)}, bf16[4,8,16,512]{3,2,1,0:T(8,128)(2,1)S(1)}, bf16[4,8,16,512...) custom-call(s32[2]{0:T(128)S(1)} %pad_add_fusion.place, ...), custom_call_target="tpu_custom_call" | custom-call | tf_op jit(solution)/shard_map/core_swap/pallas_call | solution.py:162
  14.2 0.9 collective-permute-start.4
  15.1 0.8 collective-permute-start.5
  15.9 2.3 %collective-permute-start.6 = (bf16[4,8,16,512]{3,2,1,0:T(8,128)(2,1)S(1)}, bf16[4,8,16,512]{3,2,1,0:T(8,128)(2,1)S(1)}, u32[]{:S(2)}, u32[]{:S(2)}) collective-permute-start(bf16[4,8,16,512]{3,2,1,0:T(8,128)(2,1)S(1)} %get-tuple-element.42), channel_id=1, source_target_pairs={{0,4},{128,132},{4,0},{132,128},{1,5},{129,133},{5,1},{133,129},{2... | collective-permute-start | bytes 1572872 | tf_op jit(solution)/shard_map/first_stage/ppermute | solution.py:33
  18.2 1.6 %collective-permute-start.7 = (bf16[4,8,16,512]{3,2,1,0:T(8,128)(2,1)S(1)}, bf16[4,8,16,512]{3,2,1,0:T(8,128)(2,1)S(1)}, u32[]{:S(2)}, u32[]{:S(2)}) collective-permute-start(bf16[4,8,16,512]{3,2,1,0:T(8,128)(2,1)S(1)} %get-tuple-element.43), channel_id=1, source_target_pairs={{0,132},{128,0},{4,128},{132,4},{1,133},{129,1},{5,129},{133,5},{2... | collective-permute-start | bytes 1572872 | tf_op jit(solution)/shard_map/first_stage/ppermute | solution.py:33
  19.8 1.5 %collective-permute-start.8 = (bf16[4,8,16,512]{3,2,1,0:T(8,128)(2,1)S(1)}, bf16[4,8,16,512]{3,2,1,0:T(8,128)(2,1)S(1)}, u32[]{:S(2)}, u32[]{:S(2)}) collective-permute-start(bf16[4,8,16,512]{3,2,1,0:T(8,128)(2,1)S(1)} %get-tuple-element.44), channel_id=1, source_target_pairs={{0,3},{1,0},{2,1},{3,2},{4,7},{5,4},{6,5},{7,6},{8,11},{9,8},{10,9... | collective-permute-start | bytes 1572872 | tf_op jit(solution)/shard_map/first_stage/ppermute | solution.py:33
  21.3 7.7 %collective-permute-done.4 = bf16[4,8,16,512]{3,2,1,0:T(8,128)(2,1)S(1)} collective-permute-done((bf16[4,8,16,512]{3,2,1,0:T(8,128)(2,1)S(1)}, bf16[4,8,16,512]{3,2,1,0:T(8,128)(2,1)S(1)}, u32[]{:S(2)}, u32[]{:S(2)}) %collective-permute-start.4) | collective-permute-done | bytes 524320 | tf_op jit(solution)/shard_map/first_stage/ppermute | solution.py:33
  28.9 0.9 collective-permute-start.9
  29.8 11.0 %collective-permute-done.6 = bf16[4,8,16,512]{3,2,1,0:T(8,128)(2,1)S(1)} collective-permute-done((bf16[4,8,16,512]{3,2,1,0:T(8,128)(2,1)S(1)}, bf16[4,8,16,512]{3,2,1,0:T(8,128)(2,1)S(1)}, u32[]{:S(2)}, u32[]{:S(2)}) %collective-permute-start.6) | collective-permute-done | bytes 524320 | tf_op jit(solution)/shard_map/first_stage/ppermute | solution.py:33
  40.8 0.2 collective-permute-done.7
  41.0 1.9 %collective-permute-done.9 = bf16[4,8,16,512]{3,2,1,0:T(8,128)(2,1)S(1)} collective-permute-done((bf16[4,8,16,512]{3,2,1,0:T(8,128)(2,1)S(1)}, bf16[4,8,16,512]{3,2,1,0:T(8,128)(2,1)S(1)}, u32[]{:S(2)}, u32[]{:S(2)}) %collective-permute-start.9) | collective-permute-done | bytes 524320 | tf_op jit(solution)/shard_map/first_stage/ppermute | solution.py:33
  42.9 0.3 fusion.9
  43.2 1.1 collective-permute-start.11
  44.3 1.6 %collective-permute-start.12 = (bf16[8,16,512]{2,1,0:T(8,128)(2,1)S(1)}, bf16[8,16,512]{2,1,0:T(8,128)(2,1)S(1)}, u32[]{:S(2)}, u32[]{:S(2)}) collective-permute-start(bf16[8,16,512]{2,1,0:T(8,128)(2,1)S(1)} %get-tuple-element.77), channel_id=1, source_target_pairs={{0,4},{128,132},{4,0},{132,128},{1,5},{129,133},{5,1},{133,129},{2... | collective-permute-start | bytes 393224 | tf_op jit(solution)/shard_map/second_stage/ppermute | solution.py:33
  45.9 1.1 collective-permute-start.13
  47.1 0.3 fusion.11
  47.3 1.8 %collective-permute-start.10 = (bf16[8,16,512]{2,1,0:T(8,128)(2,1)S(1)}, bf16[8,16,512]{2,1,0:T(8,128)(2,1)S(1)}, u32[]{:S(2)}, u32[]{:S(2)}) collective-permute-start(bf16[8,16,512]{2,1,0:T(8,128)(2,1)S(1)} %get-tuple-element.75), channel_id=1, source_target_pairs={{0,1},{1,2},{2,3},{3,0},{4,5},{5,6},{6,7},{7,4},{8,9},{9,10},{10,1... | collective-permute-start | bytes 393224 | tf_op jit(solution)/shard_map/second_stage/ppermute | solution.py:33
  49.1 1.0 collective-permute-start.14
  50.1 0.0 collective-permute-done.11
  50.1 1.1 collective-permute-start.15
  51.2 1.6 %collective-permute-done.10 = bf16[8,16,512]{2,1,0:T(8,128)(2,1)S(1)} collective-permute-done((bf16[8,16,512]{2,1,0:T(8,128)(2,1)S(1)}, bf16[8,16,512]{2,1,0:T(8,128)(2,1)S(1)}, u32[]{:S(2)}, u32[]{:S(2)}) %collective-permute-start.10) | collective-permute-done | bytes 131104 | tf_op jit(solution)/shard_map/second_stage/ppermute | solution.py:33
  52.8 0.5 collective-permute-done.14
  53.2 2.5 %collective-permute-done.15 = bf16[8,16,512]{2,1,0:T(8,128)(2,1)S(1)} collective-permute-done((bf16[8,16,512]{2,1,0:T(8,128)(2,1)S(1)}, bf16[8,16,512]{2,1,0:T(8,128)(2,1)S(1)}, u32[]{:S(2)}, u32[]{:S(2)}) %collective-permute-start.15) | collective-permute-done | bytes 131104 | tf_op jit(solution)/shard_map/second_stage/ppermute | solution.py:33
  55.8 0.3 fusion.2
  56.1 0.7 pad_maximum_fusion
  56.8 4.3 %collective-permute-start.16 = (bf16[2048,512]{1,0:T(8,128)(2,1)S(1)}, bf16[2048,512]{1,0:T(8,128)(2,1)}, u32[]{:S(2)}, u32[]{:S(2)}) collective-permute-start(bf16[2048,512]{1,0:T(8,128)(2,1)S(1)} %copy-done.1), channel_id=1, source_target_pairs={{0,64},{64,0},{1,65},{65,1},{2,66},{66,2},{3,67},{67,3},{4,68},{68... | collective-permute-start | bytes 6291464 | tf_op jit(solution)/shard_map/weights/ppermute | solution.py:33
  61.1 0.5 collective-permute-start.21
  61.6 7.7 %all-to-all-start = ((bf16[8,32,512]{2,1,0:T(8,128)(2,1)}), bf16[8,32,512]{2,1,0:T(8,128)(2,1)S(1)}, u32[]{:S(2)}, u32[]{:S(2)}) async-start(bf16[8,32,512]{2,1,0:T(8,128)(2,1)} %pad_maximum_fusion), calls=%async_computation | async-start | bytes 524288 | tf_op jit(solution)/shard_map/third_stage/all_to_all | solution.py:314
  69.3 0.1 pad_add_fusion.3.place
  69.4 5.5 %weights.1.rest_2_ = bf16[256,8192]{1,0:T(8,128)(2,1)} custom-call(s32[2]{0:T(128)S(1)} %pad_add_fusion.3.place, bf16[256,512]{1,0:T(8,128)(2,1)S(1)} %copy-done, bf16[2048,512]{1,0:T(8,128)(2,1)S(1)} %copy-done.1, bf16[2048,512]{1,0:T(8,128)(2,1)} %collective-permute-done.16.rest_1_), custom_call_target="tpu_custom_call" | custom-call | tf_op jit(solution)/shard_map/weights/pallas_call | solution.py:194
  75.0 6.6 %all-to-all-done = bf16[8,32,512]{2,1,0:T(8,128)(2,1)S(1)} async-done(((bf16[8,32,512]{2,1,0:T(8,128)(2,1)}), bf16[8,32,512]{2,1,0:T(8,128)(2,1)S(1)}, u32[]{:S(2)}, u32[]{:S(2)}) %all-to-all-start) | async-done | bytes 262176 | tf_op jit(solution)/shard_map/third_stage/all_to_all | solution.py:314
  81.6 0.7 fusion.12
  82.3 0.8 broadcast_in_dim.3
  83.2 3.6 %all-to-all-start.1 = ((bf16[16,32,512]{2,1,0:T(8,128)(2,1)}), bf16[16,32,512]{2,1,0:T(8,128)(2,1)S(1)}, u32[]{:S(2)}, u32[]{:S(2)}) async-start(bf16[16,32,512]{2,1,0:T(8,128)(2,1)} %broadcast_in_dim.3), calls=%async_computation.1 | async-start | bytes 1048576 | tf_op jit(solution)/shard_map/fresh_weights/all_to_all | solution.py:332
  86.8 0.0 collective-permute-done.21.rest_0_
  86.8 17.5 %all-to-all-done.1.rest_0_ = bf16[16,32,512]{2,1,0:T(8,128)(2,1)S(1)} async-done(((bf16[16,32,512]{2,1,0:T(8,128)(2,1)}), bf16[16,32,512]{2,1,0:T(8,128)(2,1)S(1)}, u32[]{:S(2)}, u32[]{:S(2)}) %all-to-all-start.1) | async-done | bytes 524320 | tf_op jit(solution)/shard_map/fresh_weights/all_to_all | solution.py:332
  104.3 2.8 %collective-permute-start.22 = (bf16[2048,512]{1,0:T(8,128)(2,1)}, bf16[2048,512]{1,0:T(8,128)(2,1)S(1)}, u32[]{:S(2)}, u32[]{:S(2)}) collective-permute-start(bf16[2048,512]{1,0:T(8,128)(2,1)} %collective-permute-done.21.rest_0_), channel_id=1, source_target_pairs={{0,64},{64,0},{1,65},{65,1},{2,66},{66,2},{3,67},{67,3},{4,68},{68... | collective-permute-start | bytes 6291464 | tf_op jit(solution)/shard_map/input_grad/ppermute | solution.py:33
  107.2 1.7 %collective-permute-start.17 = (bf16[8,32,512]{2,1,0:T(8,128)(2,1)S(1)}, bf16[8,32,512]{2,1,0:T(8,128)(2,1)S(1)}, u32[]{:S(2)}, u32[]{:S(2)}) collective-permute-start(bf16[8,32,512]{2,1,0:T(8,128)(2,1)S(1)} %get-tuple-element.80), channel_id=1, source_target_pairs={{0,1},{1,2},{2,3},{3,0},{4,5},{5,6},{6,7},{7,4},{8,9},{9,10},{10,1... | collective-permute-start | bytes 786440 | tf_op jit(solution)/shard_map/fresh_weights/ppermute | solution.py:33
  108.9 1.0 collective-permute-start.18
  109.9 0.4 collective-permute-start.19
  110.3 2.2 %collective-permute-start.20 = (bf16[8,32,512]{2,1,0:T(8,128)(2,1)S(1)}, bf16[8,32,512]{2,1,0:T(8,128)(2,1)S(1)}, u32[]{:S(2)}, u32[]{:S(2)}) collective-permute-start(bf16[8,32,512]{2,1,0:T(8,128)(2,1)S(1)} %get-tuple-element.80), channel_id=1, source_target_pairs={{0,3},{1,0},{2,1},{3,2},{4,7},{5,4},{6,5},{7,6},{8,11},{9,8},{10,9... | collective-permute-start | bytes 786440 | tf_op jit(solution)/shard_map/fresh_weights/ppermute | solution.py:33
  112.6 3.8 %collective-permute-done.17.rest_1_ = bf16[8,32,512]{2,1,0:T(8,128)(2,1)S(1)} collective-permute-done((bf16[8,32,512]{2,1,0:T(8,128)(2,1)S(1)}, bf16[8,32,512]{2,1,0:T(8,128)(2,1)S(1)}, u32[]{:S(2)}, u32[]{:S(2)}) %collective-permute-start.17) | collective-permute-done | bytes 262176 | tf_op jit(solution)/shard_map/fresh_weights/ppermute | solution.py:33
  116.4 0.4 collective-permute-start.23
  116.8 0.0 collective-permute-done.18.rest_2_
  116.8 2.2 %collective-permute-start.24 = (bf16[8,32,512]{2,1,0:T(8,128)(2,1)S(1)}, bf16[8,32,512]{2,1,0:T(8,128)(2,1)S(1)}, u32[]{:S(2)}, u32[]{:S(2)}) collective-permute-start(bf16[8,32,512]{2,1,0:T(8,128)(2,1)S(1)} %collective-permute-done.18.rest_2_), channel_id=1, source_target_pairs={{0,3},{1,0},{2,1},{3,2},{4,7},{5,4},{6,5},{7,6},{8,11},{9,8},{10,9... | collective-permute-start | bytes 786440 | tf_op jit(solution)/shard_map/fresh_weights/ppermute | solution.py:33
  119.1 0.1 pad_add_fusion.4.place
  119.1 4.8 %input_grad.1 = bf16[256,8192]{1,0:T(8,128)(2,1)} custom-call(s32[2]{0:T(128)S(1)} %pad_add_fusion.4.place, bf16[256,512]{1,0:T(8,128)(2,1)S(1)} %copy-done, bf16[2048,512]{1,0:T(8,128)(2,1)} %collective-permute-done.21.rest_0_, bf16[2048,512]{1,0:T(8,128)(2,1)S(1)} %collective-permute-done.22.rest_1_, ...), custom_call_target="tpu_custom_call", output_to_operand_aliasing={{}: (4, {})} | custom-call | tf_op jit(solution)/shard_map/input_grad/pallas_call | solution.py:194
  124.0 0.0 collective-permute-done.19.rest_3_
  124.0 2.1 %rows.2.rest_2_ = bf16[2048,512]{1,0:T(8,128)(2,1)} custom-call(s32[1]{0:T(128)} %bitcast.place, s32[1,64]{1,0:T(1,128)S(1)} %copy-done.2, bf16[16,32,512]{2,1,0:T(8,128)(2,1)S(1)} %all-to-all-done.1.rest_0_, bf16[8,32,512]{2,1,0:T(8,128)(2,1)S(1)} %collective-permute-done.17.rest_1_, bf16[8,32,512]{2,1,0:T(8,128)(2,1)S(1)} %collective-permute-done.18.rest_2_, ...), custom_call_target="tpu_custom_call" | custom-call | tf_op jit(solution)/shard_map/rows/pallas_call | solution.py:237
  126.1 1.5 %collective-permute-done.23.rest_0_ = bf16[8,32,512]{2,1,0:T(8,128)(2,1)S(1)} collective-permute-done((bf16[8,32,512]{2,1,0:T(8,128)(2,1)S(1)}, bf16[8,32,512]{2,1,0:T(8,128)(2,1)S(1)}, u32[]{:S(2)}, u32[]{:S(2)}) %collective-permute-start.23) | collective-permute-done | bytes 262176 | tf_op jit(solution)/shard_map/fresh_weights/ppermute | solution.py:33
  127.6 0.1 collective-permute-done.24.rest_1_
  127.7 1.5 %rows.3 = bf16[2048,512]{1,0:T(8,128)(2,1)} custom-call(s32[1]{0:T(128)} %bitcast.place, s32[1,64]{1,0:T(1,128)S(1)} %copy-done.2, bf16[8,32,512]{2,1,0:T(8,128)(2,1)S(1)} %collective-permute-done.23.rest_0_, bf16[8,32,512]{2,1,0:T(8,128)(2,1)S(1)} %collective-permute-done.24.rest_1_, bf16[2048,512]{1,0:T(8,128)(2,1)} %rows.2.rest_2_), custom_call_target="tpu_custom_call", output_to_operand_aliasing={{}: (4, {})} | custom-call | tf_op jit(solution)/shard_map/rows/pallas_call | solution.py:237
  (21 shorter events, 0.1 us)
Async XLA Ops:
  0.7 6.4 %copy-start = (bf16[256,512]{1,0:T(8,128)(2,1)S(1)}, bf16[256,512]{1,0:T(8,128)(2,1)}, u32[]{:S(2)}) copy-start(bf16[256,512]{1,0:T(8,128)(2,1)} %key.5) | copy-start | bytes 786436
  0.7 6.8 %copy-start.2 = (s32[1,64]{1,0:T(1,128)S(1)}, s32[1,64]{1,0:T(1,128)}, u32[]{:S(2)}) copy-start(s32[1,64]{1,0:T(1,128)} %order.3) | copy-start | bytes 772
  3.7 8.2 %collective-permute-start.1 = (bf16[256,2048]{1,0:T(8,128)(2,1)}, bf16[256,2048]{1,0:T(8,128)(2,1)S(1)}, u32[]{:S(2)}, u32[]{:S(2)}) collective-permute-start(bf16[256,2048]{1,0:T(8,128)(2,1)} %get-tuple-element.37), channel_id=1, source_target_pairs={{0,64},{64,0},{1,65},{65,1},{2,66},{66,2},{3,67},{67,3},{4,68},{68... | collective-permute-start | bytes 3145736 | tf_op jit(solution)/shard_map/core_swap/ppermute | solution.py:33
  7.0 4.9 %collective-permute-start.2 = (bf16[256,2048]{1,0:T(8,128)(2,1)}, bf16[256,2048]{1,0:T(8,128)(2,1)S(1)}, u32[]{:S(2)}, u32[]{:S(2)}) collective-permute-start(bf16[256,2048]{1,0:T(8,128)(2,1)} %get-tuple-element.38), channel_id=1, source_target_pairs={{0,64},{64,0},{1,65},{65,1},{2,66},{66,2},{3,67},{67,3},{4,68},{68... | collective-permute-start | bytes 3145736 | tf_op jit(solution)/shard_map/core_swap/ppermute | solution.py:33
  7.1 4.7 %collective-permute-start.3 = (bf16[256,512]{1,0:T(8,128)(2,1)S(1)}, bf16[256,512]{1,0:T(8,128)(2,1)S(1)}, u32[]{:S(2)}, u32[]{:S(2)}) collective-permute-start(bf16[256,512]{1,0:T(8,128)(2,1)S(1)} %copy-done), channel_id=1, source_target_pairs={{0,64},{64,0},{1,65},{65,1},{2,66},{66,2},{3,67},{67,3},{4,68},{68... | collective-permute-start | bytes 786440 | tf_op jit(solution)/shard_map/core_swap/ppermute | solution.py:33
  7.5 4.3 %collective-permute-start = (s32[1,64]{1,0:T(1,128)S(1)}, s32[1,64]{1,0:T(1,128)S(1)}, u32[]{:S(2)}, u32[]{:S(2)}) collective-permute-start(s32[1,64]{1,0:T(1,128)S(1)} %copy-done.2), channel_id=1, source_target_pairs={{0,128},{128,0},{1,129},{129,1},{2,130},{130,2},{3,131},{131,3},{4... | collective-permute-start | bytes 776 | tf_op jit(solution)/shard_map/core_swap/ppermute | solution.py:33
  14.2 14.7 %collective-permute-start.4 = (bf16[4,8,16,512]{3,2,1,0:T(8,128)(2,1)S(1)}, bf16[4,8,16,512]{3,2,1,0:T(8,128)(2,1)S(1)}, u32[]{:S(2)}, u32[]{:S(2)}) collective-permute-start(bf16[4,8,16,512]{3,2,1,0:T(8,128)(2,1)S(1)} %get-tuple-element.40), channel_id=1, source_target_pairs={{0,1},{1,2},{2,3},{3,0},{4,5},{5,6},{6,7},{7,4},{8,9},{9,10},{10,1... | collective-permute-start | bytes 1572872 | tf_op jit(solution)/shard_map/first_stage/ppermute | solution.py:33
  15.1 14.7 %collective-permute-start.5 = (bf16[4,8,16,512]{3,2,1,0:T(8,128)(2,1)S(1)}, bf16[4,8,16,512]{3,2,1,0:T(8,128)(2,1)S(1)}, u32[]{:S(2)}, u32[]{:S(2)}) collective-permute-start(bf16[4,8,16,512]{3,2,1,0:T(8,128)(2,1)S(1)} %get-tuple-element.41), channel_id=1, source_target_pairs={{0,128},{128,4},{4,132},{132,0},{1,129},{129,5},{5,133},{133,1},{2... | collective-permute-start | bytes 1572872 | tf_op jit(solution)/shard_map/first_stage/ppermute | solution.py:33
  15.9 24.9 %collective-permute-start.6 = (bf16[4,8,16,512]{3,2,1,0:T(8,128)(2,1)S(1)}, bf16[4,8,16,512]{3,2,1,0:T(8,128)(2,1)S(1)}, u32[]{:S(2)}, u32[]{:S(2)}) collective-permute-start(bf16[4,8,16,512]{3,2,1,0:T(8,128)(2,1)S(1)} %get-tuple-element.42), channel_id=1, source_target_pairs={{0,4},{128,132},{4,0},{132,128},{1,5},{129,133},{5,1},{133,129},{2... | collective-permute-start | bytes 1572872 | tf_op jit(solution)/shard_map/first_stage/ppermute | solution.py:33
  18.2 22.8 %collective-permute-start.7 = (bf16[4,8,16,512]{3,2,1,0:T(8,128)(2,1)S(1)}, bf16[4,8,16,512]{3,2,1,0:T(8,128)(2,1)S(1)}, u32[]{:S(2)}, u32[]{:S(2)}) collective-permute-start(bf16[4,8,16,512]{3,2,1,0:T(8,128)(2,1)S(1)} %get-tuple-element.43), channel_id=1, source_target_pairs={{0,132},{128,0},{4,128},{132,4},{1,133},{129,1},{5,129},{133,5},{2... | collective-permute-start | bytes 1572872 | tf_op jit(solution)/shard_map/first_stage/ppermute | solution.py:33
  19.8 21.2 %collective-permute-start.8 = (bf16[4,8,16,512]{3,2,1,0:T(8,128)(2,1)S(1)}, bf16[4,8,16,512]{3,2,1,0:T(8,128)(2,1)S(1)}, u32[]{:S(2)}, u32[]{:S(2)}) collective-permute-start(bf16[4,8,16,512]{3,2,1,0:T(8,128)(2,1)S(1)} %get-tuple-element.44), channel_id=1, source_target_pairs={{0,3},{1,0},{2,1},{3,2},{4,7},{5,4},{6,5},{7,6},{8,11},{9,8},{10,9... | collective-permute-start | bytes 1572872 | tf_op jit(solution)/shard_map/first_stage/ppermute | solution.py:33
  28.9 14.0 %collective-permute-start.9 = (bf16[4,8,16,512]{3,2,1,0:T(8,128)(2,1)S(1)}, bf16[4,8,16,512]{3,2,1,0:T(8,128)(2,1)S(1)}, u32[]{:S(2)}, u32[]{:S(2)}) collective-permute-start(bf16[4,8,16,512]{3,2,1,0:T(8,128)(2,1)S(1)} %get-tuple-element.45), channel_id=1, source_target_pairs={{0,2},{1,3},{2,0},{3,1},{4,6},{5,7},{6,4},{7,5},{8,10},{9,11},{10,... | collective-permute-start | bytes 1572872 | tf_op jit(solution)/shard_map/first_stage/ppermute | solution.py:33
  43.2 6.9 %collective-permute-start.11 = (bf16[8,16,512]{2,1,0:T(8,128)(2,1)S(1)}, bf16[8,16,512]{2,1,0:T(8,128)(2,1)S(1)}, u32[]{:S(2)}, u32[]{:S(2)}) collective-permute-start(bf16[8,16,512]{2,1,0:T(8,128)(2,1)S(1)} %get-tuple-element.78), channel_id=1, source_target_pairs={{0,128},{128,4},{4,132},{132,0},{1,129},{129,5},{5,133},{133,1},{2... | collective-permute-start | bytes 393224 | tf_op jit(solution)/shard_map/second_stage/ppermute | solution.py:33
  44.3 6.9 %collective-permute-start.12 = (bf16[8,16,512]{2,1,0:T(8,128)(2,1)S(1)}, bf16[8,16,512]{2,1,0:T(8,128)(2,1)S(1)}, u32[]{:S(2)}, u32[]{:S(2)}) collective-permute-start(bf16[8,16,512]{2,1,0:T(8,128)(2,1)S(1)} %get-tuple-element.77), channel_id=1, source_target_pairs={{0,4},{128,132},{4,0},{132,128},{1,5},{129,133},{5,1},{133,129},{2... | collective-permute-start | bytes 393224 | tf_op jit(solution)/shard_map/second_stage/ppermute | solution.py:33
  45.9 5.2 %collective-permute-start.13 = (bf16[8,16,512]{2,1,0:T(8,128)(2,1)S(1)}, bf16[8,16,512]{2,1,0:T(8,128)(2,1)S(1)}, u32[]{:S(2)}, u32[]{:S(2)}) collective-permute-start(bf16[8,16,512]{2,1,0:T(8,128)(2,1)S(1)} %get-tuple-element.76), channel_id=1, source_target_pairs={{0,132},{128,0},{4,128},{132,4},{1,133},{129,1},{5,129},{133,5},{2... | collective-permute-start | bytes 393224 | tf_op jit(solution)/shard_map/second_stage/ppermute | solution.py:33
  47.1 9.8 %copy-start.1 = (bf16[2048,512]{1,0:T(8,128)(2,1)S(1)}, bf16[2048,512]{1,0:T(8,128)(2,1)}, u32[]{:S(2)}) copy-start(bf16[2048,512]{1,0:T(8,128)(2,1)} %rest_0_) | copy-start | bytes 6291460
  47.3 5.4 %collective-permute-start.10 = (bf16[8,16,512]{2,1,0:T(8,128)(2,1)S(1)}, bf16[8,16,512]{2,1,0:T(8,128)(2,1)S(1)}, u32[]{:S(2)}, u32[]{:S(2)}) collective-permute-start(bf16[8,16,512]{2,1,0:T(8,128)(2,1)S(1)} %get-tuple-element.75), channel_id=1, source_target_pairs={{0,1},{1,2},{2,3},{3,0},{4,5},{5,6},{6,7},{7,4},{8,9},{9,10},{10,1... | collective-permute-start | bytes 393224 | tf_op jit(solution)/shard_map/second_stage/ppermute | solution.py:33
  49.1 4.1 %collective-permute-start.14 = (bf16[8,16,512]{2,1,0:T(8,128)(2,1)S(1)}, bf16[8,16,512]{2,1,0:T(8,128)(2,1)S(1)}, u32[]{:S(2)}, u32[]{:S(2)}) collective-permute-start(bf16[8,16,512]{2,1,0:T(8,128)(2,1)S(1)} %get-tuple-element.74), channel_id=1, source_target_pairs={{0,3},{1,0},{2,1},{3,2},{4,7},{5,4},{6,5},{7,6},{8,11},{9,8},{10,9... | collective-permute-start | bytes 393224 | tf_op jit(solution)/shard_map/second_stage/ppermute | solution.py:33
  50.1 5.7 %collective-permute-start.15 = (bf16[8,16,512]{2,1,0:T(8,128)(2,1)S(1)}, bf16[8,16,512]{2,1,0:T(8,128)(2,1)S(1)}, u32[]{:S(2)}, u32[]{:S(2)}) collective-permute-start(bf16[8,16,512]{2,1,0:T(8,128)(2,1)S(1)} %get-tuple-element.73), channel_id=1, source_target_pairs={{0,2},{1,3},{2,0},{3,1},{4,6},{5,7},{6,4},{7,5},{8,10},{9,11},{10,... | collective-permute-start | bytes 393224 | tf_op jit(solution)/shard_map/second_stage/ppermute | solution.py:33
  56.8 12.6 %collective-permute-start.16 = (bf16[2048,512]{1,0:T(8,128)(2,1)S(1)}, bf16[2048,512]{1,0:T(8,128)(2,1)}, u32[]{:S(2)}, u32[]{:S(2)}) collective-permute-start(bf16[2048,512]{1,0:T(8,128)(2,1)S(1)} %copy-done.1), channel_id=1, source_target_pairs={{0,64},{64,0},{1,65},{65,1},{2,66},{66,2},{3,67},{67,3},{4,68},{68... | collective-permute-start | bytes 6291464 | tf_op jit(solution)/shard_map/weights/ppermute | solution.py:33
  61.1 25.6 %collective-permute-start.21 = (bf16[2048,512]{1,0:T(8,128)(2,1)S(1)}, bf16[2048,512]{1,0:T(8,128)(2,1)}, u32[]{:S(2)}, u32[]{:S(2)}) collective-permute-start(bf16[2048,512]{1,0:T(8,128)(2,1)S(1)} %copy-done.1), channel_id=1, source_target_pairs={{0,128},{64,196},{128,4},{192,64},{4,132},{68,192},{132,0},{196,68... | collective-permute-start | bytes 6291464 | tf_op jit(solution)/shard_map/weights/ppermute | solution.py:42
  61.6 20.0 %all-to-all-start = ((bf16[8,32,512]{2,1,0:T(8,128)(2,1)}), bf16[8,32,512]{2,1,0:T(8,128)(2,1)S(1)}, u32[]{:S(2)}, u32[]{:S(2)}) async-start(bf16[8,32,512]{2,1,0:T(8,128)(2,1)} %pad_maximum_fusion), calls=%async_computation | async-start | bytes 524288 | tf_op jit(solution)/shard_map/third_stage/all_to_all | solution.py:314
  69.4 12.2 %copy-start.3 = (f32[32,512]{1,0:T(8,128)S(1)}, f32[32,512]{1,0:T(8,128)}, u32[]{:S(2)}) copy-start(f32[32,512]{1,0:T(8,128)} %param.10) | copy-start | bytes 196612
  69.4 12.2 %copy-start.4 = (f32[32,512]{1,0:T(8,128)S(1)}, f32[32,512]{1,0:T(8,128)}, u32[]{:S(2)}) copy-start(f32[32,512]{1,0:T(8,128)} %param.11) | copy-start | bytes 196612
  69.4 12.2 %copy-start.5 = (f32[32,512]{1,0:T(8,128)S(1)}, f32[32,512]{1,0:T(8,128)}, u32[]{:S(2)}) copy-start(f32[32,512]{1,0:T(8,128)} %param.12) | copy-start | bytes 196612
  83.2 21.1 %all-to-all-start.1 = ((bf16[16,32,512]{2,1,0:T(8,128)(2,1)}), bf16[16,32,512]{2,1,0:T(8,128)(2,1)S(1)}, u32[]{:S(2)}, u32[]{:S(2)}) async-start(bf16[16,32,512]{2,1,0:T(8,128)(2,1)} %broadcast_in_dim.3), calls=%async_computation.1 | async-start | bytes 1048576 | tf_op jit(solution)/shard_map/fresh_weights/all_to_all | solution.py:332
  104.3 14.8 %collective-permute-start.22 = (bf16[2048,512]{1,0:T(8,128)(2,1)}, bf16[2048,512]{1,0:T(8,128)(2,1)S(1)}, u32[]{:S(2)}, u32[]{:S(2)}) collective-permute-start(bf16[2048,512]{1,0:T(8,128)(2,1)} %collective-permute-done.21.rest_0_), channel_id=1, source_target_pairs={{0,64},{64,0},{1,65},{65,1},{2,66},{66,2},{3,67},{67,3},{4,68},{68... | collective-permute-start | bytes 6291464 | tf_op jit(solution)/shard_map/input_grad/ppermute | solution.py:33
  107.2 9.2 %collective-permute-start.17 = (bf16[8,32,512]{2,1,0:T(8,128)(2,1)S(1)}, bf16[8,32,512]{2,1,0:T(8,128)(2,1)S(1)}, u32[]{:S(2)}, u32[]{:S(2)}) collective-permute-start(bf16[8,32,512]{2,1,0:T(8,128)(2,1)S(1)} %get-tuple-element.80), channel_id=1, source_target_pairs={{0,1},{1,2},{2,3},{3,0},{4,5},{5,6},{6,7},{7,4},{8,9},{9,10},{10,1... | collective-permute-start | bytes 786440 | tf_op jit(solution)/shard_map/fresh_weights/ppermute | solution.py:33
  108.9 7.9 %collective-permute-start.18 = (bf16[8,32,512]{2,1,0:T(8,128)(2,1)S(1)}, bf16[8,32,512]{2,1,0:T(8,128)(2,1)S(1)}, u32[]{:S(2)}, u32[]{:S(2)}) collective-permute-start(bf16[8,32,512]{2,1,0:T(8,128)(2,1)S(1)} %get-tuple-element.79), channel_id=1, source_target_pairs={{0,3},{1,0},{2,1},{3,2},{4,7},{5,4},{6,5},{7,6},{8,11},{9,8},{10,9... | collective-permute-start | bytes 786440 | tf_op jit(solution)/shard_map/fresh_weights/ppermute | solution.py:33
  109.9 14.1 %collective-permute-start.19 = (bf16[8,32,512]{2,1,0:T(8,128)(2,1)S(1)}, bf16[8,32,512]{2,1,0:T(8,128)(2,1)S(1)}, u32[]{:S(2)}, u32[]{:S(2)}) collective-permute-start(bf16[8,32,512]{2,1,0:T(8,128)(2,1)S(1)} %get-tuple-element.79), channel_id=1, source_target_pairs={{0,1},{1,2},{2,3},{3,0},{4,5},{5,6},{6,7},{7,4},{8,9},{9,10},{10,1... | collective-permute-start | bytes 786440 | tf_op jit(solution)/shard_map/fresh_weights/ppermute | solution.py:33
  110.3 13.6 %collective-permute-start.20 = (bf16[8,32,512]{2,1,0:T(8,128)(2,1)S(1)}, bf16[8,32,512]{2,1,0:T(8,128)(2,1)S(1)}, u32[]{:S(2)}, u32[]{:S(2)}) collective-permute-start(bf16[8,32,512]{2,1,0:T(8,128)(2,1)S(1)} %get-tuple-element.80), channel_id=1, source_target_pairs={{0,3},{1,0},{2,1},{3,2},{4,7},{5,4},{6,5},{7,6},{8,11},{9,8},{10,9... | collective-permute-start | bytes 786440 | tf_op jit(solution)/shard_map/fresh_weights/ppermute | solution.py:33
  116.4 11.2 %collective-permute-start.23 = (bf16[8,32,512]{2,1,0:T(8,128)(2,1)S(1)}, bf16[8,32,512]{2,1,0:T(8,128)(2,1)S(1)}, u32[]{:S(2)}, u32[]{:S(2)}) collective-permute-start(bf16[8,32,512]{2,1,0:T(8,128)(2,1)S(1)} %collective-permute-done.17.rest_1_), channel_id=1, source_target_pairs={{0,1},{1,2},{2,3},{3,0},{4,5},{5,6},{6,7},{7,4},{8,9},{9,10},{10,1... | collective-permute-start | bytes 786440 | tf_op jit(solution)/shard_map/fresh_weights/ppermute | solution.py:33
  116.8 10.9 %collective-permute-start.24 = (bf16[8,32,512]{2,1,0:T(8,128)(2,1)S(1)}, bf16[8,32,512]{2,1,0:T(8,128)(2,1)S(1)}, u32[]{:S(2)}, u32[]{:S(2)}) collective-permute-start(bf16[8,32,512]{2,1,0:T(8,128)(2,1)S(1)} %collective-permute-done.18.rest_2_), channel_id=1, source_target_pairs={{0,3},{1,0},{2,1},{3,2},{4,7},{5,4},{6,5},{7,6},{8,11},{9,8},{10,9... | collective-permute-start | bytes 786440 | tf_op jit(solution)/shard_map/fresh_weights/ppermute | solution.py:33

commit v8 on v7

--- a/solution.py
+++ b/solution.py
@@ -305,14 +305,17 @@
 
     with jax.named_scope("weights"):
         held, blocks = lax.optimization_barrier((key_weight, blocks))
-        core = send(held, "c", 1)
         other = cross(held)
-        place = jnp.stack([here + c, here + 1 - c]).astype(jnp.int32)
-        input_grad = input_grad_of(place, key_cotangent, [held, core], depth)
+
+    with jax.named_scope("input_grad"):
+        place = jnp.stack([here + c]).astype(jnp.int32)
+        input_grad = input_grad_of(place, key_cotangent, [key_weight], depth)
 
     with jax.named_scope("third_stage"):
         parts = lax.all_to_all(blocks, "z", 0, 0, tiled=True)
         parts, input_grad = lax.optimization_barrier((parts, input_grad))
+        held, parts = lax.optimization_barrier((key_weight, parts))
+        core = send(held, "c", 1)
         own_block = total_of([parts[n] for n in range(NZ)])
 
     with jax.named_scope("adam"):
@@ -330,6 +333,7 @@
         fresh = master_new.astype(jnp.bfloat16)
         fresh = jnp.broadcast_to(fresh, (NZ * NYH,) + fresh.shape)
         plane = lax.all_to_all(fresh, ("z", "yh"), 0, 0, tiled=True)
+        plane, core = lax.optimization_barrier((plane, core))
         half = NZ * NYH // 2
         low, high = plane[:half], plane[half:]
         parts = {(1, 0): send(low, "x", 1), (3, half): send(high, "x", 3)}
@@ -342,9 +346,9 @@
     with jax.named_scope("input_grad"):
         other, _ = lax.optimization_barrier((other, plane))
         other_core = send(other, "c", 1)
-        place = jnp.stack([there + c, there + 1 - c]).astype(jnp.int32)
+        place = jnp.stack([here + 1 - c, there + c, there + 1 - c]).astype(jnp.int32)
         input_grad = input_grad_of(
-            place, key_cotangent, [other, other_core], depth, input_grad
+            place, key_cotangent, [core, other, other_core], depth, input_grad
         )
 
     with jax.named_scope("rows"):

time: 130 us -> 135 us (1.038)
  blocking collectives: 0 us -> 20.7 us
  waiting for transfers between devices: 55 us -> 47.1 us
  Pallas kernels: 23.4 us -> 19.7 us
  starting transfers between devices: 46.4 us -> 43.9 us
    all_to_all x0 -> x1, blocking collectives: none -> 20.7 us  [on_device(): plane = lax.all_to_all(fresh, ('z', 'yh'), 0, 0, tiled=True)]
    all_to_all x1 -> x0, waiting for transfers between devices: 17.5 us -> none  [on_device(): plane = lax.all_to_all(fresh, ('z', 'yh'), 0, 0, tiled=True)]
    ppermute x1, waiting for transfers between devices: 0.01 us -> 8.96 us  [cross(): return lax.ppermute(value, ('yl', 'c', 'yh'), pairs)]
    pallas_call x2, Pallas kernels: 10.4 us -> 6.72 us  [input_grad_of(): pl.pallas_call(functools.partial(input_grad_kernel, count), grid_spec=plt...]
    all_to_all x1 -> x0, starting transfers between devices: 3.57 us -> none  [on_device(): plane = lax.all_to_all(fresh, ('z', 'yh'), 0, 0, tiled=True)]
  transfers between devices with their start and end apart: 27 -> 26, of which waited for: 12 -> 11; matrix products, arithmetic and copies ran while one was open for 2% -> 1% of each run, Pallas kernels for 13% -> 10%
where the time goes in v8:
time: 135 us
  waiting for transfers between devices  47.1 us (35%)
  starting transfers between devices  43.9 us (33%)
  blocking collectives  20.7 us (15%)
  Pallas kernels  19.7 us (15%)
  other arithmetic  2.64 us (2%)
    ppermute x24, starting transfers between devices, send(): lax.ppermute(value, ('yl', 'yh') if axis == 'y' else axis, shift(axis, st...  35.2 us
    ppermute x24, waiting for transfers between devices, send(): lax.ppermute(value, ('yl', 'yh') if axis == 'y' else axis, shift(axis, st...  30.7 us
    all_to_all x1, blocking collectives, on_device(): plane = lax.all_to_all(fresh, ('z', 'yh'), 0, 0, tiled=True)  20.7 us
    ppermute x1, waiting for transfers between devices, cross(): return lax.ppermute(value, ('yl', 'c', 'yh'), pairs)  8.96 us
    all_to_all x1, starting transfers between devices, on_device(): parts = lax.all_to_all(blocks, 'z', 0, 0, tiled=True)  8.68 us
    all_to_all x1, waiting for transfers between devices, on_device(): parts = lax.all_to_all(blocks, 'z', 0, 0, tiled=True)  7.48 us
    pallas_call x2, Pallas kernels, input_grad_of(): pl.pallas_call(functools.partial(input_grad_kernel, count), grid_spec=plt...  6.72 us
    pallas_call x1, Pallas kernels, own_partials(): pl.pallas_call(own_kernel, grid_spec=pltpu.PrefetchScalarGridSpec(num_sca...  4.14 us
  transfers between devices with their start and end apart: 26, of which 11 were waited for; matrix products, arithmetic and copies ran while one was open for 1% of the time, Pallas kernels for 10%

profile of v8, /device:TPU:1, one launch (start us, length us, event | category | flops | bytes accessed | tf_op | source)
XLA Modules:
  0.0 135.1 jit_solution(14781399195891961548)
XLA Ops:
  0.6 0.1 pad_add_fusion.2.place
  0.7 2.9 %core_swap.4 = (bf16[256,2048]{1,0:T(8,128)(2,1)}, bf16[256,2048]{1,0:T(8,128)(2,1)}) custom-call(s32[2]{0:T(128)S(1)} %pad_add_fusion.2.place, bf16[256,8192]{1,0:T(8,128)(2,1)} %tokens.1), custom_call_target="tpu_custom_call" | custom-call | tf_op jit(solution)/shard_map/core_swap/pallas_call | solution.py:86
  3.7 3.3 %collective-permute-start.1 = (bf16[256,2048]{1,0:T(8,128)(2,1)}, bf16[256,2048]{1,0:T(8,128)(2,1)S(1)}, u32[]{:S(2)}, u32[]{:S(2)}) collective-permute-start(bf16[256,2048]{1,0:T(8,128)(2,1)} %get-tuple-element.41), channel_id=1, source_target_pairs={{0,64},{64,0},{1,65},{65,1},{2,66},{66,2},{3,67},{67,3},{4,68},{68... | collective-permute-start | bytes 3145736 | tf_op jit(solution)/shard_map/core_swap/ppermute | solution.py:33
  7.0 0.1 collective-permute-start.2
  7.1 0.4 collective-permute-start.3
  7.5 0.1 pad_add_fusion.1.place
  7.6 0.1 pad_add_fusion.place
  7.7 4.1 %core_swap.3.own = bf16[2,2048,512]{2,1,0:T(8,128)(2,1)S(1)} custom-call(s32[2]{0:T(128)S(1)} %pad_add_fusion.1.place, bf16[256,8192]{1,0:T(8,128)(2,1)} %tokens.1, bf16[256,512]{1,0:T(8,128)(2,1)S(1)} %copy-done), custom_call_target="tpu_custom_call" | custom-call | tf_op jit(solution)/shard_map/core_swap/pallas_call | solution.py:115
  11.8 0.0 collective-permute-done.3.key
  11.8 0.0 collective-permute-done.1.far
  11.9 2.4 %core_swap.5 = (f32[4,8,16,512]{3,2,1,0:T(8,128)S(1)}, bf16[4,8,16,512]{3,2,1,0:T(8,128)(2,1)S(1)}, bf16[4,8,16,512]{3,2,1,0:T(8,128)(2,1)S(1)}, bf16[4,8,16,512...) custom-call(s32[2]{0:T(128)S(1)} %pad_add_fusion.place, ...), custom_call_target="tpu_custom_call" | custom-call | tf_op jit(solution)/shard_map/core_swap/pallas_call | solution.py:162
  14.2 0.9 collective-permute-start.4
  15.1 0.8 collective-permute-start.5
  15.9 2.3 %collective-permute-start.6 = (bf16[4,8,16,512]{3,2,1,0:T(8,128)(2,1)S(1)}, bf16[4,8,16,512]{3,2,1,0:T(8,128)(2,1)S(1)}, u32[]{:S(2)}, u32[]{:S(2)}) collective-permute-start(bf16[4,8,16,512]{3,2,1,0:T(8,128)(2,1)S(1)} %get-tuple-element.46), channel_id=1, source_target_pairs={{0,4},{128,132},{4,0},{132,128},{1,5},{129,133},{5,1},{133,129},{2... | collective-permute-start | bytes 1572872 | tf_op jit(solution)/shard_map/first_stage/ppermute | solution.py:33
  18.2 1.6 %collective-permute-start.7 = (bf16[4,8,16,512]{3,2,1,0:T(8,128)(2,1)S(1)}, bf16[4,8,16,512]{3,2,1,0:T(8,128)(2,1)S(1)}, u32[]{:S(2)}, u32[]{:S(2)}) collective-permute-start(bf16[4,8,16,512]{3,2,1,0:T(8,128)(2,1)S(1)} %get-tuple-element.47), channel_id=1, source_target_pairs={{0,132},{128,0},{4,128},{132,4},{1,133},{129,1},{5,129},{133,5},{2... | collective-permute-start | bytes 1572872 | tf_op jit(solution)/shard_map/first_stage/ppermute | solution.py:33
  19.8 1.5 %collective-permute-start.8 = (bf16[4,8,16,512]{3,2,1,0:T(8,128)(2,1)S(1)}, bf16[4,8,16,512]{3,2,1,0:T(8,128)(2,1)S(1)}, u32[]{:S(2)}, u32[]{:S(2)}) collective-permute-start(bf16[4,8,16,512]{3,2,1,0:T(8,128)(2,1)S(1)} %get-tuple-element.48), channel_id=1, source_target_pairs={{0,3},{1,0},{2,1},{3,2},{4,7},{5,4},{6,5},{7,6},{8,11},{9,8},{10,9... | collective-permute-start | bytes 1572872 | tf_op jit(solution)/shard_map/first_stage/ppermute | solution.py:33
  21.3 7.7 %collective-permute-done.4 = bf16[4,8,16,512]{3,2,1,0:T(8,128)(2,1)S(1)} collective-permute-done((bf16[4,8,16,512]{3,2,1,0:T(8,128)(2,1)S(1)}, bf16[4,8,16,512]{3,2,1,0:T(8,128)(2,1)S(1)}, u32[]{:S(2)}, u32[]{:S(2)}) %collective-permute-start.4) | collective-permute-done | bytes 524320 | tf_op jit(solution)/shard_map/first_stage/ppermute | solution.py:33
  28.9 0.9 collective-permute-start.9
  29.8 0.0 collective-permute-done.5
  29.8 11.0 %collective-permute-done.6 = bf16[4,8,16,512]{3,2,1,0:T(8,128)(2,1)S(1)} collective-permute-done((bf16[4,8,16,512]{3,2,1,0:T(8,128)(2,1)S(1)}, bf16[4,8,16,512]{3,2,1,0:T(8,128)(2,1)S(1)}, u32[]{:S(2)}, u32[]{:S(2)}) %collective-permute-start.6) | collective-permute-done | bytes 524320 | tf_op jit(solution)/shard_map/first_stage/ppermute | solution.py:33
  40.8 0.2 collective-permute-done.7
  41.0 0.0 collective-permute-done.8
  41.0 1.9 %collective-permute-done.9 = bf16[4,8,16,512]{3,2,1,0:T(8,128)(2,1)S(1)} collective-permute-done((bf16[4,8,16,512]{3,2,1,0:T(8,128)(2,1)S(1)}, bf16[4,8,16,512]{3,2,1,0:T(8,128)(2,1)S(1)}, u32[]{:S(2)}, u32[]{:S(2)}) %collective-permute-start.9) | collective-permute-done | bytes 524320 | tf_op jit(solution)/shard_map/first_stage/ppermute | solution.py:33
  42.9 0.3 fusion.9
  43.2 1.1 collective-permute-start.11
  44.3 1.6 %collective-permute-start.12 = (bf16[8,16,512]{2,1,0:T(8,128)(2,1)S(1)}, bf16[8,16,512]{2,1,0:T(8,128)(2,1)S(1)}, u32[]{:S(2)}, u32[]{:S(2)}) collective-permute-start(bf16[8,16,512]{2,1,0:T(8,128)(2,1)S(1)} %get-tuple-element.85), channel_id=1, source_target_pairs={{0,4},{128,132},{4,0},{132,128},{1,5},{129,133},{5,1},{133,129},{2... | collective-permute-start | bytes 393224 | tf_op jit(solution)/shard_map/second_stage/ppermute | solution.py:33
  45.9 1.1 collective-permute-start.13
  47.0 0.3 fusion.11
  47.3 0.0 copy-start.1
  47.4 1.8 %collective-permute-start.10 = (bf16[8,16,512]{2,1,0:T(8,128)(2,1)S(1)}, bf16[8,16,512]{2,1,0:T(8,128)(2,1)S(1)}, u32[]{:S(2)}, u32[]{:S(2)}) collective-permute-start(bf16[8,16,512]{2,1,0:T(8,128)(2,1)S(1)} %get-tuple-element.83), channel_id=1, source_target_pairs={{0,1},{1,2},{2,3},{3,0},{4,5},{5,6},{6,7},{7,4},{8,9},{9,10},{10,1... | collective-permute-start | bytes 393224 | tf_op jit(solution)/shard_map/second_stage/ppermute | solution.py:33
  49.1 1.0 collective-permute-start.14
  50.1 0.0 collective-permute-done.11
  50.1 1.1 collective-permute-start.15
  51.2 1.6 %collective-permute-done.10 = bf16[8,16,512]{2,1,0:T(8,128)(2,1)S(1)} collective-permute-done((bf16[8,16,512]{2,1,0:T(8,128)(2,1)S(1)}, bf16[8,16,512]{2,1,0:T(8,128)(2,1)S(1)}, u32[]{:S(2)}, u32[]{:S(2)}) %collective-permute-start.10) | collective-permute-done | bytes 131104 | tf_op jit(solution)/shard_map/second_stage/ppermute | solution.py:33
  52.8 0.5 collective-permute-done.14
  53.2 2.5 %collective-permute-done.15 = bf16[8,16,512]{2,1,0:T(8,128)(2,1)S(1)} collective-permute-done((bf16[8,16,512]{2,1,0:T(8,128)(2,1)S(1)}, bf16[8,16,512]{2,1,0:T(8,128)(2,1)S(1)}, u32[]{:S(2)}, u32[]{:S(2)}) %collective-permute-start.15) | collective-permute-done | bytes 131104 | tf_op jit(solution)/shard_map/second_stage/ppermute | solution.py:33
  55.8 0.3 fusion.2
  56.1 0.7 pad_maximum_fusion
  56.8 8.7 %all-to-all-start = ((bf16[8,32,512]{2,1,0:T(8,128)(2,1)}), bf16[8,32,512]{2,1,0:T(8,128)(2,1)S(1)}, u32[]{:S(2)}, u32[]{:S(2)}) async-start(bf16[8,32,512]{2,1,0:T(8,128)(2,1)} %pad_maximum_fusion), calls=%async_computation | async-start | bytes 524288 | tf_op jit(solution)/shard_map/third_stage/all_to_all | solution.py:315
  65.5 0.0 copy-start.3
  65.5 0.0 copy-start.4
  65.5 0.0 copy-start.5
  65.5 1.8 %input_grad.2.rest_3_ = bf16[256,8192]{1,0:T(8,128)(2,1)} custom-call(s32[1]{0:T(128)} %bitcast.3.place, bf16[256,512]{1,0:T(8,128)(2,1)S(1)} %copy-done, bf16[2048,512]{1,0:T(8,128)(2,1)S(1)} %copy-done.1), custom_call_target="tpu_custom_call" | custom-call | tf_op jit(solution)/shard_map/input_grad/pallas_call | solution.py:194
  67.3 7.5 %all-to-all-done = bf16[8,32,512]{2,1,0:T(8,128)(2,1)S(1)} async-done(((bf16[8,32,512]{2,1,0:T(8,128)(2,1)}), bf16[8,32,512]{2,1,0:T(8,128)(2,1)S(1)}, u32[]{:S(2)}, u32[]{:S(2)}) %all-to-all-start) | async-done | bytes 262176 | tf_op jit(solution)/shard_map/third_stage/all_to_all | solution.py:315
  74.8 5.3 %collective-permute-start.16 = (bf16[2048,512]{1,0:T(8,128)(2,1)S(1)}, bf16[2048,512]{1,0:T(8,128)(2,1)S(1)}, u32[]{:S(2)}, u32[]{:S(2)}) collective-permute-start(bf16[2048,512]{1,0:T(8,128)(2,1)S(1)} %copy-done.1), channel_id=1, source_target_pairs={{0,64},{64,0},{1,65},{65,1},{2,66},{66,2},{3,67},{67,3},{4,68},{68... | collective-permute-start | bytes 6291464 | tf_op jit(solution)/shard_map/third_stage/ppermute | solution.py:33
  80.1 0.7 fusion.12
  80.9 20.7 %all_to_all.10.rest_0_ = bf16[16,32,512]{2,1,0:T(8,128)(2,1)S(1)} all-to-all(bf16[16,32,512]{2,1,0:T(8,128)(2,1)S(1)} %broadcast_in_dim.3), channel_id=1, replica_groups=mesh['yl'=2,'c'=2,'z'=8,'yh'=2,'x'=4] {'z','yh'}, dimensions={0} | all-to-all | bytes 1048576 | tf_op jit(solution)/shard_map/fresh_weights/all_to_all | solution.py:335
  101.6 0.0 collective-permute-done.16.rest_0_
  101.6 9.0 %collective-permute-done.21.rest_1_ = bf16[2048,512]{1,0:T(8,128)(2,1)S(1)} collective-permute-done((bf16[2048,512]{1,0:T(8,128)(2,1)S(1)}, bf16[2048,512]{1,0:T(8,128)(2,1)S(1)}, u32[]{:S(2)}, u32[]{:S(2)}) %collective-permute-start.21) | collective-permute-done | bytes 2097184 | tf_op jit(solution)/shard_map/weights/ppermute | solution.py:42
  110.5 2.4 %collective-permute-start.22 = (bf16[2048,512]{1,0:T(8,128)(2,1)S(1)}, bf16[2048,512]{1,0:T(8,128)(2,1)S(1)}, u32[]{:S(2)}, u32[]{:S(2)}) collective-permute-start(bf16[2048,512]{1,0:T(8,128)(2,1)S(1)} %collective-permute-done.21.rest_1_), channel_id=1, source_target_pairs={{0,64},{64,0},{1,65},{65,1},{2,66},{66,2},{3,67},{67,3},{4,68},{68... | collective-permute-start | bytes 6291464 | tf_op jit(solution)/shard_map/input_grad/ppermute | solution.py:33
  113.0 1.6 %collective-permute-start.17 = (bf16[8,32,512]{2,1,0:T(8,128)(2,1)S(1)}, bf16[8,32,512]{2,1,0:T(8,128)(2,1)S(1)}, u32[]{:S(2)}, u32[]{:S(2)}) collective-permute-start(bf16[8,32,512]{2,1,0:T(8,128)(2,1)S(1)} %get-tuple-element.88), channel_id=1, source_target_pairs={{0,1},{1,2},{2,3},{3,0},{4,5},{5,6},{6,7},{7,4},{8,9},{9,10},{10,1... | collective-permute-start | bytes 786440 | tf_op jit(solution)/shard_map/fresh_weights/ppermute | solution.py:33
  114.6 1.1 collective-permute-start.18
  115.8 0.3 collective-permute-start.19
  116.1 2.3 %collective-permute-start.20 = (bf16[8,32,512]{2,1,0:T(8,128)(2,1)S(1)}, bf16[8,32,512]{2,1,0:T(8,128)(2,1)S(1)}, u32[]{:S(2)}, u32[]{:S(2)}) collective-permute-start(bf16[8,32,512]{2,1,0:T(8,128)(2,1)S(1)} %get-tuple-element.88), channel_id=1, source_target_pairs={{0,3},{1,0},{2,1},{3,2},{4,7},{5,4},{6,5},{7,6},{8,11},{9,8},{10,9... | collective-permute-start | bytes 786440 | tf_op jit(solution)/shard_map/fresh_weights/ppermute | solution.py:33
  118.4 3.8 %collective-permute-done.17.rest_1_ = bf16[8,32,512]{2,1,0:T(8,128)(2,1)S(1)} collective-permute-done((bf16[8,32,512]{2,1,0:T(8,128)(2,1)S(1)}, bf16[8,32,512]{2,1,0:T(8,128)(2,1)S(1)}, u32[]{:S(2)}, u32[]{:S(2)}) %collective-permute-start.17) | collective-permute-done | bytes 262176 | tf_op jit(solution)/shard_map/fresh_weights/ppermute | solution.py:33
  122.2 0.3 collective-permute-start.23
  122.6 0.0 collective-permute-done.18.rest_2_
  122.6 2.3 %collective-permute-start.24 = (bf16[8,32,512]{2,1,0:T(8,128)(2,1)S(1)}, bf16[8,32,512]{2,1,0:T(8,128)(2,1)S(1)}, u32[]{:S(2)}, u32[]{:S(2)}) collective-permute-start(bf16[8,32,512]{2,1,0:T(8,128)(2,1)S(1)} %collective-permute-done.18.rest_2_), channel_id=1, source_target_pairs={{0,3},{1,0},{2,1},{3,2},{4,7},{5,4},{6,5},{7,6},{8,11},{9,8},{10,9... | collective-permute-start | bytes 786440 | tf_op jit(solution)/shard_map/fresh_weights/ppermute | solution.py:33
  124.9 0.1 pad_add_fusion.3.place
  125.0 4.9 %input_grad.3 = bf16[256,8192]{1,0:T(8,128)(2,1)} custom-call(s32[3]{0:T(128)S(1)} %pad_add_fusion.3.place, bf16[256,512]{1,0:T(8,128)(2,1)S(1)} %copy-done, bf16[2048,512]{1,0:T(8,128)(2,1)S(1)} %collective-permute-done.16.rest_0_, bf16[2048,512]{1,0:T(8,128)(2,1)S(1)} %collective-permute-done.21.rest_1_, ...), custom_call_target="tpu_custom_call", output_to_operand_aliasing={{}: (5, {})} | custom-call | tf_op jit(solution)/shard_map/input_grad/pallas_call | solution.py:194
  129.9 2.1 %rows.2.rest_2_ = bf16[2048,512]{1,0:T(8,128)(2,1)} custom-call(s32[1]{0:T(128)} %bitcast.place, s32[1,64]{1,0:T(1,128)S(1)} %copy-done.2, bf16[16,32,512]{2,1,0:T(8,128)(2,1)S(1)} %all_to_all.10.rest_0_, bf16[8,32,512]{2,1,0:T(8,128)(2,1)S(1)} %collective-permute-done.17.rest_1_, bf16[8,32,512]{2,1,0:T(8,128)(2,1)S(1)} %collective-permute-done.18.rest_2_, ...), custom_call_target="tpu_custom_call" | custom-call | tf_op jit(solution)/shard_map/rows/pallas_call | solution.py:237
  132.0 1.5 %collective-permute-done.23.rest_0_ = bf16[8,32,512]{2,1,0:T(8,128)(2,1)S(1)} collective-permute-done((bf16[8,32,512]{2,1,0:T(8,128)(2,1)S(1)}, bf16[8,32,512]{2,1,0:T(8,128)(2,1)S(1)}, u32[]{:S(2)}, u32[]{:S(2)}) %collective-permute-start.23) | collective-permute-done | bytes 262176 | tf_op jit(solution)/shard_map/fresh_weights/ppermute | solution.py:33
  133.5 0.0 collective-permute-done.24.rest_1_
  133.5 1.5 %rows.3 = bf16[2048,512]{1,0:T(8,128)(2,1)} custom-call(s32[1]{0:T(128)} %bitcast.place, s32[1,64]{1,0:T(1,128)S(1)} %copy-done.2, bf16[8,32,512]{2,1,0:T(8,128)(2,1)S(1)} %collective-permute-done.23.rest_0_, bf16[8,32,512]{2,1,0:T(8,128)(2,1)S(1)} %collective-permute-done.24.rest_1_, bf16[2048,512]{1,0:T(8,128)(2,1)} %rows.2.rest_2_), custom_call_target="tpu_custom_call", output_to_operand_aliasing={{}: (4, {})} | custom-call | tf_op jit(solution)/shard_map/rows/pallas_call | solution.py:237
  (19 shorter events, 0.1 us)
Async XLA Ops:
  0.7 6.4 %copy-start = (bf16[256,512]{1,0:T(8,128)(2,1)S(1)}, bf16[256,512]{1,0:T(8,128)(2,1)}, u32[]{:S(2)}) copy-start(bf16[256,512]{1,0:T(8,128)(2,1)} %key.5) | copy-start | bytes 786436
  0.7 6.8 %copy-start.2 = (s32[1,64]{1,0:T(1,128)S(1)}, s32[1,64]{1,0:T(1,128)}, u32[]{:S(2)}) copy-start(s32[1,64]{1,0:T(1,128)} %order.3) | copy-start | bytes 772
  3.7 8.2 %collective-permute-start.1 = (bf16[256,2048]{1,0:T(8,128)(2,1)}, bf16[256,2048]{1,0:T(8,128)(2,1)S(1)}, u32[]{:S(2)}, u32[]{:S(2)}) collective-permute-start(bf16[256,2048]{1,0:T(8,128)(2,1)} %get-tuple-element.41), channel_id=1, source_target_pairs={{0,64},{64,0},{1,65},{65,1},{2,66},{66,2},{3,67},{67,3},{4,68},{68... | collective-permute-start | bytes 3145736 | tf_op jit(solution)/shard_map/core_swap/ppermute | solution.py:33
  7.0 4.9 %collective-permute-start.2 = (bf16[256,2048]{1,0:T(8,128)(2,1)}, bf16[256,2048]{1,0:T(8,128)(2,1)S(1)}, u32[]{:S(2)}, u32[]{:S(2)}) collective-permute-start(bf16[256,2048]{1,0:T(8,128)(2,1)} %get-tuple-element.42), channel_id=1, source_target_pairs={{0,64},{64,0},{1,65},{65,1},{2,66},{66,2},{3,67},{67,3},{4,68},{68... | collective-permute-start | bytes 3145736 | tf_op jit(solution)/shard_map/core_swap/ppermute | solution.py:33
  7.1 4.7 %collective-permute-start.3 = (bf16[256,512]{1,0:T(8,128)(2,1)S(1)}, bf16[256,512]{1,0:T(8,128)(2,1)S(1)}, u32[]{:S(2)}, u32[]{:S(2)}) collective-permute-start(bf16[256,512]{1,0:T(8,128)(2,1)S(1)} %copy-done), channel_id=1, source_target_pairs={{0,64},{64,0},{1,65},{65,1},{2,66},{66,2},{3,67},{67,3},{4,68},{68... | collective-permute-start | bytes 786440 | tf_op jit(solution)/shard_map/core_swap/ppermute | solution.py:33
  7.5 4.3 %collective-permute-start = (s32[1,64]{1,0:T(1,128)S(1)}, s32[1,64]{1,0:T(1,128)S(1)}, u32[]{:S(2)}, u32[]{:S(2)}) collective-permute-start(s32[1,64]{1,0:T(1,128)S(1)} %copy-done.2), channel_id=1, source_target_pairs={{0,128},{128,0},{1,129},{129,1},{2,130},{130,2},{3,131},{131,3},{4... | collective-permute-start | bytes 776 | tf_op jit(solution)/shard_map/core_swap/ppermute | solution.py:33
  14.2 14.7 %collective-permute-start.4 = (bf16[4,8,16,512]{3,2,1,0:T(8,128)(2,1)S(1)}, bf16[4,8,16,512]{3,2,1,0:T(8,128)(2,1)S(1)}, u32[]{:S(2)}, u32[]{:S(2)}) collective-permute-start(bf16[4,8,16,512]{3,2,1,0:T(8,128)(2,1)S(1)} %get-tuple-element.44), channel_id=1, source_target_pairs={{0,1},{1,2},{2,3},{3,0},{4,5},{5,6},{6,7},{7,4},{8,9},{9,10},{10,1... | collective-permute-start | bytes 1572872 | tf_op jit(solution)/shard_map/first_stage/ppermute | solution.py:33
  15.1 14.7 %collective-permute-start.5 = (bf16[4,8,16,512]{3,2,1,0:T(8,128)(2,1)S(1)}, bf16[4,8,16,512]{3,2,1,0:T(8,128)(2,1)S(1)}, u32[]{:S(2)}, u32[]{:S(2)}) collective-permute-start(bf16[4,8,16,512]{3,2,1,0:T(8,128)(2,1)S(1)} %get-tuple-element.45), channel_id=1, source_target_pairs={{0,128},{128,4},{4,132},{132,0},{1,129},{129,5},{5,133},{133,1},{2... | collective-permute-start | bytes 1572872 | tf_op jit(solution)/shard_map/first_stage/ppermute | solution.py:33
  15.9 24.9 %collective-permute-start.6 = (bf16[4,8,16,512]{3,2,1,0:T(8,128)(2,1)S(1)}, bf16[4,8,16,512]{3,2,1,0:T(8,128)(2,1)S(1)}, u32[]{:S(2)}, u32[]{:S(2)}) collective-permute-start(bf16[4,8,16,512]{3,2,1,0:T(8,128)(2,1)S(1)} %get-tuple-element.46), channel_id=1, source_target_pairs={{0,4},{128,132},{4,0},{132,128},{1,5},{129,133},{5,1},{133,129},{2... | collective-permute-start | bytes 1572872 | tf_op jit(solution)/shard_map/first_stage/ppermute | solution.py:33
  18.2 22.8 %collective-permute-start.7 = (bf16[4,8,16,512]{3,2,1,0:T(8,128)(2,1)S(1)}, bf16[4,8,16,512]{3,2,1,0:T(8,128)(2,1)S(1)}, u32[]{:S(2)}, u32[]{:S(2)}) collective-permute-start(bf16[4,8,16,512]{3,2,1,0:T(8,128)(2,1)S(1)} %get-tuple-element.47), channel_id=1, source_target_pairs={{0,132},{128,0},{4,128},{132,4},{1,133},{129,1},{5,129},{133,5},{2... | collective-permute-start | bytes 1572872 | tf_op jit(solution)/shard_map/first_stage/ppermute | solution.py:33
  19.8 21.2 %collective-permute-start.8 = (bf16[4,8,16,512]{3,2,1,0:T(8,128)(2,1)S(1)}, bf16[4,8,16,512]{3,2,1,0:T(8,128)(2,1)S(1)}, u32[]{:S(2)}, u32[]{:S(2)}) collective-permute-start(bf16[4,8,16,512]{3,2,1,0:T(8,128)(2,1)S(1)} %get-tuple-element.48), channel_id=1, source_target_pairs={{0,3},{1,0},{2,1},{3,2},{4,7},{5,4},{6,5},{7,6},{8,11},{9,8},{10,9... | collective-permute-start | bytes 1572872 | tf_op jit(solution)/shard_map/first_stage/ppermute | solution.py:33
  28.9 14.0 %collective-permute-start.9 = (bf16[4,8,16,512]{3,2,1,0:T(8,128)(2,1)S(1)}, bf16[4,8,16,512]{3,2,1,0:T(8,128)(2,1)S(1)}, u32[]{:S(2)}, u32[]{:S(2)}) collective-permute-start(bf16[4,8,16,512]{3,2,1,0:T(8,128)(2,1)S(1)} %get-tuple-element.49), channel_id=1, source_target_pairs={{0,2},{1,3},{2,0},{3,1},{4,6},{5,7},{6,4},{7,5},{8,10},{9,11},{10,... | collective-permute-start | bytes 1572872 | tf_op jit(solution)/shard_map/first_stage/ppermute | solution.py:33
  43.2 6.9 %collective-permute-start.11 = (bf16[8,16,512]{2,1,0:T(8,128)(2,1)S(1)}, bf16[8,16,512]{2,1,0:T(8,128)(2,1)S(1)}, u32[]{:S(2)}, u32[]{:S(2)}) collective-permute-start(bf16[8,16,512]{2,1,0:T(8,128)(2,1)S(1)} %get-tuple-element.86), channel_id=1, source_target_pairs={{0,128},{128,4},{4,132},{132,0},{1,129},{129,5},{5,133},{133,1},{2... | collective-permute-start | bytes 393224 | tf_op jit(solution)/shard_map/second_stage/ppermute | solution.py:33
  44.3 6.9 %collective-permute-start.12 = (bf16[8,16,512]{2,1,0:T(8,128)(2,1)S(1)}, bf16[8,16,512]{2,1,0:T(8,128)(2,1)S(1)}, u32[]{:S(2)}, u32[]{:S(2)}) collective-permute-start(bf16[8,16,512]{2,1,0:T(8,128)(2,1)S(1)} %get-tuple-element.85), channel_id=1, source_target_pairs={{0,4},{128,132},{4,0},{132,128},{1,5},{129,133},{5,1},{133,129},{2... | collective-permute-start | bytes 393224 | tf_op jit(solution)/shard_map/second_stage/ppermute | solution.py:33
  45.9 5.3 %collective-permute-start.13 = (bf16[8,16,512]{2,1,0:T(8,128)(2,1)S(1)}, bf16[8,16,512]{2,1,0:T(8,128)(2,1)S(1)}, u32[]{:S(2)}, u32[]{:S(2)}) collective-permute-start(bf16[8,16,512]{2,1,0:T(8,128)(2,1)S(1)} %get-tuple-element.84), channel_id=1, source_target_pairs={{0,132},{128,0},{4,128},{132,4},{1,133},{129,1},{5,129},{133,5},{2... | collective-permute-start | bytes 393224 | tf_op jit(solution)/shard_map/second_stage/ppermute | solution.py:33
  47.3 18.1 %copy-start.1 = (bf16[2048,512]{1,0:T(8,128)(2,1)S(1)}, bf16[2048,512]{1,0:T(8,128)(2,1)}, u32[]{:S(2)}) copy-start(bf16[2048,512]{1,0:T(8,128)(2,1)} %rest_0_.1) | copy-start | bytes 6291460
  47.4 5.4 %collective-permute-start.10 = (bf16[8,16,512]{2,1,0:T(8,128)(2,1)S(1)}, bf16[8,16,512]{2,1,0:T(8,128)(2,1)S(1)}, u32[]{:S(2)}, u32[]{:S(2)}) collective-permute-start(bf16[8,16,512]{2,1,0:T(8,128)(2,1)S(1)} %get-tuple-element.83), channel_id=1, source_target_pairs={{0,1},{1,2},{2,3},{3,0},{4,5},{5,6},{6,7},{7,4},{8,9},{9,10},{10,1... | collective-permute-start | bytes 393224 | tf_op jit(solution)/shard_map/second_stage/ppermute | solution.py:33
  49.1 4.1 %collective-permute-start.14 = (bf16[8,16,512]{2,1,0:T(8,128)(2,1)S(1)}, bf16[8,16,512]{2,1,0:T(8,128)(2,1)S(1)}, u32[]{:S(2)}, u32[]{:S(2)}) collective-permute-start(bf16[8,16,512]{2,1,0:T(8,128)(2,1)S(1)} %get-tuple-element.82), channel_id=1, source_target_pairs={{0,3},{1,0},{2,1},{3,2},{4,7},{5,4},{6,5},{7,6},{8,11},{9,8},{10,9... | collective-permute-start | bytes 393224 | tf_op jit(solution)/shard_map/second_stage/ppermute | solution.py:33
  50.1 5.7 %collective-permute-start.15 = (bf16[8,16,512]{2,1,0:T(8,128)(2,1)S(1)}, bf16[8,16,512]{2,1,0:T(8,128)(2,1)S(1)}, u32[]{:S(2)}, u32[]{:S(2)}) collective-permute-start(bf16[8,16,512]{2,1,0:T(8,128)(2,1)S(1)} %get-tuple-element.81), channel_id=1, source_target_pairs={{0,2},{1,3},{2,0},{3,1},{4,6},{5,7},{6,4},{7,5},{8,10},{9,11},{10,... | collective-permute-start | bytes 393224 | tf_op jit(solution)/shard_map/second_stage/ppermute | solution.py:33
  56.8 18.0 %all-to-all-start = ((bf16[8,32,512]{2,1,0:T(8,128)(2,1)}), bf16[8,32,512]{2,1,0:T(8,128)(2,1)S(1)}, u32[]{:S(2)}, u32[]{:S(2)}) async-start(bf16[8,32,512]{2,1,0:T(8,128)(2,1)} %pad_maximum_fusion), calls=%async_computation | async-start | bytes 524288 | tf_op jit(solution)/shard_map/third_stage/all_to_all | solution.py:315
  65.5 14.6 %copy-start.3 = (f32[32,512]{1,0:T(8,128)S(1)}, f32[32,512]{1,0:T(8,128)}, u32[]{:S(2)}) copy-start(f32[32,512]{1,0:T(8,128)} %param.10) | copy-start | bytes 196612
  65.5 14.6 %copy-start.4 = (f32[32,512]{1,0:T(8,128)S(1)}, f32[32,512]{1,0:T(8,128)}, u32[]{:S(2)}) copy-start(f32[32,512]{1,0:T(8,128)} %param.11) | copy-start | bytes 196612
  65.5 14.6 %copy-start.5 = (f32[32,512]{1,0:T(8,128)S(1)}, f32[32,512]{1,0:T(8,128)}, u32[]{:S(2)}) copy-start(f32[32,512]{1,0:T(8,128)} %param.12) | copy-start | bytes 196612
  74.8 26.7 %collective-permute-start.16 = (bf16[2048,512]{1,0:T(8,128)(2,1)S(1)}, bf16[2048,512]{1,0:T(8,128)(2,1)S(1)}, u32[]{:S(2)}, u32[]{:S(2)}) collective-permute-start(bf16[2048,512]{1,0:T(8,128)(2,1)S(1)} %copy-done.1), channel_id=1, source_target_pairs={{0,64},{64,0},{1,65},{65,1},{2,66},{66,2},{3,67},{67,3},{4,68},{68... | collective-permute-start | bytes 6291464 | tf_op jit(solution)/shard_map/third_stage/ppermute | solution.py:33
  80.1 30.4 %collective-permute-start.21 = (bf16[2048,512]{1,0:T(8,128)(2,1)S(1)}, bf16[2048,512]{1,0:T(8,128)(2,1)S(1)}, u32[]{:S(2)}, u32[]{:S(2)}) collective-permute-start(bf16[2048,512]{1,0:T(8,128)(2,1)S(1)} %copy-done.1), channel_id=1, source_target_pairs={{0,128},{64,196},{128,4},{192,64},{4,132},{68,192},{132,0},{196,68... | collective-permute-start | bytes 6291464 | tf_op jit(solution)/shard_map/weights/ppermute | solution.py:42
  110.5 14.5 %collective-permute-start.22 = (bf16[2048,512]{1,0:T(8,128)(2,1)S(1)}, bf16[2048,512]{1,0:T(8,128)(2,1)S(1)}, u32[]{:S(2)}, u32[]{:S(2)}) collective-permute-start(bf16[2048,512]{1,0:T(8,128)(2,1)S(1)} %collective-permute-done.21.rest_1_), channel_id=1, source_target_pairs={{0,64},{64,0},{1,65},{65,1},{2,66},{66,2},{3,67},{67,3},{4,68},{68... | collective-permute-start | bytes 6291464 | tf_op jit(solution)/shard_map/input_grad/ppermute | solution.py:33
  113.0 9.2 %collective-permute-start.17 = (bf16[8,32,512]{2,1,0:T(8,128)(2,1)S(1)}, bf16[8,32,512]{2,1,0:T(8,128)(2,1)S(1)}, u32[]{:S(2)}, u32[]{:S(2)}) collective-permute-start(bf16[8,32,512]{2,1,0:T(8,128)(2,1)S(1)} %get-tuple-element.88), channel_id=1, source_target_pairs={{0,1},{1,2},{2,3},{3,0},{4,5},{5,6},{6,7},{7,4},{8,9},{9,10},{10,1... | collective-permute-start | bytes 786440 | tf_op jit(solution)/shard_map/fresh_weights/ppermute | solution.py:33
  114.6 7.9 %collective-permute-start.18 = (bf16[8,32,512]{2,1,0:T(8,128)(2,1)S(1)}, bf16[8,32,512]{2,1,0:T(8,128)(2,1)S(1)}, u32[]{:S(2)}, u32[]{:S(2)}) collective-permute-start(bf16[8,32,512]{2,1,0:T(8,128)(2,1)S(1)} %get-tuple-element.87), channel_id=1, source_target_pairs={{0,3},{1,0},{2,1},{3,2},{4,7},{5,4},{6,5},{7,6},{8,11},{9,8},{10,9... | collective-permute-start | bytes 786440 | tf_op jit(solution)/shard_map/fresh_weights/ppermute | solution.py:33
  115.8 14.1 %collective-permute-start.19 = (bf16[8,32,512]{2,1,0:T(8,128)(2,1)S(1)}, bf16[8,32,512]{2,1,0:T(8,128)(2,1)S(1)}, u32[]{:S(2)}, u32[]{:S(2)}) collective-permute-start(bf16[8,32,512]{2,1,0:T(8,128)(2,1)S(1)} %get-tuple-element.87), channel_id=1, source_target_pairs={{0,1},{1,2},{2,3},{3,0},{4,5},{5,6},{6,7},{7,4},{8,9},{9,10},{10,1... | collective-permute-start | bytes 786440 | tf_op jit(solution)/shard_map/fresh_weights/ppermute | solution.py:33
  116.1 13.8 %collective-permute-start.20 = (bf16[8,32,512]{2,1,0:T(8,128)(2,1)S(1)}, bf16[8,32,512]{2,1,0:T(8,128)(2,1)S(1)}, u32[]{:S(2)}, u32[]{:S(2)}) collective-permute-start(bf16[8,32,512]{2,1,0:T(8,128)(2,1)S(1)} %get-tuple-element.88), channel_id=1, source_target_pairs={{0,3},{1,0},{2,1},{3,2},{4,7},{5,4},{6,5},{7,6},{8,11},{9,8},{10,9... | collective-permute-start | bytes 786440 | tf_op jit(solution)/shard_map/fresh_weights/ppermute | solution.py:33
  122.2 11.2 %collective-permute-start.23 = (bf16[8,32,512]{2,1,0:T(8,128)(2,1)S(1)}, bf16[8,32,512]{2,1,0:T(8,128)(2,1)S(1)}, u32[]{:S(2)}, u32[]{:S(2)}) collective-permute-start(bf16[8,32,512]{2,1,0:T(8,128)(2,1)S(1)} %collective-permute-done.17.rest_1_), channel_id=1, source_target_pairs={{0,1},{1,2},{2,3},{3,0},{4,5},{5,6},{6,7},{7,4},{8,9},{9,10},{10,1... | collective-permute-start | bytes 786440 | tf_op jit(solution)/shard_map/fresh_weights/ppermute | solution.py:33
  122.6 10.9 %collective-permute-start.24 = (bf16[8,32,512]{2,1,0:T(8,128)(2,1)S(1)}, bf16[8,32,512]{2,1,0:T(8,128)(2,1)S(1)}, u32[]{:S(2)}, u32[]{:S(2)}) collective-permute-start(bf16[8,32,512]{2,1,0:T(8,128)(2,1)S(1)} %collective-permute-done.18.rest_2_), channel_id=1, source_target_pairs={{0,3},{1,0},{2,1},{3,2},{4,7},{5,4},{6,5},{7,6},{8,11},{9,8},{10,9... | collective-permute-start | bytes 786440 | tf_op jit(solution)/shard_map/fresh_weights/ppermute | solution.py:33
